TPU v7x, 32 devices: a whole 2x2x4 slice. The times are simulated.
32 devices in a mesh: dp: 8 (over z, y), chan: 4 (over x, core).
Axes of the slice: x: 2, y: 2, z: 4, core: 2. Of those that a mesh axis runs over, the one named last changes fastest.
Arguments:
- tokens: bfloat16 [1024, 8, 2048], P(None, 'dp'), may hold values from -6 to 6
- doc_lengths: int32 [8, 4], P('dp'), may hold values from 1 to 512, 1024 in all within a row
- gain_mix: float32 [2048], replicated, may hold values from 0.5 to 1.5
- value_weight: bfloat16 [2048, 2736], P('dp', 'chan'), may hold values from -0.125 to 0.125
- branch_weight: bfloat16 [2048, 2736], P('dp', 'chan'), may hold values from -0.125 to 0.125
- conv_weight: float32 [4, 2736], P(None, 'chan'), may hold values from -3 to 3
- conv_bias: float32 [2736], P('chan'), may hold values from -3 to 3
- recur_gate: bfloat16 [16, 171, 171], P('chan'), may hold values from -0.4375 to 0.4375
- input_gate: bfloat16 [16, 171, 171], P('chan'), may hold values from -0.4375 to 0.4375
- recur_bias: float32 [2736], P('chan'), may hold values from -3 to 3
- input_bias: float32 [2736], P('chan'), may hold values from -3 to 3
- decay_param: float32 [2736], P('chan'), may hold values from -9 to -4
- out_weight: bfloat16 [2736, 2048], P('chan', 'dp'), may hold values from -0.3125 to 0.3125
- gain_ffn: float32 [2048], replicated, may hold values from 0.5 to 1.5
- gate_weight: bfloat16 [2048, 6144], P('dp', 'chan'), may hold values from -0.125 to 0.125
- up_weight: bfloat16 [2048, 6144], P('dp', 'chan'), may hold values from -0.125 to 0.125
- down_weight: bfloat16 [6144, 2048], P('chan', 'dp'), may hold values from -0.109375 to 0.109375
- cotangent: bfloat16 [1024, 8, 2048], P('chan', 'dp'), may hold values from -6 to 6
Outputs:
- output: bfloat16 [1024, 8, 2048], P('chan', 'dp')
- grad_tokens: float32 [1024, 8, 2048], P('chan', 'dp')
- grad_gain_mix: float32 [2048], replicated
- grad_value_weight: float32 [2048, 2736], P('dp', 'chan')
- grad_branch_weight: float32 [2048, 2736], P('dp', 'chan')
- grad_conv_weight: float32 [4, 2736], P(None, 'chan')
- grad_conv_bias: float32 [2736], P('chan')
- grad_recur_gate: float32 [16, 171, 171], P('chan')
- grad_input_gate: float32 [16, 171, 171], P('chan')
- grad_recur_bias: float32 [2736], P('chan')
- grad_input_bias: float32 [2736], P('chan')
- grad_decay_param: float32 [2736], P('chan')
- grad_out_weight: float32 [2736, 2048], P('chan', 'dp')
- grad_gain_ffn: float32 [2048], replicated
- grad_gate_weight: float32 [2048, 6144], P('dp', 'chan')
- grad_up_weight: float32 [2048, 6144], P('dp', 'chan')
- grad_down_weight: float32 [6144, 2048], P('chan', 'dp')
Inputs may be any that keep to these rules, and one draw needn't show every extreme that they name: `doc_lengths`: in every row the 4 lengths add up to 1024.
All inputs are finite; a program needn't handle non-finite values.
Results may differ from a plain program's by a relative error of at most 0.0089.
Values may be sent and summed in bfloat16 or wider, within the bound.
No kernel may reach another device: no remote copies, remote signals or barrier semaphores. Data moves between devices by JAX's collectives and lax.ppermute only.
A program may use at most 384 MiB of HBM per device.

v0:
```python
from functools import partial
import math

import jax
import jax.numpy as jnp
from jax import lax
from jax.sharding import PartitionSpec as P

MICRO = 2


epsilon = 1e-06
decay_scale = 8.0
floor_value = 0.0001
floats = jnp.float32
halves = jnp.bfloat16
contract_last = (((1,), (1,)), ((), ()))
contract_first = (((0,), (0,)), ((), ()))


def rms_norm(inputs, scales):
    return inputs * lax.rsqrt(jnp.mean(inputs * inputs, axis=-1, keepdims=True) + epsilon) * scales


def shifted(inputs, offset, filler):
    if offset == 0:
        return inputs
    leading = jnp.full((offset,) + inputs.shape[1:], filler, inputs.dtype)
    return jnp.concatenate([leading, inputs[: inputs.shape[0] - offset]], axis=0)


def doc_masks(doc_lengths, seq_len, conv_len):
    doc_ends = jnp.cumsum(doc_lengths, axis=1)
    places = lax.broadcasted_iota(jnp.int32, (seq_len, 1, 1), 0)
    segment = jnp.sum((places >= doc_ends[None, :, :-1]).astype(jnp.int32), axis=2)
    starts = (segment != shifted(segment, 1, -1)).astype(floats)[:, :, None]
    same_doc = []
    for offset in range(conv_len):
        same_doc.append((shifted(segment, offset, -1) == segment).astype(floats)[:, :, None])
    return (starts, same_doc)


def convolve(inputs, weights, biases, same_doc):
    running_sum = biases + weights[0] * inputs * same_doc[0]
    for offset in range(1, weights.shape[0]):
        running_sum = (
            running_sum + weights[offset] * shifted(inputs, offset, 0.0) * same_doc[offset]
        )
    return running_sum


def link(earlier, later):
    return (earlier[0] * later[0], later[0] * earlier[1] + later[1])


def block_states(coef, drive, running):
    length = coef.shape[0]
    width = math.gcd(length, 16)
    blocks = length // width
    rest = coef.shape[1:]
    coef_b = coef.reshape((blocks, width) + rest)
    drive_b = drive.reshape((blocks, width) + rest)
    coef_in, drive_inner = lax.associative_scan(link, (coef_b, drive_b), axis=1)
    total_coef, total_drive = lax.associative_scan(link, (coef_in[:, -1], drive_inner[:, -1]))
    ends = total_drive + total_coef * running
    entering = jnp.concatenate([running[None], ends[:-1]], axis=0)
    states = drive_inner + coef_in * entering[:, None]
    return states.reshape((length,) + rest)


def recurrence(branch_y, conv_in, gate_pre, admit_pre, decay_in, starts):
    recur_rate = jax.nn.sigmoid(gate_pre)
    admit_rate = jax.nn.sigmoid(admit_pre)
    decay_rate = jax.nn.softplus(decay_in) * recur_rate
    retain = jnp.exp(-decay_scale * decay_rate)
    one_minus = jnp.maximum(-jnp.expm1(-2.0 * decay_scale * decay_rate), floor_value)
    scale_in = jnp.where(starts > 0, 1.0, jnp.sqrt(one_minus))
    carry_coef = retain * (1.0 - starts)
    drive_in = scale_in * admit_rate * conv_in
    length = carry_coef.shape[0] // MICRO
    running = jnp.zeros(carry_coef.shape[1:], floats)
    pieces = []
    for micro_idx in range(MICRO):
        lower = micro_idx * length
        states = block_states(
            carry_coef[lower : lower + length], drive_in[lower : lower + length], running
        )
        running = states[-1]
        pieces.append(states)
    return jnp.concatenate(pieces, axis=0) * jax.nn.gelu(branch_y, approximate=True)


def gated(gate_lin, up_lin):
    return jax.nn.gelu(gate_lin, approximate=True) * up_lin


def on_device(
    tokens,
    doc_lengths,
    gain_mix,
    value_weight,
    branch_weight,
    conv_weight,
    conv_bias,
    recur_gate,
    input_gate,
    recur_bias,
    input_bias,
    decay_param,
    out_weight,
    gain_ffn,
    gate_weight,
    up_weight,
    down_weight,
    cotangent,
):
    seq_len, row_count, model_width = tokens.shape
    chan_count = lax.axis_size("chan")
    part_len = seq_len // chan_count
    token_rows = seq_len * row_count
    full_value, full_branch, out_rows, full_gate, full_up, full_down = (
        lax.all_gather(value_weight, "dp", axis=0, tiled=True),
        lax.all_gather(branch_weight, "dp", axis=0, tiled=True),
        lax.all_gather(out_weight, "dp", axis=1, tiled=True),
        lax.all_gather(gate_weight, "dp", axis=0, tiled=True),
        lax.all_gather(up_weight, "dp", axis=0, tiled=True),
        lax.all_gather(down_weight, "dp", axis=1, tiled=True),
    )
    lane_count = full_value.shape[1]
    local_heads = recur_gate.shape[0]
    head_width = recur_gate.shape[1]
    hidden_width = full_gate.shape[1]
    starts, same_doc = doc_masks(doc_lengths, seq_len, conv_weight.shape[0])
    whole_tokens = tokens.astype(floats)
    low_in = rms_norm(whole_tokens, gain_mix).astype(halves).reshape(token_rows, model_width)
    branch_x = jnp.dot(low_in, full_value, preferred_element_type=floats).reshape(
        seq_len, row_count, lane_count
    )
    branch_y = jnp.dot(low_in, full_branch, preferred_element_type=floats).reshape(
        seq_len, row_count, lane_count
    )
    conv_raw, conv_pull = jax.vjp(
        partial(convolve, same_doc=same_doc), branch_x, conv_weight, conv_bias
    )
    low_conv = conv_raw.astype(halves)
    by_head = low_conv.reshape(seq_len, row_count, local_heads, head_width)
    gate_pre = (
        jnp.einsum("trhc,hcd->trhd", by_head, recur_gate, preferred_element_type=floats).reshape(
            seq_len, row_count, lane_count
        )
        + recur_bias
    )
    admit_pre = (
        jnp.einsum("trhc,hcd->trhd", by_head, input_gate, preferred_element_type=floats).reshape(
            seq_len, row_count, lane_count
        )
        + input_bias
    )
    mixed, mixer_pull = jax.vjp(
        partial(recurrence, starts=starts),
        branch_y,
        low_conv.astype(floats),
        gate_pre,
        admit_pre,
        decay_param,
    )
    low_mixed = mixed.astype(halves)
    regrouped = lax.all_to_all(low_mixed, "chan", split_axis=0, concat_axis=2, tiled=True)
    flat_part = regrouped.reshape(part_len * row_count, regrouped.shape[2])
    shard_rows = lax.all_gather(out_rows, "chan", axis=0, tiled=True)
    columns = lax.slice_in_dim(flat_part, 0, shard_rows.shape[0], axis=1)
    branch_out = jnp.dot(columns, shard_rows, preferred_element_type=floats)
    branch_out = branch_out.reshape(part_len, row_count, model_width)
    own_tokens = lax.dynamic_slice_in_dim(
        whole_tokens, lax.axis_index("chan") * part_len, part_len, 0
    )
    residual = own_tokens + branch_out
    normed_mid, mid_pull = jax.vjp(rms_norm, residual, gain_ffn)
    mid_full = lax.all_gather(normed_mid.astype(halves), "chan", axis=0, tiled=True).reshape(
        token_rows, model_width
    )
    gate_lin = jnp.dot(mid_full, full_gate, preferred_element_type=floats).reshape(
        seq_len, row_count, hidden_width
    )
    up_lin = jnp.dot(mid_full, full_up, preferred_element_type=floats).reshape(
        seq_len, row_count, hidden_width
    )
    hidden, hidden_pull = jax.vjp(gated, gate_lin, up_lin)
    low_hidden = hidden.astype(halves)
    shard_rows = low_hidden
    product = jnp.dot(
        shard_rows.reshape(part_len * lax.axis_size("chan") * row_count, hidden_width),
        full_down,
        preferred_element_type=floats,
    )
    ffn_out = lax.psum_scatter(
        product.reshape(part_len * lax.axis_size("chan"), row_count, model_width),
        "chan",
        scatter_dimension=0,
        tiled=True,
    )
    output = (residual + ffn_out).astype(halves)
    cot_full = lax.all_gather(cotangent, "chan", axis=0, tiled=True).reshape(
        token_rows, model_width
    )
    back_hidden = lax.dot_general(
        cot_full, full_down, contract_last, preferred_element_type=floats
    ).reshape(seq_len, row_count, hidden_width)
    grad_down = lax.dot_general(
        low_hidden.reshape(token_rows, hidden_width),
        cot_full,
        contract_first,
        preferred_element_type=floats,
    )
    back_gate, back_up = hidden_pull(back_hidden)
    low_back_gate = back_gate.astype(halves)
    low_back_up = back_up.astype(halves)
    grad_gate = lax.dot_general(
        mid_full,
        low_back_gate.reshape(token_rows, hidden_width),
        contract_first,
        preferred_element_type=floats,
    )
    grad_up = lax.dot_general(
        mid_full,
        low_back_up.reshape(token_rows, hidden_width),
        contract_first,
        preferred_element_type=floats,
    )
    gate_rows = low_back_gate.reshape(part_len * lax.axis_size("chan") * row_count, hidden_width)
    up_rows = low_back_up.reshape(part_len * lax.axis_size("chan") * row_count, hidden_width)
    product = lax.dot_general(gate_rows, full_gate, contract_last, preferred_element_type=floats)
    product = product + lax.dot_general(
        up_rows, full_up, contract_last, preferred_element_type=floats
    )
    back_mid = lax.psum_scatter(
        product.reshape(part_len * lax.axis_size("chan"), row_count, model_width),
        "chan",
        scatter_dimension=0,
        tiled=True,
    )
    back_resid_norm, grad_gain_ffn = mid_pull(back_mid)
    back_resid = cotangent.astype(floats) + back_resid_norm
    back_branch = lax.all_gather(back_resid.astype(halves), "chan", axis=0, tiled=True).reshape(
        token_rows, model_width
    )
    back_mixed = lax.dot_general(
        back_branch, out_rows, contract_last, preferred_element_type=floats
    ).reshape(seq_len, row_count, lane_count)
    grad_out = lax.dot_general(
        low_mixed.reshape(token_rows, lane_count),
        back_branch,
        contract_first,
        preferred_element_type=floats,
    )
    back_y, back_conv_direct, back_gate_a, back_gate_i, grad_decay = mixer_pull(back_mixed)
    low_back_a = back_gate_a.astype(halves)
    low_back_i = back_gate_i.astype(halves)
    heads_a = low_back_a.reshape(seq_len, row_count, local_heads, head_width)
    heads_i = low_back_i.reshape(seq_len, row_count, local_heads, head_width)
    grad_recur_gate = jnp.einsum("trhc,trhd->hcd", by_head, heads_a, preferred_element_type=floats)
    grad_input_gate = jnp.einsum("trhc,trhd->hcd", by_head, heads_i, preferred_element_type=floats)
    grad_recur_bias = jnp.sum(low_back_a.astype(floats), axis=(0, 1))
    grad_input_bias = jnp.sum(low_back_i.astype(floats), axis=(0, 1))
    through_gates = jnp.einsum("trhd,hcd->trhc", heads_a, recur_gate, preferred_element_type=floats)
    through_gates = through_gates + jnp.einsum(
        "trhd,hcd->trhc", heads_i, input_gate, preferred_element_type=floats
    )
    back_conv = back_conv_direct + through_gates.reshape(seq_len, row_count, lane_count)
    back_x, grad_conv_w, grad_conv_b = conv_pull(back_conv)
    low_back_x = back_x.astype(halves)
    low_back_y = back_y.astype(halves)
    grad_value = lax.dot_general(
        low_in,
        low_back_x.reshape(token_rows, lane_count),
        contract_first,
        preferred_element_type=floats,
    )
    grad_branch = lax.dot_general(
        low_in,
        low_back_y.reshape(token_rows, lane_count),
        contract_first,
        preferred_element_type=floats,
    )
    x_rows = low_back_x.reshape(part_len * lax.axis_size("chan") * row_count, lane_count)
    y_rows = low_back_y.reshape(part_len * lax.axis_size("chan") * row_count, lane_count)
    product = lax.dot_general(x_rows, full_value, contract_last, preferred_element_type=floats)
    product = product + lax.dot_general(
        y_rows, full_branch, contract_last, preferred_element_type=floats
    )
    back_norm_in = lax.psum_scatter(
        product.reshape(part_len * lax.axis_size("chan"), row_count, model_width),
        "chan",
        scatter_dimension=0,
        tiled=True,
    )
    normed_own, in_pull = jax.vjp(rms_norm, own_tokens, gain_mix)
    back_tokens_norm, grad_gain_mix = in_pull(back_norm_in)
    grad_tokens = back_resid + back_tokens_norm
    grad_gain_mix, grad_gain_ffn = lax.psum((grad_gain_mix, grad_gain_ffn), ("dp", "chan"))
    (
        grad_conv_w,
        grad_conv_b,
        grad_recur_gate,
        grad_input_gate,
        grad_recur_bias,
        grad_input_bias,
        grad_decay,
    ) = lax.psum(
        (
            grad_conv_w,
            grad_conv_b,
            grad_recur_gate,
            grad_input_gate,
            grad_recur_bias,
            grad_input_bias,
            grad_decay,
        ),
        "dp",
    )
    grad_value, grad_branch, grad_out, grad_gate, grad_up, grad_down = (
        lax.psum_scatter(grad_value, "dp", scatter_dimension=0, tiled=True),
        lax.psum_scatter(grad_branch, "dp", scatter_dimension=0, tiled=True),
        lax.psum_scatter(grad_out, "dp", scatter_dimension=1, tiled=True),
        lax.psum_scatter(grad_gate, "dp", scatter_dimension=0, tiled=True),
        lax.psum_scatter(grad_up, "dp", scatter_dimension=0, tiled=True),
        lax.psum_scatter(grad_down, "dp", scatter_dimension=1, tiled=True),
    )
    return (
        output,
        grad_tokens,
        grad_gain_mix,
        grad_value,
        grad_branch,
        grad_conv_w,
        grad_conv_b,
        grad_recur_gate,
        grad_input_gate,
        grad_recur_bias,
        grad_input_bias,
        grad_decay,
        grad_out,
        grad_gain_ffn,
        grad_gate,
        grad_up,
        grad_down,
    )


def solution(mesh):
    in_specs = (
        P(None, "dp", None),
        P("dp", None),
        P(),
        P("dp", "chan"),
        P("dp", "chan"),
        P(None, "chan"),
        P("chan"),
        P("chan", None, None),
        P("chan", None, None),
        P("chan"),
        P("chan"),
        P("chan"),
        P("chan", "dp"),
        P(),
        P("dp", "chan"),
        P("dp", "chan"),
        P("chan", "dp"),
        P("chan", "dp", None),
    )
    out_specs = (
        P("chan", "dp", None),
        P("chan", "dp", None),
        P(),
        P("dp", "chan"),
        P("dp", "chan"),
        P(None, "chan"),
        P("chan"),
        P("chan", None, None),
        P("chan", None, None),
        P("chan"),
        P("chan"),
        P("chan"),
        P("chan", "dp"),
        P(),
        P("dp", "chan"),
        P("dp", "chan"),
        P("chan", "dp"),
    )
    return jax.shard_map(
        on_device, mesh=mesh, in_specs=in_specs, out_specs=out_specs, check_vma=False
    )
```

profile of v0, /device:TPU:0, one launch (start us, length us, event | category | flops | bytes accessed | tf_op | source)
XLA Modules:
  0.0 2699.2 jit_solution(7388192691897601826)
XLA Ops:
  9.5 62.6 %all-gather.16.cloned.1.call-done = bf16[684,2048]{1,0:T(8,128)(2,1)} async-done(((bf16[684,256]{1,0:T(8,128)(2,1)}), bf16[684,2048]{1,0:T(8,128)(2,1)}) %all-gather.16.cloned.1.call-update) | async-done | bytes 2801680 | tf_op jit(solution)/shard_map/all_gather | solution.py:124
  76.4 55.1 %all-gather.12.cloned.1.call-done = bf16[2048,684]{0,1:T(8,128)(2,1)} async-done(((bf16[256,684]{0,1:T(8,128)(2,1)}), bf16[2048,684]{0,1:T(8,128)(2,1)}) %all-gather.12.cloned.1.call-update) | async-done | bytes 2801680 | tf_op jit(solution)/shard_map/all_gather | solution.py:122
  555.2 8.7 multiply_convert_fusion.3
  582.1 11.5 all-to-all-done
  603.8 12.3 reshape.1184
  628.3 29.6 %all-gather.18.cloned.1.call-done = bf16[1024,1,2048]{2,0,1:T(8,128)(2,1)} async-done(((bf16[256,1,2048]{2,0,1:T(8,128)(2,1)}), bf16[1024,1,2048]{2,0,1:T(8,128)(2,1)}) %all-gather.18.cloned.1.call-update) | async-done | bytes 4194320 | tf_op jit(solution)/shard_map/all_gather | solution.py:179
  657.9 11.7 fusion.22
  669.6 89.6 %all-gather.22.cloned.1.call-done = bf16[2048,1536]{1,0:T(8,128)(2,1)} async-done(((bf16[256,1536]{1,0:T(8,128)(2,1)}), bf16[2048,1536]{1,0:T(8,128)(2,1)}) %all-gather.22.cloned.1.call-update) | async-done | bytes 6291472 | tf_op jit(solution)/shard_map/all_gather | solution.py:126
  759.2 11.7 fusion.20
  770.8 22.6 all-gather.26.cloned.1.call-done
  793.4 102.0 %all-gather.24.cloned.1.call-done = bf16[1536,2048]{1,0:T(8,128)(2,1)} async-done(((bf16[1536,256]{1,0:T(8,128)(2,1)}), bf16[1536,2048]{1,0:T(8,128)(2,1)}) %all-gather.24.cloned.1.call-update) | async-done | bytes 6291472 | tf_op jit(solution)/shard_map/all_gather | solution.py:127
  895.4 18.5 multiply_convert_fusion.1
  914.0 10.0 fusion.156
  924.0 10.9 add_bitcast_fusion.1
  935.0 70.0 %reduce-scatter.12.cloned.1.call-done = f32[256,1,2048]{2,0,1:T(8,128)} async-done(((f32[1024,1,2048]{2,0,1:T(8,128)}), f32[256,1,2048]{2,0,1:T(8,128)}) %reduce-scatter.12.cloned.1.call-update) | async-done | bytes 2097168 | tf_op jit(solution)/shard_map/reduce_scatter | solution.py:236
  1011.8 34.6 %all-gather.28.cloned.1.call-done = bf16[1024,1,2048]{2,0,1:T(8,128)(2,1)} async-done(((bf16[256,1,2048]{2,0,1:T(8,128)(2,1)}), bf16[1024,1,2048]{2,0,1:T(8,128)(2,1)}) %all-gather.28.cloned.1.call-update) | async-done | bytes 4194320 | tf_op jit(solution)/shard_map/all_gather | solution.py:244
  1046.4 10.7 fusion.30
  1432.0 10.6 convert_reduce_fusion
  1501.1 12.0 convolution_bitcast_fusion
  1513.2 12.5 fusion.18
  1525.8 12.6 fusion.16
  1538.5 12.5 fusion.12
  1578.3 38.0 %all-reduce.253 = (f32[4,684]{1,0:T(4,128)}, f32[684]{0:T(1024)}, f32[684]{0:T(1024)}, f32[684]{0:T(1024)}, f32[684]{0:T(1024)}) all-reduce(f32[4,684]{1,0:T(4,128)S(1)} %pad_add_fusion.38, f32[684]{0:T(1024)S(1)} %get-tuple-element.157, f32[684]{0:T(1024)S(1)} %get-tuple-element.176, ...), channel_id=1, replica_groups=mesh['dp'=8,'chan'=4] {'dp'}, use_global_device_ids=true, to_apply=%region_21.22 | all-reduce | flops 5472 | bytes 43776 | tf_op jit(solution)/shard_map/psum | solution.py:309
  1621.3 25.0 reduce-scatter.14.cloned.1.call-done
  1649.1 71.6 %reduce-scatter.10.cloned.1.call-done = f32[256,1,2048]{2,0,1:T(8,128)} async-done(((f32[1024,1,2048]{2,0,1:T(8,128)}), f32[256,1,2048]{2,0,1:T(8,128)}) %reduce-scatter.10.cloned.1.call-update) | async-done | bytes 2097168 | tf_op jit(solution)/shard_map/reduce_scatter | solution.py:196
  1729.8 43.2 %all-reduce.252 = (f32[2048]{0:T(1024)}, f32[2048]{0:T(1024)}) all-reduce(f32[2048]{0:T(1024)S(1)} %get-tuple-element.153, f32[2048]{0:T(1024)S(1)} %copy-done.209), channel_id=1, replica_groups=mesh['dp'=8,'chan'=4] {'dp','chan'}, use_global_device_ids=true, to_apply=%region_14.15 | all-reduce | flops 4096 | bytes 32768 | tf_op jit(solution)/shard_map/psum | solution.py:300
  1773.0 159.6 %reduce-scatter.22.cloned.1.call-done = f32[256,1536]{1,0:T(8,128)} async-done(((f32[2048,1536]{1,0:T(8,128)}), f32[256,1536]{1,0:T(8,128)}) %reduce-scatter.22.cloned.1.call-update) | async-done | bytes 1572880 | tf_op jit(solution)/shard_map/reduce_scatter | solution.py:325
  1932.6 210.6 %reduce-scatter.24.cloned.1.call-done = f32[256,1536]{1,0:T(8,128)} async-done(((f32[2048,1536]{1,0:T(8,128)}), f32[256,1536]{1,0:T(8,128)}) %reduce-scatter.24.cloned.1.call-update) | async-done | bytes 1572880 | tf_op jit(solution)/shard_map/reduce_scatter | solution.py:326
  2143.2 210.9 %reduce-scatter.26.cloned.1.call-done = f32[1536,256]{1,0:T(8,128)} async-done(((f32[1536,2048]{1,0:T(8,128)}), f32[1536,256]{1,0:T(8,128)}) %reduce-scatter.26.cloned.1.call-update) | async-done | bytes 1572880 | tf_op jit(solution)/shard_map/reduce_scatter | solution.py:327
  2354.0 112.1 %reduce-scatter.16.cloned.1.call-done = f32[256,684]{0,1:T(8,128)} async-done(((f32[2048,684]{0,1:T(8,128)}), f32[256,684]{0,1:T(8,128)}) %reduce-scatter.16.cloned.1.call-update) | async-done | bytes 700432 | tf_op jit(solution)/shard_map/reduce_scatter | solution.py:322
  2466.2 112.9 %reduce-scatter.18.cloned.1.call-done = f32[256,684]{0,1:T(8,128)} async-done(((f32[2048,684]{0,1:T(8,128)}), f32[256,684]{0,1:T(8,128)}) %reduce-scatter.18.cloned.1.call-update) | async-done | bytes 700432 | tf_op jit(solution)/shard_map/reduce_scatter | solution.py:323
  2579.1 112.8 %reduce-scatter.20.cloned.1.call-done = f32[684,256]{1,0:T(8,128)} async-done(((f32[684,2048]{1,0:T(8,128)}), f32[684,256]{1,0:T(8,128)}) %reduce-scatter.20.cloned.1.call-update) | async-done | bytes 700432 | tf_op jit(solution)/shard_map/reduce_scatter | solution.py:324
  (1122 shorter events, 952.3 us)
Async XLA Ops:
  7.2 140.7 %copy-start = (bf16[4,171,171]{2,0,1:T(4,128)(2,1)S(1)}, bf16[4,171,171]{2,0,1:T(4,128)(2,1)}, u32[]{:S(2)}) copy-start(bf16[4,171,171]{2,0,1:T(4,128)(2,1)} %param.25) | copy-start | bytes 701788
  7.2 64.8 %all-gather.16.cloned.1.call-start = ((), (), s32[]{:S(2)}) async-start(), calls=%async_computation.12 | async-start | bytes 3170304 | tf_op jit(solution)/shard_map/all_gather | solution.py:124
  7.9 123.6 %all-gather.12.cloned.1.call-start = ((), (), s32[]{:S(2)}) async-start(), calls=%async_computation.10 | async-start | bytes 3170304 | tf_op jit(solution)/shard_map/all_gather | solution.py:122
  8.7 546.5 %all-gather.14.cloned.1.call-start = ((), (), s32[]{:S(2)}) async-start(), calls=%async_computation.11 | async-start | bytes 3170304 | tf_op jit(solution)/shard_map/all_gather | solution.py:123
  9.4 594.3 %all-gather.30.cloned.1.call-start = ((), (), s32[]{:S(2)}) async-start(), calls=%async_computation.28 | async-start | bytes 14090240 | tf_op jit(solution)/shard_map/all_gather | solution.py:170
  72.1 556.2 %all-gather.20.cloned.1.call-start = ((), (), s32[]{:S(2)}) async-start(), calls=%async_computation.14 | async-start | bytes 7077888 | tf_op jit(solution)/shard_map/all_gather | solution.py:125
  169.4 145.4 %copy-start.24 = (f32[32,8,1,684]{3,1,0,2:T(8,128)}, f32[32,8,1,684]{3,1,0,2:T(8,128)S(1)}, u32[]{:S(2)}) copy-start(f32[32,8,1,684]{3,1,0,2:T(8,128)S(1)} %slice.878) | copy-start | bytes 2101252
  372.0 94.3 %copy-start.67 = (f32[32,16,1,684]{3,0,2,1:T(8,128)S(1)}, f32[32,16,1,684]{3,0,2,1:T(8,128)}, u32[]{:S(2)}) copy-start(f32[32,16,1,684]{3,0,2,1:T(8,128)} %pad.1110) | copy-start | bytes 4202500
  407.3 128.3 %copy-start.170 = (f32[2,1,684]{2,0,1:T(2,128)}, f32[2,1,684]{2,0,1:T(2,128)S(1)}, u32[]{:S(2)}) copy-start(f32[2,1,684]{2,0,1:T(2,128)S(1)} %slice.933) | copy-start | bytes 16420
  571.0 22.6 all-to-all-start
  575.3 82.6 %all-gather.18.cloned.1.call-start = ((), (), s32[]{:S(2)}) async-start(), calls=%async_computation.13 | async-start | bytes 5242880 | tf_op jit(solution)/shard_map/all_gather | solution.py:179
  624.5 384.2 %copy-start.5 = (f32[256,1,2048]{2,0,1:T(8,128)}, f32[256,1,2048]{2,0,1:T(8,128)S(1)}, u32[]{:S(2)}) copy-start(f32[256,1,2048]{2,0,1:T(8,128)S(1)} %get-tuple-element.497) | copy-start | bytes 6291460
  626.0 133.2 %all-gather.22.cloned.1.call-start = ((), (), s32[]{:S(2)}) async-start(), calls=%async_computation.15 | async-start | bytes 7077888 | tf_op jit(solution)/shard_map/all_gather | solution.py:126
  626.8 166.7 %all-gather.26.cloned.1.call-start = ((), (), s32[]{:S(2)}) async-start(), calls=%async_computation.18 | async-start | bytes 5242880 | tf_op jit(solution)/shard_map/all_gather | solution.py:203
  627.5 267.9 %all-gather.24.cloned.1.call-start = ((), (), s32[]{:S(2)}) async-start(), calls=%async_computation.16 | async-start | bytes 7077888 | tf_op jit(solution)/shard_map/all_gather | solution.py:127
  628.3 376.7 %reduce-scatter.12.cloned.1.call-start = ((), (), s32[]{:S(2)}) async-start(), calls=%async_computation.19 | async-start | bytes 10485760 | tf_op jit(solution)/shard_map/reduce_scatter | solution.py:236
  934.9 111.5 %all-gather.28.cloned.1.call-start = ((), (), s32[]{:S(2)}) async-start(), calls=%async_computation.20 | async-start | bytes 5242880 | tf_op jit(solution)/shard_map/all_gather | solution.py:244
  1011.8 604.6 %all-reduce.257.cloned.1.call-start = ((), (), s32[]{:S(2)}) async-start(), calls=%async_computation.29 | async-start | bytes 2883584 | tf_op jit(solution)/shard_map/psum | solution.py:309
  1113.8 97.6 %slice-start.2 = ((f32[8,1,684]{2,0,1:T(8,128)}), f32[1,1,684]{2,0,1:T(1,128)S(1)}, s32[]{:S(2)}) async-start(f32[8,1,684]{2,0,1:T(8,128)} %slice.1089), calls=%async_computation.32 | async-start | bytes 6144 | tf_op jit(solution)/shard_map/transpose(jvp())/split | solution.py:64
  1485.7 160.6 %reduce-scatter.14.cloned.1.call-start = ((), (), s32[]{:S(2)}) async-start(), calls=%async_computation.21 | async-start | bytes 10485760 | tf_op jit(solution)/shard_map/reduce_scatter | solution.py:291
  1501.1 219.6 %reduce-scatter.10.cloned.1.call-start = ((), (), s32[]{:S(2)}) async-start(), calls=%async_computation.17 | async-start | bytes 10485760 | tf_op jit(solution)/shard_map/reduce_scatter | solution.py:196
  1513.1 419.5 %reduce-scatter.22.cloned.1.call-start = ((), (), s32[]{:S(2)}) async-start(), calls=%async_computation.25 | async-start | bytes 14155776 | tf_op jit(solution)/shard_map/reduce_scatter | solution.py:325
  1525.7 617.5 %reduce-scatter.24.cloned.1.call-start = ((), (), s32[]{:S(2)}) async-start(), calls=%async_computation.26 | async-start | bytes 14155776 | tf_op jit(solution)/shard_map/reduce_scatter | solution.py:326
  1538.4 815.6 %reduce-scatter.26.cloned.1.call-start = ((), (), s32[]{:S(2)}) async-start(), calls=%async_computation.27 | async-start | bytes 14155776 | tf_op jit(solution)/shard_map/reduce_scatter | solution.py:327
  1551.0 915.2 %reduce-scatter.16.cloned.1.call-start = ((), (), s32[]{:S(2)}) async-start(), calls=%async_computation.22 | async-start | bytes 6340608 | tf_op jit(solution)/shard_map/reduce_scatter | solution.py:322
  1559.9 1019.2 %reduce-scatter.18.cloned.1.call-start = ((), (), s32[]{:S(2)}) async-start(), calls=%async_computation.23 | async-start | bytes 6340608 | tf_op jit(solution)/shard_map/reduce_scatter | solution.py:323
  1567.4 1124.4 %reduce-scatter.20.cloned.1.call-start = ((), (), s32[]{:S(2)}) async-start(), calls=%async_computation.24 | async-start | bytes 6340608 | tf_op jit(solution)/shard_map/reduce_scatter | solution.py:324
  1618.8 101.9 %copy-start.6 = (f32[256,1,2048]{2,0,1:T(8,128)S(1)}, f32[256,1,2048]{2,0,1:T(8,128)}, u32[]{:S(2)}) copy-start(f32[256,1,2048]{2,0,1:T(8,128)} %copy-done.5) | copy-start | bytes 6291460
  1618.8 101.9 %copy-start.47 = (bf16[256,1,2048]{2,0,1:T(8,128)(2,1)S(1)}, bf16[256,1,2048]{2,0,1:T(8,128)(2,1)}, u32[]{:S(2)}) copy-start(bf16[256,1,2048]{2,0,1:T(8,128)(2,1)} %param.35) | copy-start | bytes 3145732
  1618.8 101.9 %copy-start.163 = (f32[2048]{0:T(1024)S(1)}, f32[2048]{0:T(1024)}, u32[]{:S(2)}) copy-start(f32[2048]{0:T(1024)} %param.31) | copy-start | bytes 24580
  1618.8 101.9 %copy-start.213 = (f32[256]{0:T(256)S(1)}, f32[256]{0:T(256)}, u32[]{:S(2)}) copy-start(f32[256]{0:T(256)} %copy-done.212) | copy-start | bytes 3076
  1618.8 101.9 %copy-start.227 = (f32[256]{0:T(256)S(1)}, f32[256]{0:T(256)}, u32[]{:S(2)}) copy-start(f32[256]{0:T(256)} %copy-done.226) | copy-start | bytes 3076
  (236 other events, 2289.0 us)
Sparse Core Ops, SparseCore 0:
  10.1 61.9 all-gather.15
  74.1 57.4 all-gather.11
  133.6 57.3 all-gather.13
  192.5 72.8 all-gather.29
  267.4 99.0 all-gather.19
  626.1 31.7 all-gather.17
  660.1 99.0 all-gather.21
  760.7 32.6 all-gather.25
  795.5 99.9 all-gather.23
  935.0 69.8 reduce-scatter.11
  1011.9 34.4 all-gather.27
  1485.8 86.7 all-reduce.256
  1575.2 71.0 reduce-scatter.13
  1648.9 71.6 reduce-scatter.9
  1724.7 207.9 reduce-scatter.21
  1936.6 206.5 reduce-scatter.23
  2147.2 206.7 reduce-scatter.25
  2358.1 107.9 reduce-scatter.15
  2470.4 108.6 reduce-scatter.17
  2583.2 108.6 reduce-scatter.19
where the time goes:
time: 2730 us; the launch traced here: 2700 us
  waiting for transfers between devices  1500 us (55%)
  local copies, waits for them, and re-layouts  601 us (22%)
  other arithmetic  298 us (11%)
  matrix products  197 us (7%)
  blocking collectives  81.2 us (3%)
    reduce_scatter x1, waiting for transfers between devices, on_device(): lax.psum_scatter(grad_down, 'dp', scatter_dimension=1, tiled=True)  211 us
    reduce_scatter x1, waiting for transfers between devices, on_device(): lax.psum_scatter(grad_up, 'dp', scatter_dimension=0, tiled=True)  211 us
    pad x68, local copies, waits for them, and re-layouts, block_states(): coef_in, drive_inner = lax.associative_scan(link, (coef_b, drive_b), axis=1)  182 us
    reduce_scatter x3, waiting for transfers between devices, on_device(): lax.psum_scatter(product.reshape(part_len * lax.axis_size('chan'), row_co...  167 us
    reduce_scatter x1, waiting for transfers between devices, on_device(): lax.psum_scatter(grad_gate, 'dp', scatter_dimension=0, tiled=True)  160 us
    reduce_scatter x1, waiting for transfers between devices, on_device(): lax.psum_scatter(grad_branch, 'dp', scatter_dimension=0, tiled=True)  113 us
    reduce_scatter x1, waiting for transfers between devices, on_device(): lax.psum_scatter(grad_out, 'dp', scatter_dimension=1, tiled=True)  113 us
    reduce_scatter x1, waiting for transfers between devices, on_device(): lax.psum_scatter(grad_value, 'dp', scatter_dimension=0, tiled=True)  112 us
  transfers between devices with their start and end apart: 21, of which 17 were waited for; matrix products, arithmetic and copies ran while one was open for 22% of the time, Pallas kernels for 0%

commit v1 on v0

v1 whole, which is shorter than its diff:
```python
from functools import partial

import jax
import jax.numpy as jnp
from jax import lax
from jax.experimental import pallas as pl
from jax.experimental.pallas import tpu as pltpu
from jax.sharding import PartitionSpec as P

epsilon = 1e-06
decay_scale = 8.0
floor_value = 0.0001
gelu_root = 0.7978845608
gelu_cube = 0.044715
floats = jnp.float32
halves = jnp.bfloat16
contract_last = (((1,), (1,)), ((), ()))
contract_first = (((0,), (0,)), ((), ()))
CHUNK = 16
VMEM_BYTES = 48 * 1024 * 1024


def round_up(number, unit):
    return -(-number // unit) * unit


def pad_dim(array, axis, size):
    widths = [(0, 0)] * array.ndim
    widths[axis] = (0, size - array.shape[axis])
    return jnp.pad(array, widths)


class Grid:
    def __init__(self, axis, inner):
        self.axis = axis
        self.count = lax.axis_size(axis)
        self.inner = inner
        self.outer = self.count // inner
        place = lax.axis_index(axis)
        self.at_outer = place // inner
        self.at_inner = place % inner

    def hop_outer(self, value, step):
        pairs = [
            (o * self.inner + i, ((o + step) % self.outer) * self.inner + i)
            for o in range(self.outer)
            for i in range(self.inner)
        ]
        return lax.ppermute(value, self.axis, pairs)

    def hop_inner(self, value, step):
        pairs = [
            (o * self.inner + i, o * self.inner + (i + step) % self.inner)
            for o in range(self.outer)
            for i in range(self.inner)
        ]
        return lax.ppermute(value, self.axis, pairs)

    def order(self):
        k = jnp.arange(self.count, dtype=jnp.int32)
        outer = (self.at_outer + k % self.outer) % self.outer
        inner = (self.at_inner + k // self.outer) % self.inner
        return outer * self.inner + inner

    def place_of(self):
        k = jnp.arange(self.count, dtype=jnp.int32)
        outer = (k // self.inner - self.at_outer) % self.outer
        inner = (k % self.inner - self.at_inner) % self.inner
        return inner * self.outer + outer

    def gather(self, own, inner_first=False):
        blocks = {(0, 0): own}
        if inner_first:
            for t in range(1, self.inner):
                blocks[t, 0] = self.hop_inner(blocks[t - 1, 0], -1)
            for s in range(1, self.outer):
                for t in range(self.inner):
                    blocks[t, s] = self.hop_outer(blocks[t, s - 1], -1)
        else:
            for s in range(self.outer):
                if s:
                    blocks[0, s] = self.hop_outer(blocks[0, s - 1], -1)
                for t in range(1, self.inner):
                    blocks[t, s] = self.hop_inner(blocks[t - 1, s], -1)
        return [blocks[t, s] for t in range(self.inner) for s in range(self.outer)]

    def reduce(self, part):
        passing = None
        for s in reversed(range(self.outer)):
            total = part(self.inner - 1, s)
            for t in reversed(range(self.inner - 1)):
                total = part(t, s) + self.hop_inner(total.astype(halves), 1).astype(floats)
            if passing is not None:
                total = total + passing
            if s:
                passing = self.hop_outer(total.astype(halves), 1).astype(floats)
        return total

    def total(self, value):
        if self.count & (self.count - 1):
            return lax.psum(value, self.axis)
        bit = 1
        while bit < self.count:
            value = value + lax.ppermute(
                value, self.axis, [(i, i ^ bit) for i in range(self.count)]
            )
            bit *= 2
        return value


def gather_rows(grid, own):
    near = [own]
    for s in range(1, grid.outer):
        near.append(grid.hop_outer(near[-1], -1))
    near = jnp.concatenate(near, axis=0) if grid.outer > 1 else own
    halves_of = [near]
    for t in range(1, grid.inner):
        halves_of.append(grid.hop_inner(halves_of[-1], -1))
    return jnp.concatenate(halves_of, axis=0)


def reduce_rows(grid, product):
    rows = product.shape[0] // grid.inner
    total = product[(grid.inner - 1) * rows :]
    for t in reversed(range(grid.inner - 1)):
        total = product[t * rows : (t + 1) * rows] + grid.hop_inner(
            total.astype(halves), 1
        ).astype(floats)
    rows = rows // grid.outer
    passing = total[(grid.outer - 1) * rows :]
    for s in reversed(range(grid.outer - 1)):
        passing = total[s * rows : (s + 1) * rows] + grid.hop_outer(
            passing.astype(halves), 1
        ).astype(floats)
    return passing


def params():
    return pltpu.CompilerParams(vmem_limit_bytes=VMEM_BYTES)


def reorder_columns(array, order, back=False):
    rows, width = array.shape
    count = order.shape[0]
    block = width // count

    def body(order_ref, in_ref, out_ref):
        out_ref[...] = in_ref[...]

    straight = pl.BlockSpec((rows, block), lambda k, order_ref: (0, k))
    picked = pl.BlockSpec((rows, block), lambda k, order_ref: (0, order_ref[k]))
    return pl.pallas_call(
        body,
        out_shape=jax.ShapeDtypeStruct(array.shape, array.dtype),
        grid_spec=pltpu.PrefetchScalarGridSpec(
            num_scalar_prefetch=1,
            grid=(count,),
            in_specs=[straight if back else picked],
            out_specs=picked if back else straight,
        ),
        compiler_params=params(),
        name="reorder_columns",
    )(order, array)


def first_norm(tokens, gain, row_order, order):
    seq_len, width = tokens.shape
    tiles, count = row_order.shape[0], order.shape[0]
    part, block = seq_len // tiles, width // count

    def body(rows_ref, order_ref, tok_ref, gain_ref, out_ref, own_ref):
        whole = tok_ref[...].astype(floats)
        inverse = lax.rsqrt(jnp.mean(whole * whole, axis=-1, keepdims=True) + epsilon)
        for k in range(count):
            source = pl.ds(pl.multiple_of(order_ref[k] * block, block), block)
            raw = tok_ref[:, source]
            normed = raw.astype(floats) * inverse * gain_ref[:, source]
            out_ref[:, k * block : (k + 1) * block] = normed.astype(halves)

            @pl.when(pl.program_id(0) == 0)
            def _():
                own_ref[:, k * block : (k + 1) * block] = raw

    return pl.pallas_call(
        body,
        out_shape=(
            jax.ShapeDtypeStruct((seq_len, width), halves),
            jax.ShapeDtypeStruct((part, width), tokens.dtype),
        ),
        grid_spec=pltpu.PrefetchScalarGridSpec(
            num_scalar_prefetch=2,
            grid=(tiles,),
            in_specs=[
                pl.BlockSpec((part, width), lambda i, rows_ref, order_ref: (rows_ref[i], 0)),
                pl.BlockSpec((1, width), lambda i, rows_ref, order_ref: (0, 0)),
            ],
            out_specs=(
                pl.BlockSpec((part, width), lambda i, rows_ref, order_ref: (i, 0)),
                pl.BlockSpec((part, width), lambda i, rows_ref, order_ref: (0, 0)),
            ),
        ),
        compiler_params=params(),
        name="first_norm",
    )(row_order, order, tokens, gain.reshape(1, width))


def segment_of(places, ends_ref):
    segment = jnp.zeros(places.shape, jnp.int32)
    for j in range(ends_ref.shape[0] - 1):
        segment = segment + (places >= ends_ref[j]).astype(jnp.int32)
    return segment


def same_behind(places, ends_ref, offset):
    agree = segment_of(places, ends_ref) == segment_of(places - offset, ends_ref)
    return jnp.logical_and(agree, places >= offset).astype(floats)


def same_ahead(places, ends_ref, offset, seq_len):
    agree = segment_of(places, ends_ref) == segment_of(places + offset, ends_ref)
    return jnp.logical_and(agree, places + offset < seq_len).astype(floats)


def lane_chunks(width):
    step = 256 if width % 256 == 0 else 128
    return [slice(at, at + step) for at in range(0, width, step)]


def gate_values(pre_a, pre_i, decay8):
    rate = jax.nn.sigmoid(pre_a)
    admit = jax.nn.sigmoid(pre_i)
    power = decay8 * rate
    alpha = jnp.exp(-power)
    twice = 2.0 * power
    series = 1.0 - twice * (1.0 / 7.0)
    for order in (6.0, 5.0, 4.0, 3.0, 2.0):
        series = 1.0 - (twice * (1.0 / order)) * series
    raw = jnp.where(twice < 0.5, twice * series, 1.0 - alpha * alpha)
    one_minus = jnp.maximum(raw, floor_value)
    inverse = lax.rsqrt(one_minus)
    return rate, admit, alpha, raw, one_minus * inverse, inverse


def gelu_parts(value):
    square = value * value
    bend = jnp.tanh(gelu_root * (value + gelu_cube * (square * value)))
    half = 0.5 * (1.0 + bend)
    slope = half + 0.5 * value * (1.0 - bend * bend) * (
        gelu_root * (1.0 + 3.0 * gelu_cube * square)
    )
    return value * half, slope


def gelu(value):
    return gelu_parts(value)[0]


def recur_forward(branches, doc_ends, vectors, gates, places):
    seq_len, lanes = branches.shape[0], branches.shape[1] // 2
    tiles = places.shape[0]
    part = seq_len // tiles
    chunks = lane_chunks(lanes)

    def body(
        places_ref, ends_ref, x_ref, y_ref, vec_ref, gate_ref,
        mixed_ref, conv_ref, pre_ref, prev_ref, xs, carry,
    ):
        tile = pl.program_id(0)

        @pl.when(tile == 0)
        def _():
            xs[0:8] = jnp.zeros((8, lanes), floats)
            carry[...] = jnp.zeros_like(carry)

        xs[8 : 8 + part] = x_ref[...]
        rows = lax.broadcasted_iota(jnp.int32, (CHUNK, 1), 0)

        def convolve(c, _):
            at = pl.multiple_of(c * CHUNK, CHUNK)
            here = tile * part + at + rows
            same = [same_behind(here, ends_ref, k) for k in range(1, 4)]
            for lane in chunks:
                window = xs[pl.ds(at, CHUNK + 8), lane]
                total = vec_ref[4:5, lane] + vec_ref[0:1, lane] * window[8:]
                for k in range(1, 4):
                    moved = pltpu.roll(window, k, 0)[8:]
                    total = total + vec_ref[k : k + 1, lane] * moved * same[k - 1]
                conv_ref[pl.ds(at, CHUNK), lane] = total.astype(halves)
            return 0

        lax.fori_loop(0, part // CHUNK, convolve, 0)
        xs[0:8] = xs[part : part + 8]
        pre_ref[...] = jnp.dot(conv_ref[...], gate_ref[...], preferred_element_type=floats)

        def advance(c, entering):
            at = pl.multiple_of(c * CHUNK, CHUNK)
            here = tile * part + at + rows
            fresh = 1.0 - same_behind(here, ends_ref, 1)
            leaving = []
            for state, lane in zip(entering, chunks):
                span = lane.stop - lane.start
                shift_lane = slice(lane.start + lanes, lane.stop + lanes)
                pre_a = pre_ref[pl.ds(at, CHUNK), lane] + vec_ref[6:7, lane]
                pre_i = pre_ref[pl.ds(at, CHUNK), shift_lane] + vec_ref[7:8, lane]
                pre_ref[pl.ds(at, CHUNK), lane] = pre_a
                pre_ref[pl.ds(at, CHUNK), shift_lane] = pre_i
                conv_in = conv_ref[pl.ds(at, CHUNK), lane].astype(floats)
                _, admit, alpha, _, root, _ = gate_values(pre_a, pre_i, vec_ref[5:6, lane])
                keep = 1.0 - fresh
                coef = alpha * keep
                drive = (fresh + root * keep) * admit * conv_in
                index = lax.broadcasted_iota(jnp.int32, (CHUNK, span), 0)
                for d in (1, 2, 4):
                    inside = (index & 7) >= d
                    drive = jnp.where(inside, drive + coef * pltpu.roll(drive, d, 0), drive)
                    coef = jnp.where(inside, coef * pltpu.roll(coef, d, 0), coef)
                groups = []
                first = state
                for g in range(CHUNK // 8):
                    group = slice(g * 8, g * 8 + 8)
                    groups.append(coef[group] * state + drive[group])
                    state = groups[-1][7:8]
                states = jnp.concatenate(groups, axis=0)
                prev_ref[pl.ds(at, CHUNK), lane] = jnp.where(
                    index == 0, first, pltpu.roll(states, 1, 0)
                )
                mixed = states * gelu(y_ref[pl.ds(at, CHUNK), lane])
                mixed_ref[pl.ds(at, CHUNK), lane] = mixed.astype(halves)
                leaving.append(state)
            return tuple(leaving)

        ended = lax.fori_loop(
            0, part // CHUNK, advance, tuple(carry[0:1, lane] for lane in chunks)
        )
        for state, lane in zip(ended, chunks):
            carry[0:1, lane] = state

    own = lambda column: pl.BlockSpec((part, lanes), lambda i, p, e: (p[i], column))
    straight = lambda width: pl.BlockSpec((part, width), lambda i, p, e: (i, 0))
    whole = lambda array: pl.BlockSpec(array.shape, lambda i, p, e: (0, 0))
    return pl.pallas_call(
        body,
        out_shape=(
            jax.ShapeDtypeStruct((seq_len, lanes), halves),
            jax.ShapeDtypeStruct((seq_len, lanes), halves),
            jax.ShapeDtypeStruct((seq_len, 2 * lanes), floats),
            jax.ShapeDtypeStruct((seq_len, lanes), floats),
        ),
        grid_spec=pltpu.PrefetchScalarGridSpec(
            num_scalar_prefetch=2,
            grid=(tiles,),
            in_specs=[own(0), own(1), whole(vectors), whole(gates)],
            out_specs=(own(0), straight(lanes), straight(2 * lanes), straight(lanes)),
            scratch_shapes=[pltpu.VMEM((part + 8, lanes), floats), pltpu.VMEM((8, lanes), floats)],
        ),
        compiler_params=params(),
        cost_estimate=pl.CostEstimate(
            flops=4 * seq_len * lanes * lanes,
            bytes_accessed=seq_len * lanes * 32,
            transcendentals=seq_len * lanes * 6,
        ),
        name="recur_forward",
    )(places, doc_ends, branches, branches, vectors, gates)


def recur_backward(back_mixed, branches, conv_in, pre, previous, doc_ends, vectors, gates, places):
    seq_len, lanes = conv_in.shape
    tiles = places.shape[0]
    part = seq_len // tiles
    chunks = lane_chunks(lanes)
    steps = part // CHUNK

    def body(
        places_ref, ends_ref, bm_ref, x_ref, y_ref, conv_ref, pre_ref, prev_ref, vec_ref, gate_ref,
        bxy_ref, bai_ref, sums_ref, ahead, sums, carry,
    ):
        tile = tiles - 1 - pl.program_id(0)

        @pl.when(pl.program_id(0) == 0)
        def _():
            ahead[part : part + 8] = jnp.zeros((8, lanes), floats)
            sums[...] = jnp.zeros_like(sums)
            carry[...] = jnp.zeros_like(carry)

        rows = lax.broadcasted_iota(jnp.int32, (CHUNK, 1), 0)

        def add_rows(which, lane, value):
            for g in range(CHUNK // 8):
                sums[which * 8 : which * 8 + 8, lane] += value[g * 8 : g * 8 + 8]

        def retreat(c, entering):
            at = pl.multiple_of((steps - 1 - c) * CHUNK, CHUNK)
            span_rows = pl.ds(at, CHUNK)
            here = tile * part + at + rows
            keep = same_behind(here, ends_ref, 1)
            fresh = 1.0 - keep
            leaving = []
            for (back_next, coef_next), lane in zip(entering, chunks):
                span = lane.stop - lane.start
                shift_lane = slice(lane.start + lanes, lane.stop + lanes)
                decay8 = vec_ref[5:6, lane]
                rate, admit, alpha, raw, root, inverse = gate_values(
                    pre_ref[span_rows, lane], pre_ref[span_rows, shift_lane], decay8
                )
                conv = conv_ref[span_rows, lane].astype(floats)
                before = prev_ref[span_rows, lane]
                scale_in = fresh + root * keep
                coef = alpha * keep
                driven = scale_in * admit
                states = coef * before + driven * conv
                active, slope = gelu_parts(y_ref[span_rows, lane])
                back_mix = bm_ref[span_rows, lane]
                bxy_ref[span_rows, shift_lane] = (back_mix * states * slope).astype(halves)
                index = lax.broadcasted_iota(jnp.int32, (CHUNK, span), 0)
                back = back_mix * active
                chain = jnp.where(index == CHUNK - 1, coef_next, pltpu.roll(coef, CHUNK - 1, 0))
                for d in (1, 2, 4):
                    inside = (index & 7) < 8 - d
                    back = jnp.where(inside, back + chain * pltpu.roll(back, CHUNK - d, 0), back)
                    chain = jnp.where(inside, chain * pltpu.roll(chain, CHUNK - d, 0), chain)
                groups = []
                for g in reversed(range(CHUNK // 8)):
                    group = slice(g * 8, g * 8 + 8)
                    groups.insert(0, back[group] + chain[group] * back_next)
                    back_next = groups[0][0:1]
                back_state = jnp.concatenate(groups, axis=0)
                through = back_state * conv
                bound = jnp.where(raw > floor_value, through * admit * alpha * inverse, 0.0)
                back_alpha = (back_state * before - bound) * keep * alpha
                add_rows(5, lane, back_alpha * rate)
                back_a = (back_alpha * (-decay8) * rate * (1.0 - rate)).astype(halves)
                back_i = (through * scale_in * admit * (1.0 - admit)).astype(halves)
                add_rows(6, lane, back_a.astype(floats))
                add_rows(7, lane, back_i.astype(floats))
                bai_ref[span_rows, lane] = back_a
                bai_ref[span_rows, shift_lane] = back_i
                ahead[span_rows, lane] = back_state * driven
                leaving.append((back_next, coef[0:1]))
            return tuple(leaving)

        ended = lax.fori_loop(
            0, steps, retreat, tuple((carry[0:1, lane], carry[8:9, lane]) for lane in chunks)
        )
        for (back_next, coef_next), lane in zip(ended, chunks):
            carry[0:1, lane] = back_next
            carry[8:9, lane] = coef_next

        ahead[0:part] += lax.dot_general(
            bai_ref[...], gate_ref[...], contract_last, preferred_element_type=floats
        )

        def convolve(c, _):
            at = pl.multiple_of(c * CHUNK, CHUNK)
            here = tile * part + at + rows
            same = [same_ahead(here, ends_ref, k, seq_len) for k in range(1, 4)]
            for lane in chunks:
                window = ahead[pl.ds(at, CHUNK + 8), lane]
                x_part = x_ref[pl.ds(at, CHUNK), lane]
                direct = window[:CHUNK]
                back_x = vec_ref[0:1, lane] * direct
                add_rows(0, lane, x_part * direct)
                add_rows(4, lane, direct)
                for k in range(1, 4):
                    moved = pltpu.roll(window, CHUNK + 8 - k, 0)[:CHUNK] * same[k - 1]
                    back_x = back_x + vec_ref[k : k + 1, lane] * moved
                    add_rows(k, lane, x_part * moved)
                bxy_ref[pl.ds(at, CHUNK), lane] = back_x.astype(halves)
            return 0

        lax.fori_loop(0, steps, convolve, 0)
        ahead[part : part + 8] = ahead[0:8]

        @pl.when(pl.program_id(0) == tiles - 1)
        def _():
            for which in range(8):
                sums_ref[which : which + 1] = jnp.sum(
                    sums[which * 8 : which * 8 + 8], axis=0, keepdims=True
                )

    own = lambda width, column: pl.BlockSpec(
        (part, width), lambda i, p, e: (p[tiles - 1 - i], column)
    )
    straight = lambda width: pl.BlockSpec((part, width), lambda i, p, e: (tiles - 1 - i, 0))
    whole = lambda array: pl.BlockSpec(array.shape, lambda i, p, e: (0, 0))
    return pl.pallas_call(
        body,
        out_shape=(
            jax.ShapeDtypeStruct((seq_len, 2 * lanes), halves),
            jax.ShapeDtypeStruct((seq_len, 2 * lanes), halves),
            jax.ShapeDtypeStruct((8, lanes), floats),
        ),
        grid_spec=pltpu.PrefetchScalarGridSpec(
            num_scalar_prefetch=2,
            grid=(tiles,),
            in_specs=[
                own(lanes, 0), own(lanes, 0), own(lanes, 1),
                straight(lanes), straight(2 * lanes), straight(lanes),
                whole(vectors), whole(gates),
            ],
            out_specs=(
                own(2 * lanes, 0), straight(2 * lanes), pl.BlockSpec((8, lanes), lambda i, p, e: (0, 0)),
            ),
            scratch_shapes=[
                pltpu.VMEM((part + 8, lanes), floats),
                pltpu.VMEM((64, lanes), floats),
                pltpu.VMEM((16, lanes), floats),
            ],
        ),
        compiler_params=params(),
        cost_estimate=pl.CostEstimate(
            flops=4 * seq_len * lanes * lanes,
            bytes_accessed=seq_len * lanes * 36,
            transcendentals=seq_len * lanes * 6,
        ),
        name="recur_backward",
    )(places, doc_ends, back_mixed, branches, branches, conv_in, pre, previous, vectors, gates)


def rms_norm(inputs, scales):
    return inputs * lax.rsqrt(jnp.mean(inputs * inputs, axis=-1, keepdims=True) + epsilon) * scales


def gated(both):
    width = both.shape[1] // 2
    return gelu(both[:, :width]) * both[:, width:]


def gated_back(both, back_hidden):
    width = both.shape[1] // 2
    active, slope = gelu_parts(both[:, :width])
    back_gate = back_hidden * both[:, width:] * slope
    return jnp.concatenate(
        [back_gate.astype(halves), (back_hidden * active).astype(halves)], axis=1
    )


def inner_of(count):
    return max(d for d in range(1, count + 1) if count % d == 0 and d * d <= count)


def on_device(
    tokens,
    doc_lengths,
    gain_mix,
    value_weight,
    branch_weight,
    conv_weight,
    conv_bias,
    recur_gate,
    input_gate,
    recur_bias,
    input_bias,
    decay_param,
    out_weight,
    gain_ffn,
    gate_weight,
    up_weight,
    down_weight,
    cotangent,
):
    seq_len, _, width = tokens.shape
    heads, head_width = recur_gate.shape[:2]
    channels = value_weight.shape[1]
    hidden_width = gate_weight.shape[1]
    lanes = round_up(channels, 128)
    sent = round_up(channels, 16)
    dp = Grid("dp", inner_of(lax.axis_size("dp")))
    chan = Grid("chan", 2 if lax.axis_size("chan") % 2 == 0 else 1)
    part = seq_len // chan.count
    block = width // dp.count
    order = dp.order()
    row_order, row_place = chan.order(), chan.place_of()

    def columns(array, place):
        return array[:, place * block : (place + 1) * block]

    vb_own = jnp.concatenate(
        [pad_dim(value_weight.T, 0, sent), pad_dim(branch_weight.T, 0, sent)], axis=0
    )
    vb_full = jnp.concatenate(dp.gather(vb_own), axis=1)
    vb_full = jnp.concatenate(
        [pad_dim(vb_full[:sent], 0, lanes), pad_dim(vb_full[sent:], 0, lanes)], axis=0
    )
    out_full = jnp.concatenate(dp.gather(pad_dim(out_weight, 0, sent), inner_first=True), axis=1)
    out_full = pad_dim(out_full, 0, lanes)
    gu_full = jnp.concatenate(
        dp.gather(jnp.concatenate([gate_weight, up_weight], axis=1)), axis=0
    )
    down_full = jnp.concatenate(dp.gather(down_weight), axis=1)

    def spread(gate):
        total = 0.0
        for h in range(heads):
            low = h * head_width
            total = total + jnp.pad(gate[h], ((low, lanes - low - head_width),) * 2)
        return total

    gates = jnp.concatenate([spread(recur_gate), spread(input_gate)], axis=1)
    vectors = pad_dim(
        jnp.concatenate(
            [
                conv_weight,
                conv_bias[None],
                decay_scale * jax.nn.softplus(decay_param)[None],
                recur_bias[None],
                input_bias[None],
            ],
            axis=0,
        ),
        1,
        lanes,
    )
    doc_ends = jnp.cumsum(doc_lengths[0])
    gains = jnp.stack([gain_mix, gain_ffn]).reshape(2, dp.count, block)
    gains = jnp.take(gains, order, axis=1).reshape(2, width)

    low_in, own_tokens = first_norm(tokens.reshape(seq_len, width), gain_mix, row_order, order)
    own_tokens = own_tokens.astype(floats)
    branches = lax.dot_general(low_in, vb_full, contract_last, preferred_element_type=floats)
    mixed, conv_in, pre, previous = recur_forward(branches, doc_ends, vectors, gates, row_place)
    product = jnp.dot(mixed, out_full, preferred_element_type=floats)
    residual = own_tokens + reduce_rows(chan, product)
    normed_mid, mid_pull = jax.vjp(rms_norm, residual, gains[1])
    mid_full = gather_rows(chan, normed_mid.astype(halves))
    cot_own = reorder_columns(cotangent.reshape(part, width), order)
    cot_full = gather_rows(chan, cot_own)

    both = jnp.dot(mid_full, gu_full, preferred_element_type=floats)
    hidden = gated(both).astype(halves)
    grad_down = dp.reduce(
        lambda t, s: lax.dot_general(
            hidden,
            columns(cot_full, t * dp.outer + s),
            contract_first,
            preferred_element_type=floats,
        )
    )
    back_hidden = lax.dot_general(
        cot_full, down_full, contract_last, preferred_element_type=floats
    )
    back_both = gated_back(both, back_hidden)
    product = lax.dot_general(back_both, gu_full, contract_last, preferred_element_type=floats)
    back_mid = reduce_rows(chan, product)
    grad_gu = dp.reduce(
        lambda t, s: lax.dot_general(
            columns(mid_full, t * dp.outer + s),
            back_both,
            contract_first,
            preferred_element_type=floats,
        )
    )
    product = jnp.dot(hidden, down_full, preferred_element_type=floats)
    output = (residual + reduce_rows(chan, product)).astype(halves)

    back_norm, grad_gain_ffn = mid_pull(back_mid)
    back_resid = cot_own.astype(floats) + back_norm
    back_branch = gather_rows(chan, back_resid.astype(halves))
    back_mixed = lax.dot_general(
        back_branch, out_full, contract_last, preferred_element_type=floats
    )
    grad_out = dp.reduce(
        lambda t, s: lax.dot_general(
            mixed,
            columns(back_branch, t * dp.outer + s),
            contract_first,
            preferred_element_type=floats,
        )[:sent]
    )
    back_xy, back_ai, sums = recur_backward(
        back_mixed, branches, conv_in, pre, previous, doc_ends, vectors, gates, row_place
    )

    def vb_part(t, s):
        whole = lax.dot_general(
            back_xy,
            columns(low_in, t * dp.outer + s),
            contract_first,
            preferred_element_type=floats,
        )
        return jnp.concatenate([whole[:sent], whole[lanes : lanes + sent]], axis=0)

    grad_vb = dp.reduce(vb_part)
    product = lax.dot_general(
        back_xy,
        vb_full,
        (((1,), (0,)), ((), ())),
        preferred_element_type=floats,
    )
    back_norm_in = reduce_rows(chan, product)
    _, in_pull = jax.vjp(rms_norm, own_tokens, gains[0])
    back_tokens, grad_gain_mix = in_pull(back_norm_in)
    grad_tokens = back_resid + back_tokens

    gate_grads = lax.dot_general(conv_in, back_ai, contract_first, preferred_element_type=floats)
    gate_grads = jnp.stack(
        [
            gate_grads[
                h * head_width : (h + 1) * head_width,
                side * lanes + h * head_width : side * lanes + (h + 1) * head_width,
            ]
            for side in range(2)
            for h in range(heads)
        ]
    )
    gate_grads = lax.psum(gate_grads, "dp")
    sums = dp.total(sums)[:, :channels]
    grad_decay = sums[5] * (-decay_scale * jax.nn.sigmoid(decay_param))
    places = dp.place_of()

    def whole_gain(gradient):
        gradient = chan.total(gradient.reshape(dp.count, block))
        return dp.total(jnp.take(gradient, places, axis=0)).reshape(width)

    return (
        reorder_columns(output, order, back=True).reshape(part, 1, width),
        reorder_columns(grad_tokens, order, back=True).reshape(part, 1, width),
        whole_gain(grad_gain_mix),
        grad_vb[:channels].T,
        grad_vb[sent : sent + channels].T,
        sums[:4],
        sums[4],
        gate_grads[:heads],
        gate_grads[heads:],
        sums[6],
        sums[7],
        grad_decay,
        grad_out[:channels],
        whole_gain(grad_gain_ffn),
        grad_gu[:, :hidden_width],
        grad_gu[:, hidden_width:],
        grad_down,
    )


def solution(mesh):
    in_specs = (
        P(None, "dp", None),
        P("dp", None),
        P(),
        P("dp", "chan"),
        P("dp", "chan"),
        P(None, "chan"),
        P("chan"),
        P("chan", None, None),
        P("chan", None, None),
        P("chan"),
        P("chan"),
        P("chan"),
        P("chan", "dp"),
        P(),
        P("dp", "chan"),
        P("dp", "chan"),
        P("chan", "dp"),
        P("chan", "dp", None),
    )
    out_specs = (
        P("chan", "dp", None),
        P("chan", "dp", None),
        P(),
        P("dp", "chan"),
        P("dp", "chan"),
        P(None, "chan"),
        P("chan"),
        P("chan", None, None),
        P("chan", None, None),
        P("chan"),
        P("chan"),
        P("chan"),
        P("chan", "dp"),
        P(),
        P("dp", "chan"),
        P("dp", "chan"),
        P("chan", "dp"),
    )
    return jax.shard_map(
        on_device, mesh=mesh, in_specs=in_specs, out_specs=out_specs, check_vma=False
    )
```

time: 2730 us -> 1040 us (0.38)
  waiting for transfers between devices: 1500 us -> 552 us
  local copies, waits for them, and re-layouts: 601 us -> 78.3 us
  other arithmetic: 298 us -> 44.7 us
  starting transfers between devices: 5.29 us -> 95.5 us
  blocking collectives: 81.2 us -> 0 us
  Pallas kernels: 0 us -> 58 us
    reduce_scatter x9 -> x0, waiting for transfers between devices: 1090 us -> none  [the longest x1 211 us: on_device(): lax.psum_scatter(grad_down, 'dp', scatter_dimension=1, tiled=True)]
    ppermute x0 -> x83, waiting for transfers between devices: none -> 510 us  [the longest x34 276 us: hop_outer(): return lax.ppermute(value, self.axis, pairs)]
    all_gather x10 -> x0, waiting for transfers between devices: 396 us -> none  [the longest x1 102 us: on_device(): lax.all_gather(down_weight, 'dp', axis=1, tiled=True)]
    pad x154 -> x2, local copies, waits for them, and re-layouts: 292 us -> 1.93 us  [pad_dim(): return jnp.pad(array, widths)]
    slice x130 -> x28, local copies, waits for them, and re-layouts: 184 us -> 20.4 us  [the longest x8 3.94 us: vb_part(): return jnp.concatenate([whole[:sent], whole[lanes:lanes + sent]], axis=0)]
    ppermute x0 -> x83, starting transfers between devices: none -> 95.5 us  [the longest x34 48.8 us: hop_outer(): return lax.ppermute(value, self.axis, pairs)]
    psum x2 -> x0, blocking collectives: 81.2 us -> none  [the longest x1 43.2 us: on_device(): lax.psum((grad_gain_mix, grad_gain_ffn), ('dp', 'chan'))]
    add_any x61 -> x0, other arithmetic: 66.6 us -> none  [the longest x24 37.5 us: link(): return (earlier[0] * later[0], later[0] * earlier[1] + later[1])]
  transfers between devices with their start and end apart: 21 -> 84, of which waited for: 17 -> 31; matrix products, arithmetic and copies ran while one was open for 22% -> 19% of each run, Pallas kernels for 0% -> 4%
where the time goes in v1:
time: 1040 us; the launch traced here: 1030 us
  waiting for transfers between devices  552 us (53%)
  matrix products  190 us (18%)
  starting transfers between devices  95.5 us (9%)
  local copies, waits for them, and re-layouts  78.3 us (8%)
  Pallas kernels  58 us (6%)
  other arithmetic  44.7 us (4%)
  between operations  15.9 us (2%)
    ppermute x34, waiting for transfers between devices, hop_outer(): return lax.ppermute(value, self.axis, pairs)  276 us
    ppermute x36, waiting for transfers between devices, hop_inner(): return lax.ppermute(value, self.axis, pairs)  229 us
    ppermute x34, starting transfers between devices, hop_outer(): return lax.ppermute(value, self.axis, pairs)  48.8 us
    dot_general x8, matrix products, on_device(): lax.dot_general(columns(mid_full, t * dp.outer + s), back_both, contract_...  47.7 us
    unnamed x194, local copies, waits for them, and re-layouts  45.1 us
    psum x1, waiting for transfers between devices, on_device(): gate_grads = lax.psum(gate_grads, 'dp')  42.2 us
    ppermute x36, starting transfers between devices, hop_inner(): return lax.ppermute(value, self.axis, pairs)  33.5 us
    pallas_call x1, Pallas kernels, recur_backward(): pl.pallas_call(body, out_shape=(jax.ShapeDtypeStruct((seq_len, 2 * lanes)...  27.2 us
  transfers between devices with their start and end apart: 84, of which 31 were waited for; matrix products, arithmetic and copies ran while one was open for 19% of the time, Pallas kernels for 4%

profile of v1, /device:TPU:0, one launch (start us, length us, event | category | flops | bytes accessed | tf_op | source)
XLA Modules:
  0.0 1034.6 jit_solution(16863911074204609455)
XLA Ops:
  23.2 14.4 %collective-permute-done.7 = bf16[688,256]{1,0:T(8,128)(2,1)} collective-permute-done((bf16[688,256]{1,0:T(8,128)(2,1)}, bf16[688,256]{1,0:T(8,128)(2,1)}, u32[]{:S(2)}, u32[]{:S(2)}) %collective-permute-start.7) | collective-permute-done | bytes 352288 | tf_op jit(solution)/shard_map/ppermute | solution.py:49
  64.7 21.7 %collective-permute-done.12 = bf16[688,256]{1,0:T(8,128)(2,1)S(1)} collective-permute-done((bf16[688,256]{1,0:T(8,128)(2,1)S(1)}, bf16[688,256]{1,0:T(8,128)(2,1)S(1)}, u32[]{:S(2)}, u32[]{:S(2)}) %collective-permute-start.12) | collective-permute-done | bytes 352288 | tf_op jit(solution)/shard_map/ppermute | solution.py:49
  100.5 11.0 %collective-permute-done.2 = bf16[1376,256]{1,0:T(8,128)(2,1)S(1)} collective-permute-done((bf16[1376,256]{1,0:T(8,128)(2,1)S(1)}, bf16[1376,256]{1,0:T(8,128)(2,1)S(1)}, u32[]{:S(2)}, u32[]{:S(2)}) %collective-permute-start.2) | collective-permute-done | bytes 704544 | tf_op jit(solution)/shard_map/ppermute | solution.py:49
  118.0 8.3 collective-permute-done.6
  132.5 9.5 fusion.25.x_ref.y_ref
  142.0 20.2 %recur_forward.1 = (bf16[1024,768]{1,0:T(8,128)(2,1)S(1)}, bf16[1024,768]{1,0:T(8,128)(2,1)S(1)}, f32[1024,1536]{1,0:T(8,128)}, f32[1024,768]{1,0:T(8,128)}) custom-call(s32[4]{0:T(128)S(1)} %fusion.116.places_ref, s32[4]{0:T(128)S(1)} %bitcast.109, f32[1024,1536]{1,0:T(8,128)} %fusion.25.x_ref.y_ref, f32[1024,1536]{1,0:T(8,128)} %fusion.25.x_ref.y_ref, ...), custom_call_target="tpu_custom_call" | custom-call | flops 2415919104 | bytes 25165824 | tf_op jit(solution)/shard_map/recur_forward/pallas_call | solution.py:341
  183.3 45.2 %collective-permute-done.25 = bf16[1536,256]{1,0:T(8,128)(2,1)} collective-permute-done((bf16[1536,256]{1,0:T(8,128)(2,1)}, bf16[1536,256]{1,0:T(8,128)(2,1)}, u32[]{:S(2)}, u32[]{:S(2)}) %collective-permute-start.25) | collective-permute-done | bytes 786464 | tf_op jit(solution)/shard_map/ppermute | solution.py:49
  238.9 12.2 %collective-permute-done.26 = bf16[1536,256]{1,0:T(8,128)(2,1)S(1)} collective-permute-done((bf16[1536,256]{1,0:T(8,128)(2,1)}, bf16[1536,256]{1,0:T(8,128)(2,1)S(1)}, u32[]{:S(2)}, u32[]{:S(2)}) %collective-permute-start.26) | collective-permute-done | bytes 786464 | tf_op jit(solution)/shard_map/ppermute | solution.py:49
  263.3 36.0 %collective-permute-done.27 = bf16[1536,256]{1,0:T(8,128)(2,1)S(1)} collective-permute-done((bf16[1536,256]{1,0:T(8,128)(2,1)S(1)}, bf16[1536,256]{1,0:T(8,128)(2,1)S(1)}, u32[]{:S(2)}, u32[]{:S(2)}) %collective-permute-start.27) | collective-permute-done | bytes 786464 | tf_op jit(solution)/shard_map/ppermute | solution.py:49
  307.5 12.6 %collective-permute-done.29 = bf16[1536,256]{1,0:T(8,128)(2,1)S(1)} collective-permute-done((bf16[1536,256]{1,0:T(8,128)(2,1)}, bf16[1536,256]{1,0:T(8,128)(2,1)S(1)}, u32[]{:S(2)}, u32[]{:S(2)}) %collective-permute-start.29) | collective-permute-done | bytes 786464 | tf_op jit(solution)/shard_map/ppermute | solution.py:57
  321.7 14.9 %collective-permute-done.30 = bf16[1536,256]{1,0:T(8,128)(2,1)S(1)} collective-permute-done((bf16[1536,256]{1,0:T(8,128)(2,1)S(1)}, bf16[1536,256]{1,0:T(8,128)(2,1)S(1)}, u32[]{:S(2)}, u32[]{:S(2)}) %collective-permute-start.30) | collective-permute-done | bytes 786464 | tf_op jit(solution)/shard_map/ppermute | solution.py:57
  346.3 44.7 %collective-permute-done.31 = bf16[1536,256]{1,0:T(8,128)(2,1)S(1)} collective-permute-done((bf16[1536,256]{1,0:T(8,128)(2,1)S(1)}, bf16[1536,256]{1,0:T(8,128)(2,1)S(1)}, u32[]{:S(2)}, u32[]{:S(2)}) %collective-permute-start.31) | collective-permute-done | bytes 786464 | tf_op jit(solution)/shard_map/ppermute | solution.py:57
  397.5 27.2 %collective-permute-done.23 = bf16[256,3072]{1,0:T(8,128)(2,1)S(1)} collective-permute-done((bf16[256,3072]{1,0:T(8,128)(2,1)S(1)}, bf16[256,3072]{1,0:T(8,128)(2,1)S(1)}, u32[]{:S(2)}, u32[]{:S(2)}) %collective-permute-start.23) | collective-permute-done | bytes 1572896 | tf_op jit(solution)/shard_map/ppermute | solution.py:57
  426.0 31.1 %collective-permute-done.24 = bf16[256,3072]{1,0:T(8,128)(2,1)S(1)} collective-permute-done((bf16[256,3072]{1,0:T(8,128)(2,1)S(1)}, bf16[256,3072]{1,0:T(8,128)(2,1)S(1)}, u32[]{:S(2)}, u32[]{:S(2)}) %collective-permute-start.24) | collective-permute-done | bytes 1572896 | tf_op jit(solution)/shard_map/ppermute | solution.py:57
  460.7 17.8 %fusion.147 = f32[1024,3072]{1,0:T(8,128)} fusion(bf16[2048,3072]{1,0:T(8,128)(2,1)} %constant_dynamic-update-slice_fusion.18, bf16[512,2048]{1,0:T(8,128)(2,1)S(1)} %collective-permute-done.17, bf16[256,2048]{1,0:T(8,128)(2,1)S(1)} %collective-permute-done.16, bf16[256,2048]{1,0:T(8,128)(2,1)S(1)} %multiply_convert_fusion.2), kind=kOutput, calls=%fused_computation.351 | convolution fusion | flops 12897484800 | bytes 29360128 | tf_op jit(solution)/shard_map/dot_general | solution.py:628
  478.5 18.7 %fusion.10 = (bf16[1024,1536]{1,0:T(8,128)(2,1)}, bf16[1024,1536]{1,0:T(8,128)(2,1)}, bf16[1024,1536]{1,0:T(8,128)(2,1)}) fusion(f32[1024,3072]{1,0:T(8,128)} %fusion.147, bf16[1536,2048]{1,0:T(8,128)(2,1)} %copy-done.48, bf16[512,2048]{1,0:T(8,128)(2,1)} %copy-done.37, bf16[256,2048]{1,0:T(8,128)(2,1)} %collective-permute-done.34, ...), kind=kOutput, calls=%fused_computation.16 | convolution fusion | flops 6492782592 | bytes 32505856 | tf_op jit(solution)/shard_map/dot_general | solution.py:638
  508.8 16.5 %fusion.148 = f32[1024,2048]{1,0:T(8,128)S(1)} fusion(bf16[2048,3072]{1,0:T(8,128)(2,1)} %constant_dynamic-update-slice_fusion.18, bf16[1024,1536]{1,0:T(8,128)(2,1)S(1)} %copy-done.72, bf16[1024,1536]{1,0:T(8,128)(2,1)S(1)} %copy-done.68), kind=kOutput, calls=%fused_computation.352 | convolution fusion | flops 12897484800 | bytes 27262976 | tf_op jit(solution)/shard_map/dot_general | solution.py:642
  525.3 9.3 fusion.166
  556.9 9.0 collective-permute-done.79
  575.5 58.0 %collective-permute-done.72 = bf16[256,3072]{1,0:T(8,128)(2,1)} collective-permute-done((bf16[256,3072]{1,0:T(8,128)(2,1)}, bf16[256,3072]{1,0:T(8,128)(2,1)}, u32[]{:S(2)}, u32[]{:S(2)}) %collective-permute-start.72) | collective-permute-done | bytes 1572896 | tf_op jit(solution)/shard_map/ppermute | solution.py:57
  641.3 13.3 %collective-permute-done.33 = bf16[256,2048]{1,0:T(8,128)(2,1)S(1)} collective-permute-done((bf16[256,2048]{1,0:T(8,128)(2,1)S(1)}, bf16[256,2048]{1,0:T(8,128)(2,1)S(1)}, u32[]{:S(2)}, u32[]{:S(2)}) %collective-permute-start.33) | collective-permute-done | bytes 1048608 | tf_op jit(solution)/shard_map/ppermute | solution.py:49
  659.3 32.9 %collective-permute-done.80 = bf16[1536,256]{1,0:T(8,128)(2,1)S(1)} collective-permute-done((bf16[1536,256]{1,0:T(8,128)(2,1)S(1)}, bf16[1536,256]{1,0:T(8,128)(2,1)S(1)}, u32[]{:S(2)}, u32[]{:S(2)}) %collective-permute-start.80) | collective-permute-done | bytes 786464 | tf_op jit(solution)/shard_map/ppermute | solution.py:49
  704.6 7.9 collective-permute-done.38
  729.2 34.9 %collective-permute-done.82 = bf16[1536,256]{1,0:T(8,128)(2,1)S(1)} collective-permute-done((bf16[1536,256]{1,0:T(8,128)(2,1)S(1)}, bf16[1536,256]{1,0:T(8,128)(2,1)S(1)}, u32[]{:S(2)}, u32[]{:S(2)}) %collective-permute-start.82) | collective-permute-done | bytes 786464 | tf_op jit(solution)/shard_map/ppermute | solution.py:49
  791.2 27.2 %recur_backward.1 = (bf16[1024,1536]{1,0:T(8,128)(2,1)}, bf16[1024,1536]{1,0:T(8,128)(2,1)}, f32[8,768]{1,0:T(8,128)S(1)}) custom-call(s32[4]{0:T(128)S(1)} %copy-done.15, s32[4]{0:T(128)S(1)} %bitcast.110, f32[1024,768]{1,0:T(8,128)} %fusion.19.bm_ref, f32[1024,1536]{1,0:T(8,128)} %fusion.25.x_ref.y_ref, f32[1024,1536]{1,0:T(8,128)} %fusion.25.x_ref.y_ref, ...), custom_call_target="tpu_custom_call" | custom-call | flops 2415919104 | bytes 28311552 | tf_op jit(solution)/shard_map/recur_backward/pallas_call | solution.py:485
  818.5 8.7 fusion.23
  874.7 16.1 %collective-permute-done.50 = bf16[1376,256]{1,0:T(8,128)(2,1)S(1)} collective-permute-done((bf16[1376,256]{1,0:T(8,128)(2,1)S(1)}, bf16[1376,256]{1,0:T(8,128)(2,1)S(1)}, u32[]{:S(2)}, u32[]{:S(2)}) %collective-permute-start.50) | collective-permute-done | bytes 704544 | tf_op jit(solution)/shard_map/ppermute | solution.py:57
  895.8 8.0 collective-permute-done.61
  907.6 9.2 collective-permute-done.51
  921.7 10.7 %collective-permute-done.62 = bf16[688,256]{1,0:T(8,128)(2,1)S(1)} collective-permute-done((bf16[688,256]{1,0:T(8,128)(2,1)S(1)}, bf16[688,256]{1,0:T(8,128)(2,1)S(1)}, u32[]{:S(2)}, u32[]{:S(2)}) %collective-permute-start.62) | collective-permute-done | bytes 352288 | tf_op jit(solution)/shard_map/ppermute | solution.py:49
  938.8 10.1 collective-permute-done.52
  950.3 42.2 %all-reduce.16.cloned.1.call-done = f32[8,171,171]{2,1,0:T(8,128)} async-done(((f32[8,171,171]{2,1,0:T(8,128)}), f32[8,171,171]{2,1,0:T(8,128)}) %all-reduce.16.cloned.1.call-update) | async-done | bytes 935728 | tf_op jit(solution)/shard_map/psum | solution.py:705
  (490 shorter events, 359.2 us)
Async XLA Ops:
  7.2 985.2 %all-reduce.16.cloned.1.call-start = ((), (), s32[]{:S(2)}) async-start(), calls=%async_computation | async-start | bytes 2883584 | tf_op jit(solution)/shard_map/psum | solution.py:705
  14.7 99.3 %collective-permute-start.3 = (bf16[1376,256]{1,0:T(8,128)(2,1)}, bf16[1376,256]{1,0:T(8,128)(2,1)}, u32[]{:S(2)}, u32[]{:S(2)}) collective-permute-start(bf16[1376,256]{1,0:T(8,128)(2,1)} %get-tuple-element.117), channel_id=1, source_target_pairs={{0,4},{4,0},{8,12},{12,8},{16,20},{20,16},{24,28},{28,24},{1,5},{5... | collective-permute-start | bytes 2113544 | tf_op jit(solution)/shard_map/ppermute | solution.py:57
  51.5 64.6 %collective-permute-start.4 = (bf16[1376,256]{1,0:T(8,128)(2,1)}, bf16[1376,256]{1,0:T(8,128)(2,1)S(1)}, u32[]{:S(2)}, u32[]{:S(2)}) collective-permute-start(bf16[1376,256]{1,0:T(8,128)(2,1)} %collective-permute-done), channel_id=1, source_target_pairs={{0,4},{4,0},{8,12},{12,8},{16,20},{20,16},{24,28},{28,24},{1,5},{5... | collective-permute-start | bytes 2113544 | tf_op jit(solution)/shard_map/ppermute | solution.py:57
  170.2 85.1 %collective-permute-start.14 = (bf16[512,2048]{1,0:T(8,128)(2,1)}, bf16[512,2048]{1,0:T(8,128)(2,1)}, u32[]{:S(2)}, u32[]{:S(2)}) collective-permute-start(bf16[512,2048]{1,0:T(8,128)(2,1)} %slice.715), channel_id=1, source_target_pairs={{0,1},{1,0},{2,3},{3,2},{4,5},{5,4},{6,7},{7,6},{8,9},{9,8},{10,11... | collective-permute-start | bytes 6291464 | tf_op jit(solution)/shard_map/ppermute | solution.py:57
  173.5 65.3 %collective-permute-start.18 = (bf16[256,3072]{1,0:T(8,128)(2,1)}, bf16[256,3072]{1,0:T(8,128)(2,1)}, u32[]{:S(2)}, u32[]{:S(2)}) collective-permute-start(bf16[256,3072]{1,0:T(8,128)(2,1)} %get-tuple-element.113), channel_id=1, source_target_pairs={{0,24},{4,28},{8,0},{12,4},{16,8},{20,12},{24,16},{28,20},{1,25},{... | collective-permute-start | bytes 4718600 | tf_op jit(solution)/shard_map/ppermute | solution.py:49
  177.8 214.6 %collective-permute-start.21 = (bf16[256,3072]{1,0:T(8,128)(2,1)}, bf16[256,3072]{1,0:T(8,128)(2,1)}, u32[]{:S(2)}, u32[]{:S(2)}) collective-permute-start(bf16[256,3072]{1,0:T(8,128)(2,1)} %get-tuple-element.113), channel_id=1, source_target_pairs={{0,4},{4,0},{8,12},{12,8},{16,20},{20,16},{24,28},{28,24},{1,5},{5... | collective-permute-start | bytes 4718600 | tf_op jit(solution)/shard_map/ppermute | solution.py:57
  180.4 55.4 %collective-permute-start.34 = (bf16[256,2048]{1,0:T(8,128)(2,1)S(1)}, bf16[256,2048]{1,0:T(8,128)(2,1)}, u32[]{:S(2)}, u32[]{:S(2)}) collective-permute-start(bf16[256,2048]{1,0:T(8,128)(2,1)S(1)} %reorder_columns.4), channel_id=1, source_target_pairs={{0,2},{1,3},{2,0},{3,1},{4,6},{5,7},{6,4},{7,5},{8,10},{9,11},{10,... | collective-permute-start | bytes 3145736 | tf_op jit(solution)/shard_map/ppermute | solution.py:49
  235.8 63.7 %collective-permute-start.28 = (bf16[1536,256]{1,0:T(8,128)(2,1)}, bf16[1536,256]{1,0:T(8,128)(2,1)S(1)}, u32[]{:S(2)}, u32[]{:S(2)}) collective-permute-start(bf16[1536,256]{1,0:T(8,128)(2,1)} %param.36), channel_id=1, source_target_pairs={{0,4},{4,0},{8,12},{12,8},{16,20},{20,16},{24,28},{28,24},{1,5},{5... | collective-permute-start | bytes 2359304 | tf_op jit(solution)/shard_map/ppermute | solution.py:57
  238.8 62.3 %collective-permute-start.19 = (bf16[256,3072]{1,0:T(8,128)(2,1)}, bf16[256,3072]{1,0:T(8,128)(2,1)S(1)}, u32[]{:S(2)}, u32[]{:S(2)}) collective-permute-start(bf16[256,3072]{1,0:T(8,128)(2,1)} %collective-permute-done.18), channel_id=1, source_target_pairs={{0,24},{4,28},{8,0},{12,4},{16,8},{20,12},{24,16},{28,20},{1,25},{... | collective-permute-start | bytes 4718600 | tf_op jit(solution)/shard_map/ppermute | solution.py:49
  336.6 59.7 %collective-permute-start.22 = (bf16[256,3072]{1,0:T(8,128)(2,1)}, bf16[256,3072]{1,0:T(8,128)(2,1)S(1)}, u32[]{:S(2)}, u32[]{:S(2)}) collective-permute-start(bf16[256,3072]{1,0:T(8,128)(2,1)} %collective-permute-done.18), channel_id=1, source_target_pairs={{0,4},{4,0},{8,12},{12,8},{16,20},{20,16},{24,28},{28,24},{1,5},{5... | collective-permute-start | bytes 4718600 | tf_op jit(solution)/shard_map/ppermute | solution.py:57
  338.2 52.7 %collective-permute-start.31 = (bf16[1536,256]{1,0:T(8,128)(2,1)S(1)}, bf16[1536,256]{1,0:T(8,128)(2,1)S(1)}, u32[]{:S(2)}, u32[]{:S(2)}) collective-permute-start(bf16[1536,256]{1,0:T(8,128)(2,1)S(1)} %collective-permute-done.27), channel_id=1, source_target_pairs={{0,4},{4,0},{8,12},{12,8},{16,20},{20,16},{24,28},{28,24},{1,5},{5... | collective-permute-start | bytes 2359304 | tf_op jit(solution)/shard_map/ppermute | solution.py:57
  343.5 81.1 %collective-permute-start.23 = (bf16[256,3072]{1,0:T(8,128)(2,1)S(1)}, bf16[256,3072]{1,0:T(8,128)(2,1)S(1)}, u32[]{:S(2)}, u32[]{:S(2)}) collective-permute-start(bf16[256,3072]{1,0:T(8,128)(2,1)S(1)} %collective-permute-done.19), channel_id=1, source_target_pairs={{0,4},{4,0},{8,12},{12,8},{16,20},{20,16},{24,28},{28,24},{1,5},{5... | collective-permute-start | bytes 4718600 | tf_op jit(solution)/shard_map/ppermute | solution.py:57
  345.0 112.0 %collective-permute-start.24 = (bf16[256,3072]{1,0:T(8,128)(2,1)S(1)}, bf16[256,3072]{1,0:T(8,128)(2,1)S(1)}, u32[]{:S(2)}, u32[]{:S(2)}) collective-permute-start(bf16[256,3072]{1,0:T(8,128)(2,1)S(1)} %collective-permute-done.20), channel_id=1, source_target_pairs={{0,4},{4,0},{8,12},{12,8},{16,20},{20,16},{24,28},{28,24},{1,5},{5... | collective-permute-start | bytes 4718600 | tf_op jit(solution)/shard_map/ppermute | solution.py:57
  390.9 67.4 %collective-permute-start.17 = (bf16[512,2048]{1,0:T(8,128)(2,1)S(1)}, bf16[512,2048]{1,0:T(8,128)(2,1)S(1)}, u32[]{:S(2)}, u32[]{:S(2)}) collective-permute-start(bf16[512,2048]{1,0:T(8,128)(2,1)S(1)} %pad_maximum_fusion.5), channel_id=1, source_target_pairs={{0,1},{1,0},{2,3},{3,2},{4,5},{5,4},{6,7},{7,6},{8,9},{9,8},{10,11... | collective-permute-start | bytes 6291464 | tf_op jit(solution)/shard_map/ppermute | solution.py:57
  547.0 110.8 %collective-permute-start.78 = (bf16[1536,256]{1,0:T(8,128)(2,1)}, bf16[1536,256]{1,0:T(8,128)(2,1)}, u32[]{:S(2)}, u32[]{:S(2)}) collective-permute-start(bf16[1536,256]{1,0:T(8,128)(2,1)} %convolution_convert_fusion.5), channel_id=1, source_target_pairs={{0,4},{4,0},{8,12},{12,8},{16,20},{20,16},{24,28},{28,24},{1,5},{5... | collective-permute-start | bytes 2359304 | tf_op jit(solution)/shard_map/ppermute | solution.py:57
  547.5 167.9 %collective-permute-start.77 = (bf16[1536,256]{1,0:T(8,128)(2,1)}, bf16[1536,256]{1,0:T(8,128)(2,1)}, u32[]{:S(2)}, u32[]{:S(2)}) collective-permute-start(bf16[1536,256]{1,0:T(8,128)(2,1)} %convolution_convert_fusion.6), channel_id=1, source_target_pairs={{0,4},{4,0},{8,12},{12,8},{16,20},{20,16},{24,28},{28,24},{1,5},{5... | collective-permute-start | bytes 2359304 | tf_op jit(solution)/shard_map/ppermute | solution.py:57
  565.9 67.5 %collective-permute-start.72 = (bf16[256,3072]{1,0:T(8,128)(2,1)}, bf16[256,3072]{1,0:T(8,128)(2,1)}, u32[]{:S(2)}, u32[]{:S(2)}) collective-permute-start(bf16[256,3072]{1,0:T(8,128)(2,1)} %convolution_convert_fusion), channel_id=1, source_target_pairs={{0,4},{4,0},{8,12},{12,8},{16,20},{20,16},{24,28},{28,24},{1,5},{5... | collective-permute-start | bytes 4718600 | tf_op jit(solution)/shard_map/ppermute | solution.py:57
  571.3 124.6 %collective-permute-start.71 = (bf16[256,3072]{1,0:T(8,128)(2,1)}, bf16[256,3072]{1,0:T(8,128)(2,1)}, u32[]{:S(2)}, u32[]{:S(2)}) collective-permute-start(bf16[256,3072]{1,0:T(8,128)(2,1)} %convolution_convert_fusion.1), channel_id=1, source_target_pairs={{0,4},{4,0},{8,12},{12,8},{16,20},{20,16},{24,28},{28,24},{1,5},{5... | collective-permute-start | bytes 4718600 | tf_op jit(solution)/shard_map/ppermute | solution.py:57
  572.9 67.6 %collective-permute-start.37 = (bf16[256,2048]{1,0:T(8,128)(2,1)S(1)}, bf16[256,2048]{1,0:T(8,128)(2,1)S(1)}, u32[]{:S(2)}, u32[]{:S(2)}) collective-permute-start(bf16[256,2048]{1,0:T(8,128)(2,1)S(1)} %slice.717), channel_id=1, source_target_pairs={{0,2},{1,3},{2,0},{3,1},{4,6},{5,7},{6,4},{7,5},{8,10},{9,11},{10,... | collective-permute-start | bytes 3145736 | tf_op jit(solution)/shard_map/ppermute | solution.py:49
  640.5 57.0 %collective-permute-start.73 = (bf16[256,3072]{1,0:T(8,128)(2,1)}, bf16[256,3072]{1,0:T(8,128)(2,1)}, u32[]{:S(2)}, u32[]{:S(2)}) collective-permute-start(bf16[256,3072]{1,0:T(8,128)(2,1)} %fusion.16), channel_id=1, source_target_pairs={{0,8},{4,12},{8,16},{12,20},{16,24},{20,28},{24,0},{28,4},{1,9},{5... | collective-permute-start | bytes 4718600 | tf_op jit(solution)/shard_map/ppermute | solution.py:49
  657.8 69.8 %collective-permute-start.76 = (bf16[1536,256]{1,0:T(8,128)(2,1)}, bf16[1536,256]{1,0:T(8,128)(2,1)}, u32[]{:S(2)}, u32[]{:S(2)}) collective-permute-start(bf16[1536,256]{1,0:T(8,128)(2,1)} %convolution_convert_fusion.7), channel_id=1, source_target_pairs={{0,4},{4,0},{8,12},{12,8},{16,20},{20,16},{24,28},{28,24},{1,5},{5... | collective-permute-start | bytes 2359304 | tf_op jit(solution)/shard_map/ppermute | solution.py:57
  695.9 73.7 %collective-permute-start.70 = (bf16[256,3072]{1,0:T(8,128)(2,1)}, bf16[256,3072]{1,0:T(8,128)(2,1)}, u32[]{:S(2)}, u32[]{:S(2)}) collective-permute-start(bf16[256,3072]{1,0:T(8,128)(2,1)} %convolution_convert_fusion.2), channel_id=1, source_target_pairs={{0,4},{4,0},{8,12},{12,8},{16,20},{20,16},{24,28},{28,24},{1,5},{5... | collective-permute-start | bytes 4718600 | tf_op jit(solution)/shard_map/ppermute | solution.py:57
  712.6 57.1 %collective-permute-start.74 = (bf16[256,3072]{1,0:T(8,128)(2,1)}, bf16[256,3072]{1,0:T(8,128)(2,1)}, u32[]{:S(2)}, u32[]{:S(2)}) collective-permute-start(bf16[256,3072]{1,0:T(8,128)(2,1)} %fusion.17), channel_id=1, source_target_pairs={{0,8},{4,12},{8,16},{12,20},{16,24},{20,28},{24,0},{28,4},{1,9},{5... | collective-permute-start | bytes 4718600 | tf_op jit(solution)/shard_map/ppermute | solution.py:49
  715.5 61.3 %collective-permute-start.39 = (bf16[512,2048]{1,0:T(8,128)(2,1)}, bf16[512,2048]{1,0:T(8,128)(2,1)}, u32[]{:S(2)}, u32[]{:S(2)}) collective-permute-start(bf16[512,2048]{1,0:T(8,128)(2,1)} %pad_maximum_fusion.7), channel_id=1, source_target_pairs={{0,1},{1,0},{2,3},{3,2},{4,5},{5,4},{6,7},{7,6},{8,9},{9,8},{10,11... | collective-permute-start | bytes 6291464 | tf_op jit(solution)/shard_map/ppermute | solution.py:57
  727.6 135.0 %collective-permute-start.69 = (bf16[256,3072]{1,0:T(8,128)(2,1)}, bf16[256,3072]{1,0:T(8,128)(2,1)}, u32[]{:S(2)}, u32[]{:S(2)}) collective-permute-start(bf16[256,3072]{1,0:T(8,128)(2,1)} %convolution_convert_fusion.3), channel_id=1, source_target_pairs={{0,4},{4,0},{8,12},{12,8},{16,20},{20,16},{24,28},{28,24},{1,5},{5... | collective-permute-start | bytes 4718600 | tf_op jit(solution)/shard_map/ppermute | solution.py:57
  776.8 87.3 %collective-permute-start.75 = (bf16[256,3072]{1,0:T(8,128)(2,1)}, bf16[256,3072]{1,0:T(8,128)(2,1)}, u32[]{:S(2)}, u32[]{:S(2)}) collective-permute-start(bf16[256,3072]{1,0:T(8,128)(2,1)} %fusion.18), channel_id=1, source_target_pairs={{0,8},{4,12},{8,16},{12,20},{16,24},{20,28},{24,0},{28,4},{1,9},{5... | collective-permute-start | bytes 4718600 | tf_op jit(solution)/shard_map/ppermute | solution.py:49
  841.8 75.2 %collective-permute-start.40 = (bf16[512,2048]{1,0:T(8,128)(2,1)}, bf16[512,2048]{1,0:T(8,128)(2,1)}, u32[]{:S(2)}, u32[]{:S(2)}) collective-permute-start(bf16[512,2048]{1,0:T(8,128)(2,1)} %slice.712), channel_id=1, source_target_pairs={{0,1},{1,0},{2,3},{3,2},{4,5},{5,4},{6,7},{7,6},{8,9},{9,8},{10,11... | collective-permute-start | bytes 6291464 | tf_op jit(solution)/shard_map/ppermute | solution.py:57
  843.4 52.0 %collective-permute-start.59 = (bf16[688,256]{1,0:T(8,128)(2,1)}, bf16[688,256]{1,0:T(8,128)(2,1)}, u32[]{:S(2)}, u32[]{:S(2)}) collective-permute-start(bf16[688,256]{1,0:T(8,128)(2,1)} %slice.721), channel_id=1, source_target_pairs={{0,4},{4,0},{8,12},{12,8},{16,20},{20,16},{24,28},{28,24},{1,5},{5... | collective-permute-start | bytes 1056776 | tf_op jit(solution)/shard_map/ppermute | solution.py:57
  895.4 102.4 %collective-permute-start.57 = (bf16[688,256]{1,0:T(8,128)(2,1)}, bf16[688,256]{1,0:T(8,128)(2,1)}, u32[]{:S(2)}, u32[]{:S(2)}) collective-permute-start(bf16[688,256]{1,0:T(8,128)(2,1)} %slice.723), channel_id=1, source_target_pairs={{0,4},{4,0},{8,12},{12,8},{16,20},{20,16},{24,28},{28,24},{1,5},{5... | collective-permute-start | bytes 1056776 | tf_op jit(solution)/shard_map/ppermute | solution.py:57
  921.2 80.3 %collective-permute-start.47 = (bf16[1376,256]{1,0:T(8,128)(2,1)}, bf16[1376,256]{1,0:T(8,128)(2,1)}, u32[]{:S(2)}, u32[]{:S(2)}) collective-permute-start(bf16[1376,256]{1,0:T(8,128)(2,1)} %pad_maximum_fusion.8), channel_id=1, source_target_pairs={{0,4},{4,0},{8,12},{12,8},{16,20},{20,16},{24,28},{28,24},{1,5},{5... | collective-permute-start | bytes 2113544 | tf_op jit(solution)/shard_map/ppermute | solution.py:57
  932.4 64.3 %collective-permute-start.41 = (bf16[256,2048]{1,0:T(8,128)(2,1)}, bf16[256,2048]{1,0:T(8,128)(2,1)S(1)}, u32[]{:S(2)}, u32[]{:S(2)}) collective-permute-start(bf16[256,2048]{1,0:T(8,128)(2,1)} %slice.716), channel_id=1, source_target_pairs={{0,2},{1,3},{2,0},{3,1},{4,6},{5,7},{6,4},{7,5},{8,10},{9,11},{10,... | collective-permute-start | bytes 3145736 | tf_op jit(solution)/shard_map/ppermute | solution.py:49
  938.8 59.0 %collective-permute-start.63 = (bf16[688,256]{1,0:T(8,128)(2,1)}, bf16[688,256]{1,0:T(8,128)(2,1)}, u32[]{:S(2)}, u32[]{:S(2)}) collective-permute-start(bf16[688,256]{1,0:T(8,128)(2,1)} %fusion.51), channel_id=1, source_target_pairs={{0,8},{4,12},{8,16},{12,20},{16,24},{20,28},{24,0},{28,4},{1,9},{5... | collective-permute-start | bytes 1056776 | tf_op jit(solution)/shard_map/ppermute | solution.py:49
  (130 other events, 2737.7 us)
Sparse Core Ops, SparseCore 0:
  849.6 142.8 all-reduce.15

commit v2 on v1

v2 whole, which is shorter than its diff:
```python
from functools import partial

import jax
import jax.numpy as jnp
from jax import lax
from jax.experimental import pallas as pl
from jax.experimental.pallas import tpu as pltpu
from jax.sharding import PartitionSpec as P

epsilon = 1e-06
decay_scale = 8.0
floor_value = 0.0001
gelu_root = 0.7978845608
gelu_cube = 0.044715
floats = jnp.float32
halves = jnp.bfloat16
contract_last = (((1,), (1,)), ((), ()))
contract_first = (((0,), (0,)), ((), ()))
CHUNK = 16
DP, CHAN = "dp", "chan"
VMEM_BYTES = 48 * 1024 * 1024
HEAVY = pl.CostEstimate(flops=2 * 10**11, bytes_accessed=1, transcendentals=0)


def round_up(number, unit):
    return -(-number // unit) * unit


def pad_dim(array, axis, size):
    widths = [(0, 0)] * array.ndim
    widths[axis] = (0, size - array.shape[axis])
    return jnp.pad(array, widths)


class Ring:
    def __init__(self, axis, inner):
        self.axis = axis
        self.count = lax.axis_size(axis)
        outer = self.count // inner
        self.path = [(o, 0) for o in range(outer)]
        for n, o in enumerate(reversed(range(outer))):
            columns = list(range(1, inner))
            self.path += [(o, i) for i in (reversed(columns) if n % 2 else columns)]
        self.path = [o * inner + i for o, i in self.path]
        spots = [self.path.index(i) for i in range(self.count)]
        self.spot = self.look(spots, lax.axis_index(axis))
        far = self.count // 2
        self.distances = [far]
        for j in range(1, far):
            self.distances += [far + j, far - j]
        self.distances += [0]
        self.slots = {distance: j for j, distance in enumerate(self.distances)}

    def look(self, table, index):
        return sum(jnp.where(index == i, entry, 0) for i, entry in enumerate(table))

    def hop(self, value, step):
        pairs = [
            (self.path[n], self.path[(n + step) % self.count]) for n in range(self.count)
        ]
        return lax.ppermute(value, self.axis, pairs)

    def order(self):
        ahead = self.look(self.distances, jnp.arange(self.count, dtype=jnp.int32))
        return self.look(self.path, (self.spot + ahead) % self.count).astype(jnp.int32)

    def ways(self, flip):
        ahead = (self.count - 1) // 2 if flip else self.count // 2
        return [
            (AHEAD, list(range(1, ahead + 1)), -1),
            (BACK, list(range(self.count - 1, ahead, -1)), 1),
        ]


LINK_RATE = 46e3
HOP_COST = 3.5
EARLY = 4.0
QUEUED = 2.5
CORE, AHEAD, BACK, CHIPS, CROSS, TWIN, SMALL = range(7)
DEPTHS = {AHEAD: 1, BACK: 1, CHIPS: 9, CROSS: 1, TWIN: 1, SMALL: 2}
STARTS = {AHEAD: 1.5, BACK: 0.8, CHIPS: 0.5, CROSS: 1.5, TWIN: 1.5, SMALL: 2.0}
HOPPING = (AHEAD, BACK, CROSS, TWIN, SMALL)
HOPS = 5
MARGINS = {CORE: 3.0, AHEAD: 0.5, BACK: 0.5, CHIPS: 1.0, CROSS: 0.5, TWIN: 0.5, SMALL: 2.0}


class Task:
    def __init__(self, number, resource, cost, needs, run, bias):
        self.number, self.resource, self.cost, self.needs = number, resource, cost, needs
        self.run, self.bias, self.level, self.users = run, bias, 0.0, []


class Plan:
    def __init__(self):
        self.tasks, self.log = [], []

    def add(self, resource, cost, needs, run, bias=0.0):
        task = Task(len(self.tasks), resource, cost, list(needs), run, bias)
        self.tasks.append(task)
        return task

    def compute(self, cost, needs, run, bias=0.0):
        return self.add(CORE, cost, needs, run, bias)

    def levels(self):
        for task in self.tasks:
            for need in task.needs:
                need.users.append(task)
        for task in reversed(self.tasks):
            task.level = task.cost + max([user.level for user in task.users], default=0.0)

    def execute(self, results):
        self.levels()
        waiting = sorted(self.tasks, key=lambda task: (-task.bias, -task.level))
        values, flying, free, shown = {}, {}, {}, set()
        now, fresh = 0.0, False

        def when(task):
            times = [
                0.0 if need in values else flying[need][0] if need in flying else None
                for need in task.needs
            ]
            if None in times:
                return None
            late = max(times, default=0.0)
            return late + MARGINS[task.resource] if late > 0.0 else 0.0

        def issue(task):
            nonlocal fresh
            ended = [need for need in task.needs if need in flying]
            if task.resource in HOPPING:
                under = sorted(
                    (end, other.number, other)
                    for other, (end, _) in flying.items()
                    if other.resource in HOPPING and other not in ended
                )
                ended += [other for _, _, other in under[: max(0, len(under) + 1 - HOPS)]]
            for need in ended:
                values[need] = flying.pop(need)[1]
                self.log.append((now, 1, need))
                fresh = True
            if fresh:
                wanted = {need for other in waiting for need in other.needs}
                first = {done for done in values if done in results} - shown
                names = sorted(
                    {done for done in values if done in wanted} | first,
                    key=lambda done: done.number,
                )
                tied = lax.optimization_barrier(tuple(values[done] for done in names))
                values.update(zip(names, tied))
                shown.update(first)
                fresh = False
            waiting.remove(task)
            self.log.append((now, 0, task))
            return task.run(values)

        while waiting:
            wakes, chosen = [], None
            for task in waiting:
                at, link = when(task), task.resource
                if at is None:
                    continue
                if link != CORE:
                    ends = sorted(
                        end for other, (end, _) in flying.items() if other.resource == link and end > now
                    )
                    if len(ends) >= DEPTHS[link]:
                        early = EARLY if link in (AHEAD, BACK) and len(ends) == 1 else 0.0
                        at = max(at, ends[-DEPTHS[link]] - early)
                    others = [
                        end
                        for other, (end, _) in flying.items()
                        if other.resource in HOPPING and other not in task.needs
                    ]
                    if link in HOPPING and len(others) >= HOPS:
                        at = max(at, sorted(others)[len(others) - HOPS] + MARGINS[SMALL])
                if at > now:
                    wakes.append(at)
                elif link != CORE:
                    chosen = task
                    break
                elif chosen is None:
                    chosen = task
            if chosen is None:
                now = min(wakes)
                continue
            result = issue(chosen)
            link = chosen.resource
            if link == CORE:
                values[chosen] = result
                now += chosen.cost
                fresh = True
                continue
            behind = free.get(link, 0.0) > now and link != SMALL
            end = free[link] + chosen.cost - QUEUED if behind else now + chosen.cost
            if link != SMALL:
                free[link] = end
            flying[chosen] = (end, result)
            now += STARTS[link]
        for task in results:
            if task in flying:
                values[task] = flying.pop(task)[1]
        self.log.append((now, 1, None))
        return [values[task] for task in results]


def dot_cost(rows, inner, columns):
    return 1.0 + 2.0 * rows * inner * columns / DOT_RATE


def move_cost(count):
    return 1.0 + count / 2e6


def ring_gather(plan, ring, own, count, flip=False, bias=0.0, after={}):
    blocks = {0: own}
    for link, way, step in ring.ways(flip):
        source = own
        for n, distance in enumerate(way):

            def move(v, source=source, step=step):
                return ring.hop(v[source], step)

            held = [after[link, n]] if (link, n) in after else []
            cost = HOP_COST + count * 2 / LINK_RATE
            source = plan.add(link, cost, [source, *held], move, bias)
            blocks[distance] = source
    return blocks


def ring_reduce(plan, ring, parts, count, finish, flip=False, bias=2.0, after=()):
    half = ring.count // 2

    def total(distance, sources):
        slot = ring.slots[distance]
        part = parts[slot // half]
        if not sources:
            return plan.compute(0.0, [part], lambda v: v[part][slot % half], 20.0)

        def add(v):
            terms = [v[part][slot % half], *(v[source] for source in sources)]
            if distance:
                return add_up([(term, 0) for term in terms], halves)
            return finish(sum(term.astype(floats) for term in terms))

        cost = move_cost((2.0 + len(sources)) * count)
        if not distance:
            cost = cost + move_cost(3 * count)
        return plan.compute(cost, [part, *sources], add, 10.0 if distance else -1.0)

    passings = []
    for link, way, step in ring.ways(flip):
        passing = []
        for distance in reversed(way):
            made = total(distance, passing)

            def move(v, made=made, step=step):
                return ring.hop(v[made], -step)

            cost = HOP_COST + count * 2 / LINK_RATE
            passing = [plan.add(link, cost, [made, *after], move, bias)]
        passings.extend(passing)
    return total(0, passings)


def params():
    return pltpu.CompilerParams(vmem_limit_bytes=VMEM_BYTES)


def place(full, piece, at, shape, steps, in_block, in_index, out_block, out_index):
    short = in_block[0] < out_block[0]

    def body(at_ref, in_ref, *refs):
        out_ref = refs[-1]
        if short:
            out_ref[: in_block[0]] = in_ref[...]
            out_ref[in_block[0] :] = jnp.zeros(
                (out_block[0] - in_block[0], out_block[1]), out_ref.dtype
            )
        else:
            out_ref[...] = in_ref[...]

    return pl.pallas_call(
        body,
        out_shape=jax.ShapeDtypeStruct(shape, piece.dtype),
        grid_spec=pltpu.PrefetchScalarGridSpec(
            num_scalar_prefetch=1,
            grid=(steps,),
            in_specs=[
                pl.BlockSpec(in_block, in_index),
                *([] if full is None else [pl.BlockSpec(memory_space=pl.ANY)]),
            ],
            out_specs=pl.BlockSpec(out_block, out_index),
        ),
        input_output_aliases={} if full is None else {2: 0},
        compiler_params=params(),
        cost_estimate=HEAVY,
    )(at, piece, *([] if full is None else [full]))


def add_up(terms, dtype, rows=None):
    rows = rows or terms[0][0].shape[0]
    width = terms[0][0].shape[1]
    steps = next(n for n in (4, 3, 2, 1) if rows % (16 * n) == 0)
    tile = rows // steps

    def body(*refs):
        total = refs[0][...].astype(floats)
        for ref in refs[1:-1]:
            total = total + ref[...].astype(floats)
        refs[-1][...] = total.astype(dtype)

    def spec(first):
        return pl.BlockSpec((tile, width), lambda i: (first // tile + i, 0))

    return pl.pallas_call(
        body,
        out_shape=jax.ShapeDtypeStruct((rows, width), dtype),
        grid=(steps,),
        in_specs=[spec(first) for _, first in terms],
        out_specs=spec(0),
        compiler_params=params(),
        cost_estimate=HEAVY,
    )(*(array for array, _ in terms))


def first_norm(tokens, gain, tiles, own):
    seq_len, width = tokens.shape
    part = seq_len // tiles

    def body(own_ref, tok_ref, gain_ref, out_ref, rows_ref, factor_ref):
        whole = tok_ref[...].astype(floats)
        inverse = lax.rsqrt(jnp.mean(whole * whole, axis=-1, keepdims=True) + epsilon)
        out_ref[...] = (whole * inverse * gain_ref[...]).astype(halves)
        factor_ref[...] = jnp.broadcast_to(inverse, factor_ref.shape)

        @pl.when(pl.program_id(0) == own_ref[0])
        def _():
            rows_ref[...] = tok_ref[...]

    return pl.pallas_call(
        body,
        out_shape=(
            jax.ShapeDtypeStruct((seq_len, width), halves),
            jax.ShapeDtypeStruct((part, width), tokens.dtype),
            jax.ShapeDtypeStruct((seq_len, 128), floats),
        ),
        grid_spec=pltpu.PrefetchScalarGridSpec(
            num_scalar_prefetch=1,
            grid=(tiles,),
            in_specs=[
                pl.BlockSpec((part, width), lambda i, own_ref: (i, 0)),
                pl.BlockSpec((1, width), lambda i, own_ref: (0, 0)),
            ],
            out_specs=(
                pl.BlockSpec((part, width), lambda i, own_ref: (i, 0)),
                pl.BlockSpec((part, width), lambda i, own_ref: (0, 0)),
                pl.BlockSpec((part, 128), lambda i, own_ref: (i, 0)),
            ),
        ),
        compiler_params=params(),
        cost_estimate=HEAVY,
    )(own, tokens, gain.reshape(1, width))


def tile_of(size):
    return max(step for step in range(128, 513, 128) if size % step == 0)


def gradient_blocks(lhs, rhs, order, half, tile=None, keep=None):
    sides, tokens, height = lhs.shape
    count = order.shape[0] // 2
    block = rhs.shape[1] // order.shape[0]
    tile = tile or tile_of(height)
    keep = keep or tile
    steps = height // tile

    def body(order_ref, lhs_ref, *refs):
        turned = lhs_ref[0].T
        for rhs_ref, out_ref in zip(refs[:count], refs[count:]):
            product = jnp.dot(turned, rhs_ref[...], preferred_element_type=floats)
            out_ref[...] = product[:keep].astype(halves)

    def column(j):
        return pl.BlockSpec(
            (tokens, block), lambda side, i, order_ref: (0, order_ref[half * count + j])
        )

    return pl.pallas_call(
        body,
        out_shape=[jax.ShapeDtypeStruct((sides * steps * keep, block), halves)] * count,
        grid_spec=pltpu.PrefetchScalarGridSpec(
            num_scalar_prefetch=1,
            grid=(sides, steps),
            in_specs=[
                pl.BlockSpec((1, tokens, tile), lambda side, i, order_ref: (side, 0, i)),
                *(column(j) for j in range(count)),
            ],
            out_specs=[
                pl.BlockSpec((keep, block), lambda side, i, order_ref: (side * steps + i, 0))
            ]
            * count,
        ),
        compiler_params=params(),
        cost_estimate=HEAVY,
    )(order, lhs, *([rhs] * count))


def matmul_across(lhs, rhs, first, count):
    tall, inner = lhs.shape
    tile = 256 if count % 256 == 0 and first % 256 == 0 else 128

    def body(lhs_ref, rhs_ref, out_ref):
        out_ref[...] = lax.dot_general(
            lhs_ref[...], rhs_ref[...], contract_last, preferred_element_type=floats
        )

    return pl.pallas_call(
        body,
        out_shape=jax.ShapeDtypeStruct((tall, count), floats),
        grid=(count // tile,),
        in_specs=[
            pl.BlockSpec((tall, inner), lambda j: (0, 0)),
            pl.BlockSpec((tile, inner), lambda j: (first // tile + j, 0)),
        ],
        out_specs=pl.BlockSpec((tall, tile), lambda j: (0, j)),
        compiler_params=params(),
        cost_estimate=HEAVY,
    )(lhs, rhs)


def halves_spec(parts, inner, tall, tile):
    half, part = tall // inner, tall // parts

    def put(places_ref, product, own_ref, other_ref):
        for a in range(parts):
            rows = product[a * part : (a + 1) * part]
            place = places_ref[a]

            @pl.when(place < parts // inner)
            def _():
                own_ref[pl.ds(pl.multiple_of(place * part, part), part)] = rows

            if inner > 1:

                @pl.when(place >= parts // inner)
                def _():
                    at = pl.multiple_of(place * part - half, part)
                    other_ref[pl.ds(at, part)] = rows.astype(halves)

    return half, pl.BlockSpec((half, tile), lambda j, p: (0, j)), put


def matmul_halves(lhs, rhs, places, inner, first=0, scaled=None):
    tall, depth = lhs.shape
    wide = rhs.shape[1]
    tile = 256 if wide % 256 == 0 else 128
    half, spec, put = halves_spec(places.shape[0], inner, tall, tile)

    def body(places_ref, lhs_ref, rhs_ref, *refs):
        product = jnp.dot(lhs_ref[...], rhs_ref[...], preferred_element_type=floats)
        put(places_ref, product, *refs[len(scaled or ()) :][:2])
        if scaled:
            array_ref, factor_ref, sums_ref = refs[0], refs[1], refs[-1]
            terms = product * array_ref[...].astype(floats) * factor_ref[:, :1]
            sums_ref[...] = jnp.sum(terms.reshape(tall // 8, 8, tile), axis=0)

    more_in, more_out, more_shapes = [], [], []
    if scaled:
        more_in = [
            pl.BlockSpec((tall, tile), lambda j, p: (0, j)),
            pl.BlockSpec(scaled[1].shape, lambda j, p: (0, 0)),
        ]
        more_out = [pl.BlockSpec((8, tile), lambda j, p: (0, j))]
        more_shapes = [jax.ShapeDtypeStruct((8, wide), floats)]
    return pl.pallas_call(
        body,
        out_shape=(
            jax.ShapeDtypeStruct((half, wide), floats),
            jax.ShapeDtypeStruct((half, wide), halves),
            *more_shapes,
        ),
        grid_spec=pltpu.PrefetchScalarGridSpec(
            num_scalar_prefetch=1,
            grid=(wide // tile,),
            in_specs=[
                pl.BlockSpec((tall, depth), lambda j, p: (0, 0)),
                pl.BlockSpec((depth, tile), lambda j, p: (first // depth, j)),
                *more_in,
            ],
            out_specs=(spec, spec, *more_out),
        ),
        compiler_params=params(),
        cost_estimate=HEAVY,
    )(places, lhs, rhs, *(scaled or ()))


def gated_forward(normed, weights):
    tokens, inner = normed.shape
    hidden = weights.shape[1] // 2
    tile = 256 if hidden % 256 == 0 else 128
    steps = hidden // tile

    def body(in_ref, gate_ref, up_ref, gate_out, up_out, hidden_out):
        gate = jnp.dot(in_ref[...], gate_ref[...], preferred_element_type=floats)
        up = jnp.dot(in_ref[...], up_ref[...], preferred_element_type=floats)
        gate_out[...] = gate
        up_out[...] = up
        hidden_out[...] = (gelu(gate) * up).astype(halves)

    column = pl.BlockSpec((tokens, tile), lambda j: (0, j))
    return pl.pallas_call(
        body,
        out_shape=(
            jax.ShapeDtypeStruct((tokens, hidden), floats),
            jax.ShapeDtypeStruct((tokens, hidden), floats),
            jax.ShapeDtypeStruct((tokens, hidden), halves),
        ),
        grid=(steps,),
        in_specs=[
            pl.BlockSpec((tokens, inner), lambda j: (0, 0)),
            pl.BlockSpec((inner, tile), lambda j: (0, j)),
            pl.BlockSpec((inner, tile), lambda j: (0, steps + j)),
        ],
        out_specs=(column, column, column),
        compiler_params=params(),
        cost_estimate=HEAVY,
    )(normed, weights, weights)


def gated_backward(cotangent, down, gate, up):
    tokens, inner = cotangent.shape
    hidden = down.shape[0]
    tile = 256 if hidden % 256 == 0 else 128

    def body(cot_ref, down_ref, gate_ref, up_ref, out_ref):
        back = lax.dot_general(
            cot_ref[...], down_ref[...], contract_last, preferred_element_type=floats
        )
        active, slope = gelu_parts(gate_ref[...])
        out_ref[0] = (back * up_ref[...] * slope).astype(halves)
        out_ref[1] = (back * active).astype(halves)

    column = pl.BlockSpec((tokens, tile), lambda j: (0, j))
    return pl.pallas_call(
        body,
        out_shape=jax.ShapeDtypeStruct((2, tokens, hidden), halves),
        grid=(hidden // tile,),
        in_specs=[
            pl.BlockSpec((tokens, inner), lambda j: (0, 0)),
            pl.BlockSpec((tile, inner), lambda j: (j, 0)),
            column,
            column,
        ],
        out_specs=pl.BlockSpec((2, tokens, tile), lambda j: (0, 0, j)),
        compiler_params=params(),
        cost_estimate=HEAVY,
    )(cotangent, down, gate, up)


def pair_halves(pair, weights, places, inner):
    _, tall, hidden = pair.shape
    wide = weights.shape[0]
    tile = 256 if wide % 256 == 0 else 128
    half, spec, put = halves_spec(places.shape[0], inner, tall, tile)

    def body(places_ref, pair_ref, gate_ref, up_ref, own_ref, other_ref):
        product = 0.0
        for side, ref in enumerate((gate_ref, up_ref)):
            product = product + lax.dot_general(
                pair_ref[side], ref[...], contract_last, preferred_element_type=floats
            )
        put(places_ref, product, own_ref, other_ref)

    weight = lambda side: pl.BlockSpec((tile, hidden), lambda j, p: (j, side))
    return pl.pallas_call(
        body,
        out_shape=(
            jax.ShapeDtypeStruct((half, wide), floats),
            jax.ShapeDtypeStruct((half, wide), halves),
        ),
        grid_spec=pltpu.PrefetchScalarGridSpec(
            num_scalar_prefetch=1,
            grid=(wide // tile,),
            in_specs=[pl.BlockSpec((2, tall, hidden), lambda j, p: (0, 0, 0)), weight(0), weight(1)],
            out_specs=(spec, spec),
        ),
        compiler_params=params(),
        cost_estimate=HEAVY,
    )(places, pair, weights, weights)


def segment_of(places, ends_ref):
    segment = jnp.zeros(places.shape, jnp.int32)
    for j in range(ends_ref.shape[0] - 1):
        segment = segment + (places >= ends_ref[j]).astype(jnp.int32)
    return segment


def same_behind(places, ends_ref, offset):
    agree = segment_of(places, ends_ref) == segment_of(places - offset, ends_ref)
    return jnp.logical_and(agree, places >= offset).astype(floats)


def same_ahead(places, ends_ref, offset, seq_len):
    agree = segment_of(places, ends_ref) == segment_of(places + offset, ends_ref)
    return jnp.logical_and(agree, places + offset < seq_len).astype(floats)


def lane_chunks(width):
    step = 256 if width % 256 == 0 else 128
    return [slice(at, at + step) for at in range(0, width, step)]


def gate_values(pre_a, pre_i, decay8):
    rate = jax.nn.sigmoid(pre_a)
    admit = jax.nn.sigmoid(pre_i)
    power = decay8 * rate
    alpha = jnp.exp(-power)
    twice = 2.0 * power
    series = 1.0 - twice * (1.0 / 7.0)
    for order in (6.0, 5.0, 4.0, 3.0, 2.0):
        series = 1.0 - (twice * (1.0 / order)) * series
    raw = jnp.where(twice < 0.5, twice * series, 1.0 - alpha * alpha)
    one_minus = jnp.maximum(raw, floor_value)
    inverse = lax.rsqrt(one_minus)
    return rate, admit, alpha, raw, one_minus * inverse, inverse


def gelu_parts(value):
    square = value * value
    bend = jnp.tanh(gelu_root * (value + gelu_cube * (square * value)))
    half = 0.5 * (1.0 + bend)
    slope = half + 0.5 * value * (1.0 - bend * bend) * (
        gelu_root * (1.0 + 3.0 * gelu_cube * square)
    )
    return value * half, slope


def gelu(value):
    return gelu_parts(value)[0]


def recur_forward(branches, doc_ends, vectors, gates, tiles):
    seq_len, lanes = branches.shape[0], branches.shape[1] // 2
    part = seq_len // tiles
    chunks = lane_chunks(lanes)

    def body(
        ends_ref, x_ref, y_ref, vec_ref, gate_ref,
        mixed_ref, conv_ref, pre_ref, prev_ref, xs, carry,
    ):
        tile = pl.program_id(0)

        @pl.when(tile == 0)
        def _():
            xs[0:8] = jnp.zeros((8, lanes), floats)
            carry[...] = jnp.zeros_like(carry)

        xs[8 : 8 + part] = x_ref[...]
        rows = lax.broadcasted_iota(jnp.int32, (CHUNK, 1), 0)

        def convolve(c, _):
            at = pl.multiple_of(c * CHUNK, CHUNK)
            here = tile * part + at + rows
            same = [same_behind(here, ends_ref, k) for k in range(1, 4)]
            for lane in chunks:
                window = xs[pl.ds(at, CHUNK + 8), lane]
                total = vec_ref[4:5, lane] + vec_ref[0:1, lane] * window[8:]
                for k in range(1, 4):
                    moved = pltpu.roll(window, k, 0)[8:]
                    total = total + vec_ref[k : k + 1, lane] * moved * same[k - 1]
                conv_ref[pl.ds(at, CHUNK), lane] = total.astype(halves)
            return 0

        lax.fori_loop(0, part // CHUNK, convolve, 0)
        xs[0:8] = xs[part : part + 8]
        pre_ref[...] = jnp.dot(conv_ref[...], gate_ref[...], preferred_element_type=floats)

        def advance(c, entering):
            at = pl.multiple_of(c * CHUNK, CHUNK)
            here = tile * part + at + rows
            fresh = 1.0 - same_behind(here, ends_ref, 1)
            leaving = []
            for state, lane in zip(entering, chunks):
                span = lane.stop - lane.start
                shift_lane = slice(lane.start + lanes, lane.stop + lanes)
                pre_a = pre_ref[pl.ds(at, CHUNK), lane] + vec_ref[6:7, lane]
                pre_i = pre_ref[pl.ds(at, CHUNK), shift_lane] + vec_ref[7:8, lane]
                pre_ref[pl.ds(at, CHUNK), lane] = pre_a
                pre_ref[pl.ds(at, CHUNK), shift_lane] = pre_i
                conv_in = conv_ref[pl.ds(at, CHUNK), lane].astype(floats)
                _, admit, alpha, _, root, _ = gate_values(pre_a, pre_i, vec_ref[5:6, lane])
                keep = 1.0 - fresh
                coef = alpha * keep
                drive = (fresh + root * keep) * admit * conv_in
                index = lax.broadcasted_iota(jnp.int32, (CHUNK, span), 0)
                for d in (1, 2, 4):
                    inside = (index & 7) >= d
                    drive = jnp.where(inside, drive + coef * pltpu.roll(drive, d, 0), drive)
                    coef = jnp.where(inside, coef * pltpu.roll(coef, d, 0), coef)
                groups = []
                first = state
                for g in range(CHUNK // 8):
                    group = slice(g * 8, g * 8 + 8)
                    groups.append(coef[group] * state + drive[group])
                    state = groups[-1][7:8]
                states = jnp.concatenate(groups, axis=0)
                prev_ref[pl.ds(at, CHUNK), lane] = jnp.where(
                    index == 0, first, pltpu.roll(states, 1, 0)
                )
                mixed = states * gelu(y_ref[pl.ds(at, CHUNK), lane])
                mixed_ref[pl.ds(at, CHUNK), lane] = mixed.astype(halves)
                leaving.append(state)
            return tuple(leaving)

        ended = lax.fori_loop(
            0, part // CHUNK, advance, tuple(carry[0:1, lane] for lane in chunks)
        )
        for state, lane in zip(ended, chunks):
            carry[0:1, lane] = state

    own = lambda column: pl.BlockSpec((part, lanes), lambda i, e: (i, column))
    straight = lambda width: pl.BlockSpec((part, width), lambda i, e: (i, 0))
    whole = lambda array: pl.BlockSpec(array.shape, lambda i, e: (0, 0))
    return pl.pallas_call(
        body,
        out_shape=(
            jax.ShapeDtypeStruct((seq_len, lanes), halves),
            jax.ShapeDtypeStruct((seq_len, lanes), halves),
            jax.ShapeDtypeStruct((seq_len, 2 * lanes), floats),
            jax.ShapeDtypeStruct((seq_len, lanes), floats),
        ),
        grid_spec=pltpu.PrefetchScalarGridSpec(
            num_scalar_prefetch=1,
            grid=(tiles,),
            in_specs=[own(0), own(1), whole(vectors), whole(gates)],
            out_specs=(own(0), straight(lanes), straight(2 * lanes), straight(lanes)),
            scratch_shapes=[pltpu.VMEM((part + 8, lanes), floats), pltpu.VMEM((8, lanes), floats)],
        ),
        compiler_params=params(),
        cost_estimate=HEAVY,
    )(doc_ends, branches, branches, vectors, gates)


def recur_backward(back_mixed, branches, conv_in, pre, previous, doc_ends, vectors, gates, tiles):
    seq_len, lanes = conv_in.shape
    part = seq_len // tiles
    chunks = lane_chunks(lanes)
    steps = part // CHUNK

    def body(
        ends_ref, bm_ref, x_ref, y_ref, conv_ref, pre_ref, prev_ref, vec_ref, gate_ref,
        bxy_ref, bai_ref, sums_ref, ahead, sums, carry,
    ):
        tile = tiles - 1 - pl.program_id(0)

        @pl.when(pl.program_id(0) == 0)
        def _():
            ahead[part : part + 8] = jnp.zeros((8, lanes), floats)
            sums[...] = jnp.zeros_like(sums)
            carry[...] = jnp.zeros_like(carry)

        rows = lax.broadcasted_iota(jnp.int32, (CHUNK, 1), 0)

        def add_rows(which, lane, value):
            for g in range(CHUNK // 8):
                sums[which * 8 : which * 8 + 8, lane] += value[g * 8 : g * 8 + 8]

        def retreat(c, entering):
            at = pl.multiple_of((steps - 1 - c) * CHUNK, CHUNK)
            span_rows = pl.ds(at, CHUNK)
            here = tile * part + at + rows
            keep = same_behind(here, ends_ref, 1)
            fresh = 1.0 - keep
            leaving = []
            for (back_next, coef_next), lane in zip(entering, chunks):
                span = lane.stop - lane.start
                shift_lane = slice(lane.start + lanes, lane.stop + lanes)
                decay8 = vec_ref[5:6, lane]
                rate, admit, alpha, raw, root, inverse = gate_values(
                    pre_ref[span_rows, lane], pre_ref[span_rows, shift_lane], decay8
                )
                conv = conv_ref[span_rows, lane].astype(floats)
                before = prev_ref[span_rows, lane]
                scale_in = fresh + root * keep
                coef = alpha * keep
                driven = scale_in * admit
                states = coef * before + driven * conv
                active, slope = gelu_parts(y_ref[span_rows, lane])
                back_mix = bm_ref[span_rows, lane]
                bxy_ref[span_rows, shift_lane] = (back_mix * states * slope).astype(halves)
                index = lax.broadcasted_iota(jnp.int32, (CHUNK, span), 0)
                back = back_mix * active
                chain = jnp.where(index == CHUNK - 1, coef_next, pltpu.roll(coef, CHUNK - 1, 0))
                for d in (1, 2, 4):
                    inside = (index & 7) < 8 - d
                    back = jnp.where(inside, back + chain * pltpu.roll(back, CHUNK - d, 0), back)
                    chain = jnp.where(inside, chain * pltpu.roll(chain, CHUNK - d, 0), chain)
                groups = []
                for g in reversed(range(CHUNK // 8)):
                    group = slice(g * 8, g * 8 + 8)
                    groups.insert(0, back[group] + chain[group] * back_next)
                    back_next = groups[0][0:1]
                back_state = jnp.concatenate(groups, axis=0)
                through = back_state * conv
                bound = jnp.where(raw > floor_value, through * admit * alpha * inverse, 0.0)
                back_alpha = (back_state * before - bound) * keep * alpha
                add_rows(5, lane, back_alpha * rate)
                back_a = (back_alpha * (-decay8) * rate * (1.0 - rate)).astype(halves)
                back_i = (through * scale_in * admit * (1.0 - admit)).astype(halves)
                add_rows(6, lane, back_a.astype(floats))
                add_rows(7, lane, back_i.astype(floats))
                bai_ref[span_rows, lane] = back_a
                bai_ref[span_rows, shift_lane] = back_i
                ahead[span_rows, lane] = back_state * driven
                leaving.append((back_next, coef[0:1]))
            return tuple(leaving)

        ended = lax.fori_loop(
            0, steps, retreat, tuple((carry[0:1, lane], carry[8:9, lane]) for lane in chunks)
        )
        for (back_next, coef_next), lane in zip(ended, chunks):
            carry[0:1, lane] = back_next
            carry[8:9, lane] = coef_next

        ahead[0:part] += lax.dot_general(
            bai_ref[...], gate_ref[...], contract_last, preferred_element_type=floats
        )

        def convolve(c, _):
            at = pl.multiple_of(c * CHUNK, CHUNK)
            here = tile * part + at + rows
            same = [same_ahead(here, ends_ref, k, seq_len) for k in range(1, 4)]
            for lane in chunks:
                window = ahead[pl.ds(at, CHUNK + 8), lane]
                x_part = x_ref[pl.ds(at, CHUNK), lane]
                direct = window[:CHUNK]
                back_x = vec_ref[0:1, lane] * direct
                add_rows(0, lane, x_part * direct)
                add_rows(4, lane, direct)
                for k in range(1, 4):
                    moved = pltpu.roll(window, CHUNK + 8 - k, 0)[:CHUNK] * same[k - 1]
                    back_x = back_x + vec_ref[k : k + 1, lane] * moved
                    add_rows(k, lane, x_part * moved)
                bxy_ref[pl.ds(at, CHUNK), lane] = back_x.astype(halves)
            return 0

        lax.fori_loop(0, steps, convolve, 0)
        ahead[part : part + 8] = ahead[0:8]

        @pl.when(pl.program_id(0) == tiles - 1)
        def _():
            for which in range(8):
                sums_ref[which : which + 1] = jnp.sum(
                    sums[which * 8 : which * 8 + 8], axis=0, keepdims=True
                )

    own = lambda width, column: pl.BlockSpec((part, width), lambda i, e: (tiles - 1 - i, column))
    straight = lambda width: pl.BlockSpec((part, width), lambda i, e: (tiles - 1 - i, 0))
    whole = lambda array: pl.BlockSpec(array.shape, lambda i, e: (0, 0))
    return pl.pallas_call(
        body,
        out_shape=(
            jax.ShapeDtypeStruct((seq_len, 2 * lanes), halves),
            jax.ShapeDtypeStruct((seq_len, 2 * lanes), halves),
            jax.ShapeDtypeStruct((8, lanes), floats),
        ),
        grid_spec=pltpu.PrefetchScalarGridSpec(
            num_scalar_prefetch=1,
            grid=(tiles,),
            in_specs=[
                own(lanes, 0), own(lanes, 0), own(lanes, 1),
                straight(lanes), straight(2 * lanes), straight(lanes),
                whole(vectors), whole(gates),
            ],
            out_specs=(
                own(2 * lanes, 0), straight(2 * lanes), pl.BlockSpec((8, lanes), lambda i, e: (0, 0)),
            ),
            scratch_shapes=[
                pltpu.VMEM((part + 8, lanes), floats),
                pltpu.VMEM((64, lanes), floats),
                pltpu.VMEM((16, lanes), floats),
            ],
        ),
        compiler_params=params(),
        cost_estimate=HEAVY,
    )(doc_ends, back_mixed, branches, branches, conv_in, pre, previous, vectors, gates)


def rms_norm(inputs, scales):
    return inputs * lax.rsqrt(jnp.mean(inputs * inputs, axis=-1, keepdims=True) + epsilon) * scales


def inner_of(count):
    return max(d for d in range(1, count + 1) if count % d == 0 and d * d <= count)


def on_device(
    tokens,
    doc_lengths,
    gain_mix,
    value_weight,
    branch_weight,
    conv_weight,
    conv_bias,
    recur_gate,
    input_gate,
    recur_bias,
    input_bias,
    decay_param,
    out_weight,
    gain_ffn,
    gate_weight,
    up_weight,
    down_weight,
    cotangent,
):
    seq_len, _, width = tokens.shape
    heads, head_width = recur_gate.shape[:2]
    channels = value_weight.shape[1]
    hidden_width = gate_weight.shape[1]
    lanes = round_up(channels, 128)
    sent = round_up(channels, 16)
    dp = Ring(DP, inner_of(lax.axis_size(DP)))
    parts = lax.axis_size(CHAN)
    part = seq_len // parts
    block = width // dp.count
    order = dp.order()
    chan = lax.axis_index(CHAN)
    own_tile = chan.reshape(1).astype(jnp.int32)
    cores = 2 if parts % 2 == 0 else 1
    chips = parts // cores
    tiles = jnp.arange(parts, dtype=jnp.int32)
    row_places = ((tiles - chan) % cores) * chips + (tiles // cores - chan // cores) % chips
    doc_ends = jnp.cumsum(doc_lengths[0])
    plan = Plan()
    compute = plan.compute

    def gather_weight(own, count, flip, bias, after, put):
        blocks = ring_gather(plan, dp, own, count, flip, bias, after)
        full = None
        for distance in sorted(blocks, key=lambda d: min(d, dp.count - d)):

            def extend(v, before=full, piece=blocks[distance], slot=dp.slots[distance]):
                return put(
                    None if before is None else v[before], v[piece], order[slot : slot + 1]
                )

            needs = [blocks[distance]] if full is None else [full, blocks[distance]]
            full = compute(3.5, needs, extend)
        return full, blocks

    def put_mix(full, piece, at):
        return place(
            full, piece, at, (3 * lanes, width), 3,
            (sent, block), lambda i, at: (i, 0),
            (lanes, block), lambda i, at: (i, at[0]),
        )

    def put_rows(full, piece, at):
        return place(
            full, piece, at, (width, 2 * hidden_width), 2,
            (block, hidden_width), lambda i, at: (0, i),
            (block, hidden_width), lambda i, at: (at[0], i),
        )

    def put_columns(full, piece, at):
        tall = hidden_width // 2
        return place(
            full, piece, at, (hidden_width, width), 2,
            (tall, block), lambda i, at: (i, 0),
            (tall, block), lambda i, at: (i, at[0]),
        )

    def mix_of(value, branch, out):
        return jnp.concatenate(
            [pad_dim(array, 0, sent) for array in (value.T, branch.T, out)], axis=0
        )

    mix = compute(3.0, [], lambda v: mix_of(value_weight, branch_weight, out_weight), 8.0)
    both_own = compute(2.0, [], lambda v: jnp.concatenate([gate_weight, up_weight], axis=1), 1.0)
    mix_full, mix_blocks = gather_weight(mix, 3 * sent * block, False, 9.0, {}, put_mix)
    far = dp.count // 2
    both_full, both_blocks = gather_weight(
        both_own, 2 * hidden_width * block, True, 8.0,
        {(AHEAD, 0): mix_blocks[far], (BACK, 0): mix_blocks[far + 1]}, put_rows,
    )
    down_own = compute(0.5, [], lambda v: down_weight)
    down_full, down_blocks = gather_weight(
        down_own, hidden_width * block, False, 7.0,
        {(AHEAD, 0): both_blocks[far - 1], (BACK, 0): both_blocks[far]}, put_columns,
    )

    def spread(gate):
        total = 0.0
        for h in range(heads):
            low = h * head_width
            total = total + jnp.pad(gate[h], ((low, lanes - low - head_width),) * 2)
        return total

    def small_parameters(v):
        gates = jnp.concatenate([spread(recur_gate), spread(input_gate)], axis=1)
        vectors = [
            conv_weight,
            conv_bias[None],
            decay_scale * jax.nn.softplus(decay_param)[None],
            recur_bias[None],
            input_bias[None],
        ]
        return gates, pad_dim(jnp.concatenate(vectors, axis=0), 1, lanes)

    small = compute(8.0, [], small_parameters)

    def cross(value, step):
        pairs = [
            (x * cores + c, ((x + step) % chips) * cores + c)
            for x in range(chips)
            for c in range(cores)
        ]
        return lax.ppermute(value, CHAN, pairs)

    def swap(value):
        pairs = [(x * cores + c, x * cores + (c + 1) % cores) for x in range(chips) for c in range(cores)]
        return lax.ppermute(value, CHAN, pairs)

    def gather_rows(own):
        return plan.add(
            CHIPS, 33.0, [own], lambda v: lax.all_gather(v[own], CHAN, axis=0, tiled=True)
        )

    def reduce_rows(product, after=()):
        terms = []
        if cores > 1:
            terms = [plan.add(TWIN, 9.0, [product, *after], lambda v: swap(v[product][1]), 3.0)]
        passing = []
        for s in reversed(range(chips)):

            def add(v, s=s, passing=tuple(passing)):
                pieces = [(v[product][0], s * part), *((v[term], s * part) for term in terms)]
                pieces += [(v[term], 0) for term in passing]
                return add_up(pieces, halves if s else floats, part)

            made = compute(3.0, [product, *terms, *passing], add, 10.0)
            if s:
                passing = [
                    plan.add(CROSS, 26.5, [made], lambda v, made=made: cross(v[made], 1), 3.0)
                ]
        return made

    def small_total(source, axes):
        for axis in axes:
            count = lax.axis_size(axis)
            assert count & (count - 1) == 0
            bit = 1
            while bit < count:
                pairs = [(i, i ^ bit) for i in range(count)]

                def send(v, source=source, axis=axis, pairs=pairs):
                    return lax.ppermute(v[source], axis, pairs)

                other = plan.add(SMALL, 18.0 if axis == DP else 8.0, [source], send)

                def add(v, source=source, other=other):
                    return v[source] + v[other]

                source = compute(0.5, [source, other], add)
                bit *= 2
        return source

    norm_in = compute(
        5.0, [], lambda v: first_norm(tokens.reshape(seq_len, width), gain_mix, parts, own_tile)
    )
    cot = compute(1.5, [], lambda v: cotangent.reshape(part, width))
    cot_full = gather_rows(cot)
    branches = compute(
        10.8,
        [norm_in, mix_full],
        lambda v: matmul_across(v[norm_in][0], v[mix_full], 0, 2 * lanes),
    )
    recur = compute(
        20.2,
        [branches, small],
        lambda v: recur_forward(v[branches], doc_ends, v[small][1], v[small][0], parts),
    )
    mixed = compute(0.0, [recur], lambda v: v[recur][0], 30.0)
    mixed_out = compute(
        9.2,
        [mixed, mix_full],
        lambda v: matmul_halves(v[mixed], v[mix_full], row_places, cores, 2 * lanes),
    )
    branch_out = reduce_rows(mixed_out)

    def middle_of(v):
        residual = v[norm_in][1].astype(floats) + v[branch_out]
        return residual, rms_norm(residual, gain_ffn).astype(halves)

    middle = compute(3.0, [norm_in, branch_out], middle_of)
    mid = compute(0.0, [middle], lambda v: v[middle][1], 30.0)
    mid_full = gather_rows(mid)

    gated = compute(
        19.7,
        [mid_full, both_full],
        lambda v: gated_forward(v[mid_full], v[both_full]),
    )
    hidden = compute(0.0, [gated], lambda v: v[gated][2], 30.0)

    def gradient(lhs, lhs_of, rhs, rhs_of, cost, bias, tile=None, keep=None):
        return [
            compute(
                cost,
                [lhs, rhs],
                lambda v, h=h: gradient_blocks(lhs_of(v), rhs_of(v), order, h, tile, keep),
                bias - 3 * h,
            )
            for h in range(2)
        ]

    grad_down = ring_reduce(
        plan,
        dp,
        gradient(
            hidden, lambda v: v[hidden][None], cot_full, lambda v: v[cot_full], 7.0, 6.0
        ),
        hidden_width * block,
        lambda total: total,
        after=[down_blocks[far]],
    )
    back_both = compute(
        14.7,
        [gated, cot_full, down_full],
        lambda v: gated_backward(v[cot_full], v[down_full], *v[gated][:2]),
    )
    back_product = compute(
        20.5,
        [back_both, both_full],
        lambda v: pair_halves(v[back_both], v[both_full], row_places, cores),
    )
    back_mid = reduce_rows(back_product)
    grad_both = ring_reduce(
        plan,
        dp,
        gradient(back_both, lambda v: v[back_both], mid_full, lambda v: v[mid_full], 11.0, 0.0),
        2 * hidden_width * block,
        lambda total: (total[:hidden_width].T, total[hidden_width:].T),
        True,
    )
    ffn_product = compute(
        12.0,
        [hidden, down_full],
        lambda v: matmul_halves(v[hidden], v[down_full], row_places, cores),
        -2.0,
    )

    def norm_back(inputs, gain, back):
        scale = lax.rsqrt(jnp.mean(inputs * inputs, axis=-1, keepdims=True) + epsilon)
        scaled = back * gain
        mean = jnp.mean(scaled * inputs, axis=-1, keepdims=True)
        through = scale * scaled - inputs * (scale * scale * scale * mean)
        return through

    def back_middle_of(v):
        residual, back = v[middle][0], v[back_mid]
        scale = lax.rsqrt(jnp.mean(residual * residual, axis=-1, keepdims=True) + epsilon)
        gain = jnp.sum((back * residual * scale).reshape(part // 8, 8, width), axis=0)
        back = v[cot].astype(floats) + norm_back(residual, gain_ffn, back)
        return back, back.astype(halves), gain

    back_middle = compute(4.0, [middle, back_mid, cot], back_middle_of)
    back_resid = compute(0.0, [back_middle], lambda v: v[back_middle][1], 30.0)
    branch_full = gather_rows(back_resid)
    ffn_out = reduce_rows(ffn_product, [branch_full])
    output = compute(
        4.0, [middle, ffn_out], lambda v: (v[middle][0] + v[ffn_out]).astype(halves), -1.0
    )
    back_mixed = compute(
        6.7,
        [branch_full, mix_full],
        lambda v: matmul_across(v[branch_full], v[mix_full], 2 * lanes, lanes),
    )
    recur_back = compute(
        26.5,
        [back_mixed, branches, recur, small],
        lambda v: recur_backward(
            v[back_mixed], v[branches], *v[recur][1:], doc_ends, v[small][1], v[small][0], parts
        ),
    )
    grad_out = ring_reduce(
        plan,
        dp,
        gradient(
            mixed, lambda v: v[mixed][None], branch_full, lambda v: v[branch_full],
            3.5, 2.0, lanes, sent,
        ),
        sent * block,
        lambda total: total[:channels],
        True,
    )
    grad_pair = ring_reduce(
        plan,
        dp,
        gradient(
            recur_back, lambda v: v[recur_back][0][None], norm_in, lambda v: v[norm_in][0],
            5.5, 4.0, lanes, sent,
        ),
        2 * sent * block,
        lambda total: (total[:channels].T, total[sent : sent + channels].T),
    )
    back_pair = compute(
        13.0,
        [recur_back, mix_full, norm_in],
        lambda v: matmul_halves(
            v[recur_back][0], v[mix_full], row_places, cores, 0,
            (tokens.reshape(seq_len, width), v[norm_in][2]),
        ),
        2.0,
    )
    back_norm_in = reduce_rows(back_pair)

    def back_first_of(v):
        through = norm_back(v[norm_in][1].astype(floats), gain_mix, v[back_norm_in])
        return v[back_middle][0] + through

    back_first = compute(5.0, [norm_in, back_norm_in, back_middle], back_first_of)

    def gate_grads_of(v):
        whole = lax.dot_general(
            v[recur][1], v[recur_back][1], contract_first, preferred_element_type=floats
        )
        return jnp.stack(
            [
                whole[
                    h * head_width : (h + 1) * head_width,
                    side * lanes + h * head_width : side * lanes + (h + 1) * head_width,
                ]
                for side in range(2)
                for h in range(heads)
            ]
        )

    gate_terms = compute(
        5.0, [recur, recur_back], lambda v: gate_grads_of(v).astype(halves), 3.5
    )
    gate_sums = plan.add(CHIPS, 60.0, [gate_terms], lambda v: lax.psum(v[gate_terms], DP), 3.0)
    gate_result = compute(
        4.0, [gate_sums], lambda v: tuple(jnp.split(v[gate_sums].astype(floats), 2))
    )
    def both_gains(v):
        gains = [jnp.sum(terms, axis=0).reshape(8, -1) for terms in (v[back_middle][2], v[back_pair][2])]
        return jnp.concatenate(gains, axis=1)

    gain_rows = small_total(compute(2.0, [back_middle, back_pair], both_gains, 1.0), [CHAN])
    sums = small_total(
        compute(
            1.0,
            [recur_back, gain_rows],
            lambda v: jnp.concatenate([v[recur_back][2], v[gain_rows]], axis=1),
        ),
        [DP],
    )

    def sum_results_of(v):
        total = v[sums][:, :channels]
        decay = total[5] * (-decay_scale * jax.nn.sigmoid(decay_param))
        gains = v[sums][:, lanes:]
        return (
            total[:4], total[4], total[6], total[7], decay,
            gains[:, : width // 8].reshape(width), gains[:, width // 8 :].reshape(width),
        )

    sum_results = compute(3.0, [sums], sum_results_of)

    done = plan.execute(
        [
            output, back_first, grad_pair, grad_out, sum_results, gate_result,
            grad_both, grad_down,
        ]
    )
    output, first, (value, branch), out, summed, (recur, admit), (gate, up), down = done
    return (
        output.reshape(part, 1, width),
        first.reshape(part, 1, width),
        summed[6],
        value,
        branch,
        summed[0],
        summed[1],
        recur,
        admit,
        summed[2],
        summed[3],
        summed[4],
        out,
        summed[5],
        gate,
        up,
        down,
    )


def solution(mesh):
    tokens, split, columns = P(None, DP, None), P(DP, CHAN), P(CHAN, DP)
    own, channels, heads = P(CHAN, DP, None), P(CHAN), P(CHAN, None, None)
    in_specs = (
        tokens, P(DP, None), P(), split, split, P(None, CHAN), channels, heads, heads,
        channels, channels, channels, columns, P(), split, split, columns, own,
    )
    out_specs = (
        own, own, P(), split, split, P(None, CHAN), channels, heads, heads,
        channels, channels, channels, columns, P(), split, split, columns,
    )
    return jax.shard_map(
        on_device, mesh=mesh, in_specs=in_specs, out_specs=out_specs, check_vma=False
    )
```

time: 1040 us -> 800 us (0.77)
  Pallas kernels: 58 us -> 370 us
  waiting for transfers between devices: 552 us -> 261 us
  matrix products: 190 us -> 2.96 us
  starting transfers between devices: 95.5 us -> 62.7 us
  local copies, waits for them, and re-layouts: 78.3 us -> 48.4 us
  other arithmetic: 44.7 us -> 28.4 us
    pallas_call x3 -> x68, Pallas kernels: 5.54 us -> 320 us  [the longest x28 80.7 us: add_up(): pl.pallas_call(body, out_shape=jax.ShapeDtypeStruct((rows, width), dtype)...]
    ppermute x83 -> x62, waiting for transfers between devices: 510 us -> 246 us  [the longest x49 211 us: hop(): return lax.ppermute(value, self.axis, pairs)]
    dot_general x41 -> x1, matrix products: 190 us -> 2.96 us  [gate_grads_of(): lax.dot_general(v[recur][1], v[recur_back][1], contract_first, preferred_...]
    psum x1, waiting for transfers between devices: 42.2 us -> 7.96 us  [on_device(): lax.psum(v[gate_terms], DP)]
    ppermute x83 -> x62, starting transfers between devices: 95.5 us -> 62.5 us  [the longest x49 54.4 us: hop(): return lax.ppermute(value, self.axis, pairs)]
    slice x26 -> x3, local copies, waits for them, and re-layouts: 19.4 us -> 1.84 us  [the longest x1 0.63 us: sum_results_of(): decay = total[5] * (-decay_scale * jax.nn.sigmoid(decay_param))]
    concatenate x12 -> x5, other arithmetic: 17.2 us -> 5.1 us  [the longest x1 2.35 us: mix_of(): jnp.concatenate([pad_dim(array, 0, sent) for array in (value.T, branch.T,...]
    unnamed x194 -> x187, local copies, waits for them, and re-layouts: 45.1 us -> 39.9 us
  transfers between devices with their start and end apart: 84 -> 66, of which waited for: 31 -> 28; matrix products, arithmetic and copies ran while one was open for 19% -> 6% of each run, Pallas kernels for 4% -> 44%
where the time goes in v2:
time: 800 us; the launch traced here: 788 us
  Pallas kernels  370 us (46%)
  waiting for transfers between devices  261 us (33%)
  starting transfers between devices  62.7 us (8%)
  local copies, waits for them, and re-layouts  48.4 us (6%)
  other arithmetic  28.4 us (4%)
  between operations  15.1 us (2%)
    ppermute x49, waiting for transfers between devices, hop(): return lax.ppermute(value, self.axis, pairs)  211 us
    pallas_call x28, Pallas kernels, add_up(): pl.pallas_call(body, out_shape=jax.ShapeDtypeStruct((rows, width), dtype)...  80.7 us
    pallas_call x24, Pallas kernels, place(): pl.pallas_call(body, out_shape=jax.ShapeDtypeStruct(shape, piece.dtype),...  76.1 us
    pallas_call x8, Pallas kernels, gradient_blocks(): pl.pallas_call(body, out_shape=[jax.ShapeDtypeStruct((sides * steps * kee...  55.6 us
    ppermute x49, starting transfers between devices, hop(): return lax.ppermute(value, self.axis, pairs)  54.4 us
    unnamed x187, local copies, waits for them, and re-layouts  39.9 us
    pallas_call x3, Pallas kernels, matmul_halves(): pl.pallas_call(body, out_shape=(jax.ShapeDtypeStruct((half, wide), floats...  35.1 us
    ppermute x4, waiting for transfers between devices, cross(): return lax.ppermute(value, CHAN, pairs)  29.9 us
  transfers between devices with their start and end apart: 66, of which 28 were waited for; matrix products, arithmetic and copies ran while one was open for 6% of the time, Pallas kernels for 44%

profile of v2, /device:TPU:0, one launch (start us, length us, event | category | flops | bytes accessed | tf_op | source)
XLA Modules:
  0.0 787.9 jit_solution(4093761140316769944)
XLA Ops:
  45.8 15.3 %collective-permute-done.2.in_ref = bf16[2064,256]{1,0:T(8,128)(2,1)} collective-permute-done((bf16[2064,256]{1,0:T(8,128)(2,1)}, bf16[2064,256]{1,0:T(8,128)(2,1)}, u32[]{:S(2)}, u32[]{:S(2)}) %collective-permute-start.2) | collective-permute-done | bytes 1056800 | tf_op jit(solution)/shard_map/ppermute | solution.py:61
  70.7 14.4 %collective-permute-done.4.in_ref = bf16[2064,256]{1,0:T(8,128)(2,1)} collective-permute-done((bf16[2064,256]{1,0:T(8,128)(2,1)}, bf16[2064,256]{1,0:T(8,128)(2,1)}, u32[]{:S(2)}, u32[]{:S(2)}) %collective-permute-start.4) | collective-permute-done | bytes 1056800 | tf_op jit(solution)/shard_map/ppermute | solution.py:61
  94.5 13.5 %collective-permute-done.6.in_ref = bf16[2064,256]{1,0:T(8,128)(2,1)} collective-permute-done((bf16[2064,256]{1,0:T(8,128)(2,1)}, bf16[2064,256]{1,0:T(8,128)(2,1)}, u32[]{:S(2)}, u32[]{:S(2)}) %collective-permute-start.6) | collective-permute-done | bytes 1056800 | tf_op jit(solution)/shard_map/ppermute | solution.py:61
  112.8 10.8 %shard_map.316.x_ref.y_ref = f32[1024,1536]{1,0:T(8,128)} custom-call(bf16[1024,2048]{1,0:T(8,128)(2,1)S(1)} %copy-done.32, bf16[2304,2048]{1,0:T(8,128)(2,1)} %shard_map.315.rhs_ref), custom_call_target="tpu_custom_call" | custom-call | flops 199999995904 | bytes 1 | tf_op jit(solution)/shard_map/pallas_call | solution.py:418
  124.9 20.1 %shard_map.317 = (bf16[1024,768]{1,0:T(8,128)(2,1)S(1)}, bf16[1024,768]{1,0:T(8,128)(2,1)S(1)}, f32[1024,1536]{1,0:T(8,128)}, f32[1024,768]{1,0:T(8,128)}) custom-call(s32[4]{0:T(128)S(1)} %bitcast.89, f32[1024,1536]{1,0:T(8,128)} %shard_map.316.x_ref.y_ref, f32[1024,1536]{1,0:T(8,128)} %shard_map.316.x_ref.y_ref, f32[8,768]{1,0:T(8,128)S(1)} %pad.53.vec_ref, ...), custom_call_target="tpu_custom_call" | custom-call | flops 199999995904 | bytes 1 | tf_op jit(solution)/shard_map/pallas_call | solution.py:726
  145.0 10.0 %shard_map.318 = (f32[512,2048]{1,0:T(8,128)}, bf16[512,2048]{1,0:T(8,128)(2,1)}) custom-call(s32[4]{0:T(128)S(1)} %fusion.28.places_ref, bf16[1024,768]{1,0:T(8,128)(2,1)S(1)} %get-tuple-element.5554.lhs_ref, bf16[2304,2048]{1,0:T(8,128)(2,1)} %shard_map.315.rhs_ref), custom_call_target="tpu_custom_call" | custom-call | flops 199999995904 | bytes 1 | tf_op jit(solution)/shard_map/pallas_call | solution.py:476
  167.1 20.6 %collective-permute-done.11.in_ref = bf16[256,3072]{1,0:T(8,128)(2,1)} collective-permute-done((bf16[256,3072]{1,0:T(8,128)(2,1)}, bf16[256,3072]{1,0:T(8,128)(2,1)}, u32[]{:S(2)}, u32[]{:S(2)}) %collective-permute-start.11) | collective-permute-done | bytes 1572896 | tf_op jit(solution)/shard_map/ppermute | solution.py:61
  194.2 17.0 %collective-permute-done.12.refs_2_ = bf16[256,2048]{1,0:T(8,128)(2,1)} collective-permute-done((bf16[256,2048]{1,0:T(8,128)(2,1)}, bf16[256,2048]{1,0:T(8,128)(2,1)}, u32[]{:S(2)}, u32[]{:S(2)}) %collective-permute-start.12) | collective-permute-done | bytes 1048608 | tf_op jit(solution)/shard_map/ppermute | solution.py:1021
  219.3 32.4 %collective-permute-done.14.in_ref = bf16[256,3072]{1,0:T(8,128)(2,1)} collective-permute-done((bf16[256,3072]{1,0:T(8,128)(2,1)}, bf16[256,3072]{1,0:T(8,128)(2,1)}, u32[]{:S(2)}, u32[]{:S(2)}) %collective-permute-start.14) | collective-permute-done | bytes 1572896 | tf_op jit(solution)/shard_map/ppermute | solution.py:61
  263.1 19.6 %shard_map.328 = (f32[1024,1536]{1,0:T(8,128)}, f32[1024,1536]{1,0:T(8,128)}, bf16[1024,1536]{1,0:T(8,128)(2,1)S(1)}) custom-call(bf16[1024,2048]{1,0:T(8,128)(2,1)} %all-gather.4.cloned.1.call-done.in_ref.refs_0_.refs_1_.refs_2_.refs_3_, bf16[2048,3072]{1,0:T(8,128)(2,1)} %shard_map.327.gate_ref.up_ref, bf16[2048,3072]{1,0:T(8,128)(2,1)} %shard_map.327.gate_ref.up_ref), custom_call_target="tpu_custom_call" | custom-call | flops 199999995904 | bytes 1 | tf_op jit(solution)/shard_map/pallas_call | solution.py:512
  287.7 6.6 shard_map.329
  294.3 6.4 shard_map.330
  313.1 12.8 %collective-permute-done.20.in_ref = bf16[1536,256]{1,0:T(8,128)(2,1)} collective-permute-done((bf16[1536,256]{1,0:T(8,128)(2,1)}, bf16[1536,256]{1,0:T(8,128)(2,1)}, u32[]{:S(2)}, u32[]{:S(2)}) %collective-permute-start.20) | collective-permute-done | bytes 786464 | tf_op jit(solution)/shard_map/ppermute | solution.py:61
  332.6 12.5 %collective-permute-done.22.in_ref = bf16[1536,256]{1,0:T(8,128)(2,1)} collective-permute-done((bf16[1536,256]{1,0:T(8,128)(2,1)}, bf16[1536,256]{1,0:T(8,128)(2,1)}, u32[]{:S(2)}, u32[]{:S(2)}) %collective-permute-start.22) | collective-permute-done | bytes 786464 | tf_op jit(solution)/shard_map/ppermute | solution.py:61
  348.0 14.8 %shard_map.338.pair_ref.lhs_ref = bf16[2,1024,1536]{2,1,0:T(8,128)(2,1)} custom-call(bf16[1024,2048]{1,0:T(8,128)(2,1)S(1)} %copy-done.10, bf16[1536,2048]{1,0:T(8,128)(2,1)} %shard_map.337.down_ref.rhs_ref, f32[1024,1536]{1,0:T(8,128)} %get-tuple-element.3999.gate_ref, f32[1024,1536]{1,0:T(8,128)} %get-tuple-element.4000.up_ref), custom_call_target="tpu_custom_call" | custom-call | flops 199999995904 | bytes 1 | tf_op jit(solution)/shard_map/pallas_call | solution.py:545
  364.4 20.2 %shard_map.339 = (f32[512,2048]{1,0:T(8,128)}, bf16[512,2048]{1,0:T(8,128)(2,1)}) custom-call(s32[4]{0:T(128)S(1)} %copy-done.23, bf16[2,1024,1536]{2,1,0:T(8,128)(2,1)} %shard_map.338.pair_ref.lhs_ref, bf16[2048,3072]{1,0:T(8,128)(2,1)} %shard_map.327.gate_ref.up_ref, bf16[2048,3072]{1,0:T(8,128)(2,1)} %shard_map.327.gate_ref.up_ref), custom_call_target="tpu_custom_call" | custom-call | flops 199999995904 | bytes 1 | tf_op jit(solution)/shard_map/pallas_call | solution.py:576
  388.4 14.2 %collective-permute-done.24.refs_1_ = bf16[1536,256]{1,0:T(8,128)(2,1)} collective-permute-done((bf16[1536,256]{1,0:T(8,128)(2,1)}, bf16[1536,256]{1,0:T(8,128)(2,1)}, u32[]{:S(2)}, u32[]{:S(2)}) %collective-permute-start.24) | collective-permute-done | bytes 786464 | tf_op jit(solution)/shard_map/ppermute | solution.py:61
  406.0 11.3 %shard_map.342 = (bf16[3072,256]{1,0:T(8,128)(2,1)}, bf16[3072,256]{1,0:T(8,128)(2,1)S(1)}, bf16[3072,256]{1,0:T(8,128)(2,1)}, bf16[3072,256]{1,0:T(8,128)(2,1)}) custom-call(s32[8]{0:T(128)S(1)} %copy-done.7, bf16[2,1024,1536]{2,1,0:T(8,128)(2,1)} %shard_map.338.pair_ref.lhs_ref, ...), custom_call_target="tpu_custom_call" | custom-call | flops 199999995904 | bytes 1 | tf_op jit(solution)/shard_map/pallas_call | solution.py:389
  424.5 12.0 %shard_map.344 = (f32[512,2048]{1,0:T(8,128)}, bf16[512,2048]{1,0:T(8,128)(2,1)S(1)}) custom-call(s32[4]{0:T(128)S(1)} %copy-done.24, bf16[1024,1536]{1,0:T(8,128)(2,1)S(1)} %copy-done.15, bf16[1536,2048]{1,0:T(8,128)(2,1)} %shard_map.337.down_ref.rhs_ref), custom_call_target="tpu_custom_call" | custom-call | flops 199999995904 | bytes 1 | tf_op jit(solution)/shard_map/pallas_call | solution.py:476
  446.0 11.0 %shard_map.347 = (bf16[3072,256]{1,0:T(8,128)(2,1)S(1)}, bf16[3072,256]{1,0:T(8,128)(2,1)S(1)}, bf16[3072,256]{1,0:T(8,128)(2,1)S(1)}, bf16[3072,256]{1,0:T(8,128)(2,1)}) custom-call(s32[8]{0:T(128)S(1)} %copy-done.7, bf16[2,1024,1536]{2,1,0:T(8,128)(2,1)} %shard_map.338.pair_ref.lhs_ref, ...), custom_call_target="tpu_custom_call" | custom-call | flops 199999995904 | bytes 1 | tf_op jit(solution)/shard_map/pallas_call | solution.py:389
  474.9 6.7 collective-permute-done.29.refs_1_
  493.0 5.5 collective-permute-done.31.refs_1_
  514.1 6.7 shard_map.353.bm_ref
  522.5 26.3 %shard_map.354 = (bf16[1024,1536]{1,0:T(8,128)(2,1)}, bf16[1024,1536]{1,0:T(8,128)(2,1)}, f32[8,768]{1,0:T(8,128)S(1)}) custom-call(s32[4]{0:T(128)S(1)} %bitcast.90, f32[1024,768]{1,0:T(8,128)} %copy-done.33, f32[1024,1536]{1,0:T(8,128)} %shard_map.316.x_ref.y_ref, f32[1024,1536]{1,0:T(8,128)} %shard_map.316.x_ref.y_ref, bf16[1024,768]{1,0:T(8,128)(2,1)S(1)} %copy-done.29, ...), custom_call_target="tpu_custom_call" | custom-call | flops 199999995904 | bytes 1 | tf_op jit(solution)/shard_map/pallas_call | solution.py:862
  562.3 5.9 shard_map.358
  578.4 13.1 %shard_map.360 = (f32[512,2048]{1,0:T(8,128)}, bf16[512,2048]{1,0:T(8,128)(2,1)}, f32[8,2048]{1,0:T(8,128)S(1)}) custom-call(s32[4]{0:T(128)S(1)} %copy-done.25, bf16[1024,1536]{1,0:T(8,128)(2,1)S(1)} %copy-done.17, bf16[2304,2048]{1,0:T(8,128)(2,1)} %shard_map.315.rhs_ref, bf16[1024,2048]{1,0:T(8,128)(2,1)} %bitcast.100, f32[1024,128]{1,0:T(8,128)S(1)} %copy-done.54), custom_call_target="tpu_custom_call" | custom-call | flops 199999995904 | bytes 1 | tf_op jit(solution)/shard_map/pallas_call | solution.py:476
  593.6 7.7 collective-permute-done.37.refs_2_
  608.9 5.9 shard_map.362
  617.4 21.7 %collective-permute-done.40.refs_1_ = bf16[3072,256]{1,0:T(8,128)(2,1)} collective-permute-done((bf16[3072,256]{1,0:T(8,128)(2,1)}, bf16[3072,256]{1,0:T(8,128)(2,1)}, u32[]{:S(2)}, u32[]{:S(2)}) %collective-permute-start.40) | collective-permute-done | bytes 1572896 | tf_op jit(solution)/shard_map/ppermute | solution.py:61
  672.7 8.0 %all-reduce.14.cloned.1.call-done = bf16[8,171,171]{2,1,0:T(8,128)(2,1)} async-done(((bf16[8,171,171]{2,1,0:T(8,128)(2,1)}), bf16[8,171,171]{2,1,0:T(8,128)(2,1)}) %all-reduce.14.cloned.1.call-update) | async-done | bytes 467872 | tf_op jit(solution)/shard_map/psum | solution.py:1245
  722.5 8.6 %collective-permute-done.54.refs_1_ = bf16[1376,256]{1,0:T(8,128)(2,1)} collective-permute-done((bf16[1376,256]{1,0:T(8,128)(2,1)}, bf16[1376,256]{1,0:T(8,128)(2,1)}, u32[]{:S(2)}, u32[]{:S(2)}) %collective-permute-start.54) | collective-permute-done | bytes 704544 | tf_op jit(solution)/shard_map/ppermute | solution.py:61
  753.4 14.3 %collective-permute-done.58 = bf16[1376,256]{1,0:T(8,128)(2,1)} collective-permute-done((bf16[1376,256]{1,0:T(8,128)(2,1)}, bf16[1376,256]{1,0:T(8,128)(2,1)}, u32[]{:S(2)}, u32[]{:S(2)}) %collective-permute-start.58) | collective-permute-done | bytes 704544 | tf_op jit(solution)/shard_map/ppermute | solution.py:61
  (418 shorter events, 347.1 us)
Async XLA Ops:
  7.2 255.8 %all-gather.4.cloned.1.call-start = ((), (), s32[]{:S(2)}) async-start(), calls=%async_computation | async-start | bytes 5242880 | tf_op jit(solution)/shard_map/all_gather | solution.py:1029
  86.1 37.5 %collective-permute-start.7 = (bf16[256,3072]{1,0:T(8,128)(2,1)}, bf16[256,3072]{1,0:T(8,128)(2,1)}, u32[]{:S(2)}, u32[]{:S(2)}) collective-permute-start(bf16[256,3072]{1,0:T(8,128)(2,1)} %pad_maximum_fusion.1.in_ref), channel_id=1, source_target_pairs={{0,8},{8,16},{16,24},{24,28},{28,20},{20,12},{12,4},{4,0},{1,9},{9... | collective-permute-start | bytes 4718600 | tf_op jit(solution)/shard_map/ppermute | solution.py:61
  112.1 42.9 %collective-permute-start.8 = (bf16[256,3072]{1,0:T(8,128)(2,1)}, bf16[256,3072]{1,0:T(8,128)(2,1)}, u32[]{:S(2)}, u32[]{:S(2)}) collective-permute-start(bf16[256,3072]{1,0:T(8,128)(2,1)} %pad_maximum_fusion.1.in_ref), channel_id=1, source_target_pairs={{0,4},{8,0},{16,8},{24,16},{28,24},{20,28},{12,20},{4,12},{1,5},{9... | collective-permute-start | bytes 4718600 | tf_op jit(solution)/shard_map/ppermute | solution.py:61
  123.6 38.2 %collective-permute-start.9 = (bf16[256,3072]{1,0:T(8,128)(2,1)}, bf16[256,3072]{1,0:T(8,128)(2,1)}, u32[]{:S(2)}, u32[]{:S(2)}) collective-permute-start(bf16[256,3072]{1,0:T(8,128)(2,1)} %collective-permute-done.7.in_ref), channel_id=1, source_target_pairs={{0,8},{8,16},{16,24},{24,28},{28,20},{20,12},{12,4},{4,0},{1,9},{9... | collective-permute-start | bytes 4718600 | tf_op jit(solution)/shard_map/ppermute | solution.py:61
  155.0 32.7 %collective-permute-start.11 = (bf16[256,3072]{1,0:T(8,128)(2,1)}, bf16[256,3072]{1,0:T(8,128)(2,1)}, u32[]{:S(2)}, u32[]{:S(2)}) collective-permute-start(bf16[256,3072]{1,0:T(8,128)(2,1)} %collective-permute-done.8.in_ref), channel_id=1, source_target_pairs={{0,4},{8,0},{16,8},{24,16},{28,24},{20,28},{12,20},{4,12},{1,5},{9... | collective-permute-start | bytes 4718600 | tf_op jit(solution)/shard_map/ppermute | solution.py:61
  161.8 52.3 %collective-permute-start.13 = (bf16[256,3072]{1,0:T(8,128)(2,1)}, bf16[256,3072]{1,0:T(8,128)(2,1)}, u32[]{:S(2)}, u32[]{:S(2)}) collective-permute-start(bf16[256,3072]{1,0:T(8,128)(2,1)} %collective-permute-done.9.in_ref), channel_id=1, source_target_pairs={{0,8},{8,16},{16,24},{24,28},{28,20},{20,12},{12,4},{4,0},{1,9},{9... | collective-permute-start | bytes 4718600 | tf_op jit(solution)/shard_map/ppermute | solution.py:61
  217.1 70.6 %all-gather.6.cloned.1.call-start = ((), (), s32[]{:S(2)}) async-start(), calls=%async_computation.1 | async-start | bytes 5242880 | tf_op jit(solution)/shard_map/all_gather | solution.py:1029
  217.1 34.6 %collective-permute-start.14 = (bf16[256,3072]{1,0:T(8,128)(2,1)}, bf16[256,3072]{1,0:T(8,128)(2,1)}, u32[]{:S(2)}, u32[]{:S(2)}) collective-permute-start(bf16[256,3072]{1,0:T(8,128)(2,1)} %collective-permute-done.11.in_ref), channel_id=1, source_target_pairs={{0,4},{8,0},{16,8},{24,16},{28,24},{20,28},{12,20},{4,12},{1,5},{9... | collective-permute-start | bytes 4718600 | tf_op jit(solution)/shard_map/ppermute | solution.py:61
  217.8 289.3 %all-gather.8.cloned.1.call-start = ((), (), s32[]{:S(2)}) async-start(), calls=%async_computation.2 | async-start | bytes 5242880 | tf_op jit(solution)/shard_map/all_gather | solution.py:1029
  217.9 40.0 %collective-permute-start.15 = (bf16[256,3072]{1,0:T(8,128)(2,1)}, bf16[256,3072]{1,0:T(8,128)(2,1)}, u32[]{:S(2)}, u32[]{:S(2)}) collective-permute-start(bf16[256,3072]{1,0:T(8,128)(2,1)} %collective-permute-done.13.in_ref), channel_id=1, source_target_pairs={{0,8},{8,16},{16,24},{24,28},{28,20},{20,12},{12,4},{4,0},{1,9},{9... | collective-permute-start | bytes 4718600 | tf_op jit(solution)/shard_map/ppermute | solution.py:61
  251.7 32.6 %collective-permute-start.16 = (bf16[1536,256]{1,0:T(8,128)(2,1)}, bf16[1536,256]{1,0:T(8,128)(2,1)}, u32[]{:S(2)}, u32[]{:S(2)}) collective-permute-start(bf16[1536,256]{1,0:T(8,128)(2,1)} %in_ref), channel_id=1, source_target_pairs={{0,4},{8,0},{16,8},{24,16},{28,24},{20,28},{12,20},{4,12},{1,5},{9... | collective-permute-start | bytes 2359304 | tf_op jit(solution)/shard_map/ppermute | solution.py:61
  257.9 27.2 %collective-permute-start.17 = (bf16[1536,256]{1,0:T(8,128)(2,1)}, bf16[1536,256]{1,0:T(8,128)(2,1)}, u32[]{:S(2)}, u32[]{:S(2)}) collective-permute-start(bf16[1536,256]{1,0:T(8,128)(2,1)} %in_ref), channel_id=1, source_target_pairs={{0,8},{8,16},{16,24},{24,28},{28,20},{20,12},{12,4},{4,0},{1,9},{9... | collective-permute-start | bytes 2359304 | tf_op jit(solution)/shard_map/ppermute | solution.py:61
  385.1 35.5 %collective-permute-start.25 = (bf16[512,2048]{1,0:T(8,128)(2,1)}, bf16[512,2048]{1,0:T(8,128)(2,1)}, u32[]{:S(2)}, u32[]{:S(2)}) collective-permute-start(bf16[512,2048]{1,0:T(8,128)(2,1)} %get-tuple-element.4058), channel_id=1, source_target_pairs={{0,1},{1,0},{2,3},{3,2},{4,5},{5,4},{6,7},{7,6},{8,9},{9,8},{10,11... | collective-permute-start | bytes 6291464 | tf_op jit(solution)/shard_map/ppermute | solution.py:1025
  444.0 37.6 %collective-permute-start.29 = (bf16[3072,256]{1,0:T(8,128)(2,1)}, bf16[3072,256]{1,0:T(8,128)(2,1)}, u32[]{:S(2)}, u32[]{:S(2)}) collective-permute-start(bf16[3072,256]{1,0:T(8,128)(2,1)} %get-tuple-element.4516), channel_id=1, source_target_pairs={{0,8},{8,16},{16,24},{24,28},{28,20},{20,12},{12,4},{4,0},{1,9},{9... | collective-permute-start | bytes 4718600 | tf_op jit(solution)/shard_map/ppermute | solution.py:61
  445.5 41.5 %collective-permute-start.30 = (bf16[3072,256]{1,0:T(8,128)(2,1)}, bf16[3072,256]{1,0:T(8,128)(2,1)}, u32[]{:S(2)}, u32[]{:S(2)}) collective-permute-start(bf16[3072,256]{1,0:T(8,128)(2,1)} %get-tuple-element.4548), channel_id=1, source_target_pairs={{0,4},{8,0},{16,8},{24,16},{28,24},{20,28},{12,20},{4,12},{1,5},{9... | collective-permute-start | bytes 4718600 | tf_op jit(solution)/shard_map/ppermute | solution.py:61
  474.3 206.4 %all-reduce.14.cloned.1.call-start = ((), (), s32[]{:S(2)}) async-start(), calls=%async_computation.3 | async-start | bytes 1441792 | tf_op jit(solution)/shard_map/psum | solution.py:1245
  474.3 74.4 %collective-permute-start.32 = (bf16[1536,256]{1,0:T(8,128)(2,1)}, bf16[1536,256]{1,0:T(8,128)(2,1)}, u32[]{:S(2)}, u32[]{:S(2)}) collective-permute-start(bf16[1536,256]{1,0:T(8,128)(2,1)} %shard_map.346), channel_id=1, source_target_pairs={{0,4},{8,0},{16,8},{24,16},{28,24},{20,28},{12,20},{4,12},{1,5},{9... | collective-permute-start | bytes 2359304 | tf_op jit(solution)/shard_map/ppermute | solution.py:61
  490.8 58.0 %collective-permute-start.33 = (bf16[3072,256]{1,0:T(8,128)(2,1)}, bf16[3072,256]{1,0:T(8,128)(2,1)}, u32[]{:S(2)}, u32[]{:S(2)}) collective-permute-start(bf16[3072,256]{1,0:T(8,128)(2,1)} %shard_map.350), channel_id=1, source_target_pairs={{0,4},{8,0},{16,8},{24,16},{28,24},{20,28},{12,20},{4,12},{1,5},{9... | collective-permute-start | bytes 4718600 | tf_op jit(solution)/shard_map/ppermute | solution.py:61
  491.1 61.5 %collective-permute-start.34 = (bf16[3072,256]{1,0:T(8,128)(2,1)}, bf16[3072,256]{1,0:T(8,128)(2,1)}, u32[]{:S(2)}, u32[]{:S(2)}) collective-permute-start(bf16[3072,256]{1,0:T(8,128)(2,1)} %shard_map.349), channel_id=1, source_target_pairs={{0,8},{8,16},{16,24},{24,28},{28,20},{20,12},{12,4},{4,0},{1,9},{9... | collective-permute-start | bytes 4718600 | tf_op jit(solution)/shard_map/ppermute | solution.py:61
  507.1 51.3 %collective-permute-start.35 = (bf16[512,2048]{1,0:T(8,128)(2,1)}, bf16[512,2048]{1,0:T(8,128)(2,1)}, u32[]{:S(2)}, u32[]{:S(2)}) collective-permute-start(bf16[512,2048]{1,0:T(8,128)(2,1)} %copy-done.11), channel_id=1, source_target_pairs={{0,1},{1,0},{2,3},{3,2},{4,5},{5,4},{6,7},{7,6},{8,9},{9,8},{10,11... | collective-permute-start | bytes 6291464 | tf_op jit(solution)/shard_map/ppermute | solution.py:1025
  554.1 50.9 %collective-permute-start.38 = (bf16[688,256]{1,0:T(8,128)(2,1)}, bf16[688,256]{1,0:T(8,128)(2,1)}, u32[]{:S(2)}, u32[]{:S(2)}) collective-permute-start(bf16[688,256]{1,0:T(8,128)(2,1)} %get-tuple-element.5347), channel_id=1, source_target_pairs={{0,8},{8,16},{16,24},{24,28},{28,20},{20,12},{12,4},{4,0},{1,9},{9... | collective-permute-start | bytes 1056776 | tf_op jit(solution)/shard_map/ppermute | solution.py:61
  591.5 47.6 %collective-permute-start.40 = (bf16[3072,256]{1,0:T(8,128)(2,1)}, bf16[3072,256]{1,0:T(8,128)(2,1)}, u32[]{:S(2)}, u32[]{:S(2)}) collective-permute-start(bf16[3072,256]{1,0:T(8,128)(2,1)} %shard_map.355), channel_id=1, source_target_pairs={{0,4},{8,0},{16,8},{24,16},{28,24},{20,28},{12,20},{4,12},{1,5},{9... | collective-permute-start | bytes 4718600 | tf_op jit(solution)/shard_map/ppermute | solution.py:61
  593.3 53.4 %collective-permute-start.41 = (bf16[3072,256]{1,0:T(8,128)(2,1)}, bf16[3072,256]{1,0:T(8,128)(2,1)}, u32[]{:S(2)}, u32[]{:S(2)}) collective-permute-start(bf16[3072,256]{1,0:T(8,128)(2,1)} %shard_map.356), channel_id=1, source_target_pairs={{0,8},{8,16},{16,24},{24,28},{28,20},{20,12},{12,4},{4,0},{1,9},{9... | collective-permute-start | bytes 4718600 | tf_op jit(solution)/shard_map/ppermute | solution.py:61
  605.0 51.1 %collective-permute-start.43 = (bf16[1376,256]{1,0:T(8,128)(2,1)}, bf16[1376,256]{1,0:T(8,128)(2,1)}, u32[]{:S(2)}, u32[]{:S(2)}) collective-permute-start(bf16[1376,256]{1,0:T(8,128)(2,1)} %copy-done.13), channel_id=1, source_target_pairs={{0,4},{8,0},{16,8},{24,16},{28,24},{20,28},{12,20},{4,12},{1,5},{9... | collective-permute-start | bytes 2113544 | tf_op jit(solution)/shard_map/ppermute | solution.py:61
  606.4 51.6 %collective-permute-start.44 = (bf16[1376,256]{1,0:T(8,128)(2,1)}, bf16[1376,256]{1,0:T(8,128)(2,1)}, u32[]{:S(2)}, u32[]{:S(2)}) collective-permute-start(bf16[1376,256]{1,0:T(8,128)(2,1)} %copy-done.12), channel_id=1, source_target_pairs={{0,8},{8,16},{16,24},{24,28},{28,20},{20,12},{12,4},{4,0},{1,9},{9... | collective-permute-start | bytes 2113544 | tf_op jit(solution)/shard_map/ppermute | solution.py:61
  617.4 35.4 %collective-permute-start.42 = (f32[8,512]{1,0:T(8,128)}, f32[8,512]{1,0:T(8,128)}, u32[]{:S(2)}, u32[]{:S(2)}) collective-permute-start(f32[8,512]{1,0:T(8,128)} %pad_maximum_fusion.3), channel_id=1, source_target_pairs={{0,1},{1,0},{2,3},{3,2},{4,5},{5,4},{6,7},{7,6},{8,9},{9,8},{10,11... | collective-permute-start | bytes 49160 | tf_op jit(solution)/shard_map/ppermute | solution.py:1060
  646.7 36.3 %collective-permute-start.46 = (bf16[256,2048]{1,0:T(8,128)(2,1)}, bf16[256,2048]{1,0:T(8,128)(2,1)}, u32[]{:S(2)}, u32[]{:S(2)}) collective-permute-start(bf16[256,2048]{1,0:T(8,128)(2,1)} %shard_map.364), channel_id=1, source_target_pairs={{0,2},{1,3},{2,0},{3,1},{4,6},{5,7},{6,4},{7,5},{8,10},{9,11},{10,... | collective-permute-start | bytes 3145736 | tf_op jit(solution)/shard_map/ppermute | solution.py:1021
  648.4 49.1 %collective-permute-start.48 = (bf16[3072,256]{1,0:T(8,128)(2,1)}, bf16[3072,256]{1,0:T(8,128)(2,1)}, u32[]{:S(2)}, u32[]{:S(2)}) collective-permute-start(bf16[3072,256]{1,0:T(8,128)(2,1)} %shard_map.363), channel_id=1, source_target_pairs={{0,4},{8,0},{16,8},{24,16},{28,24},{20,28},{12,20},{4,12},{1,5},{9... | collective-permute-start | bytes 4718600 | tf_op jit(solution)/shard_map/ppermute | solution.py:61
  665.4 38.3 %collective-permute-start.49 = (bf16[1376,256]{1,0:T(8,128)(2,1)}, bf16[1376,256]{1,0:T(8,128)(2,1)}, u32[]{:S(2)}, u32[]{:S(2)}) collective-permute-start(bf16[1376,256]{1,0:T(8,128)(2,1)} %shard_map.368), channel_id=1, source_target_pairs={{0,8},{8,16},{16,24},{24,28},{28,20},{20,12},{12,4},{4,0},{1,9},{9... | collective-permute-start | bytes 2113544 | tf_op jit(solution)/shard_map/ppermute | solution.py:61
  672.2 33.5 %collective-permute-start.50 = (f32[8,1280]{1,0:T(8,128)}, f32[8,1280]{1,0:T(8,128)}, u32[]{:S(2)}, u32[]{:S(2)}) collective-permute-start(f32[8,1280]{1,0:T(8,128)} %pad_maximum_fusion.2), channel_id=1, source_target_pairs={{0,4},{4,0},{8,12},{12,8},{16,20},{20,16},{24,28},{28,24},{1,5},{5... | collective-permute-start | bytes 122888 | tf_op jit(solution)/shard_map/ppermute | solution.py:1060
  749.5 29.4 %collective-permute-start.60 = (bf16[688,256]{1,0:T(8,128)(2,1)}, bf16[688,256]{1,0:T(8,128)(2,1)}, u32[]{:S(2)}, u32[]{:S(2)}) collective-permute-start(bf16[688,256]{1,0:T(8,128)(2,1)} %shard_map.371), channel_id=1, source_target_pairs={{0,8},{8,16},{16,24},{24,28},{28,20},{20,12},{12,4},{4,0},{1,9},{9... | collective-permute-start | bytes 1056776 | tf_op jit(solution)/shard_map/ppermute | solution.py:61
  751.0 27.9 %collective-permute-start.61 = (bf16[688,256]{1,0:T(8,128)(2,1)S(1)}, bf16[688,256]{1,0:T(8,128)(2,1)S(1)}, u32[]{:S(2)}, u32[]{:S(2)}) collective-permute-start(bf16[688,256]{1,0:T(8,128)(2,1)S(1)} %shard_map.375), channel_id=1, source_target_pairs={{0,4},{8,0},{16,8},{24,16},{28,24},{20,28},{12,20},{4,12},{1,5},{9... | collective-permute-start | bytes 1056776 | tf_op jit(solution)/shard_map/ppermute | solution.py:61
  (120 other events, 1492.2 us)
Sparse Core Ops, SparseCore 0:
  217.2 34.3 all-gather.3
  253.1 34.4 all-gather.5
  474.4 32.6 all-gather.7
  593.7 86.8 all-reduce.13

commit v3 on v2

--- a/solution.py
+++ b/solution.py
@@ -243,7 +243,7 @@
                 return add_up([(term, 0) for term in terms], halves)
             return finish(sum(term.astype(floats) for term in terms))
 
-        cost = move_cost((2.0 + len(sources)) * count)
+        cost = 0.5 + count / 5e5
         if not distance:
             cost = cost + move_cost(3 * count)
         return plan.compute(cost, [part, *sources], add, 10.0 if distance else -1.0)
@@ -267,61 +267,9 @@
     return pltpu.CompilerParams(vmem_limit_bytes=VMEM_BYTES)
 
 
-def place(full, piece, at, shape, steps, in_block, in_index, out_block, out_index):
-    short = in_block[0] < out_block[0]
-
-    def body(at_ref, in_ref, *refs):
-        out_ref = refs[-1]
-        if short:
-            out_ref[: in_block[0]] = in_ref[...]
-            out_ref[in_block[0] :] = jnp.zeros(
-                (out_block[0] - in_block[0], out_block[1]), out_ref.dtype
-            )
-        else:
-            out_ref[...] = in_ref[...]
-
-    return pl.pallas_call(
-        body,
-        out_shape=jax.ShapeDtypeStruct(shape, piece.dtype),
-        grid_spec=pltpu.PrefetchScalarGridSpec(
-            num_scalar_prefetch=1,
-            grid=(steps,),
-            in_specs=[
-                pl.BlockSpec(in_block, in_index),
-                *([] if full is None else [pl.BlockSpec(memory_space=pl.ANY)]),
-            ],
-            out_specs=pl.BlockSpec(out_block, out_index),
-        ),
-        input_output_aliases={} if full is None else {2: 0},
-        compiler_params=params(),
-        cost_estimate=HEAVY,
-    )(at, piece, *([] if full is None else [full]))
-
-
 def add_up(terms, dtype, rows=None):
     rows = rows or terms[0][0].shape[0]
-    width = terms[0][0].shape[1]
-    steps = next(n for n in (4, 3, 2, 1) if rows % (16 * n) == 0)
-    tile = rows // steps
-
-    def body(*refs):
-        total = refs[0][...].astype(floats)
-        for ref in refs[1:-1]:
-            total = total + ref[...].astype(floats)
-        refs[-1][...] = total.astype(dtype)
-
-    def spec(first):
-        return pl.BlockSpec((tile, width), lambda i: (first // tile + i, 0))
-
-    return pl.pallas_call(
-        body,
-        out_shape=jax.ShapeDtypeStruct((rows, width), dtype),
-        grid=(steps,),
-        in_specs=[spec(first) for _, first in terms],
-        out_specs=spec(0),
-        compiler_params=params(),
-        cost_estimate=HEAVY,
-    )(*(array for array, _ in terms))
+    return sum(array[first : first + rows].astype(floats) for array, first in terms).astype(dtype)
 
 
 def first_norm(tokens, gain, tiles, own):
@@ -367,43 +315,56 @@
     return max(step for step in range(128, 513, 128) if size % step == 0)
 
 
-def gradient_blocks(lhs, rhs, order, half, tile=None, keep=None):
-    sides, tokens, height = lhs.shape
+def gradient_blocks(groups, order, half, tile, keep):
     count = order.shape[0] // 2
-    block = rhs.shape[1] // order.shape[0]
-    tile = tile or tile_of(height)
-    keep = keep or tile
-    steps = height // tile
-
-    def body(order_ref, lhs_ref, *refs):
-        turned = lhs_ref[0].T
-        for rhs_ref, out_ref in zip(refs[:count], refs[count:]):
-            product = jnp.dot(turned, rhs_ref[...], preferred_element_type=floats)
-            out_ref[...] = product[:keep].astype(halves)
-
-    def column(j):
-        return pl.BlockSpec(
-            (tokens, block), lambda side, i, order_ref: (0, order_ref[half * count + j])
-        )
+    block = groups[0][1].shape[1] // order.shape[0]
+    starts, total = [], 0
+    for lhs, _ in groups:
+        starts.append(total)
+        total += lhs.shape[0] * lhs.shape[2] // tile
+    in_specs, operands = [], []
+    for start, (lhs, rhs) in zip(starts, groups):
+        sides, tokens, height = lhs.shape
+        steps = height // tile
+
+        def place_of(i, order_ref, start=start, sides=sides, steps=steps):
+            step = jnp.clip(i - start, 0, sides * steps - 1)
+            return step // steps, 0, step % steps
+
+        def column(j, tokens=tokens):
+            return pl.BlockSpec(
+                (tokens, block), lambda i, order_ref: (0, order_ref[half * count + j])
+            )
+
+        in_specs += [pl.BlockSpec((1, tokens, tile), place_of), *(column(j) for j in range(count))]
+        operands += [lhs, *([rhs] * count)]
+
+    def body(order_ref, *refs):
+        out_refs = refs[len(operands) :]
+        step = pl.program_id(0)
+        for n, start in enumerate(starts):
+            end = starts[n + 1] if n + 1 < len(starts) else total
+            lhs_ref, *rhs_refs = refs[n * (count + 1) : (n + 1) * (count + 1)]
+
+            @pl.when(jnp.logical_and(step >= start, step < end))
+            def _():
+                turned = lhs_ref[0].T
+                for rhs_ref, out_ref in zip(rhs_refs, out_refs):
+                    product = jnp.dot(turned, rhs_ref[...], preferred_element_type=floats)
+                    out_ref[...] = product[:keep].astype(halves)
 
     return pl.pallas_call(
         body,
-        out_shape=[jax.ShapeDtypeStruct((sides * steps * keep, block), halves)] * count,
+        out_shape=[jax.ShapeDtypeStruct((total * keep, block), halves)] * count,
         grid_spec=pltpu.PrefetchScalarGridSpec(
             num_scalar_prefetch=1,
-            grid=(sides, steps),
-            in_specs=[
-                pl.BlockSpec((1, tokens, tile), lambda side, i, order_ref: (side, 0, i)),
-                *(column(j) for j in range(count)),
-            ],
-            out_specs=[
-                pl.BlockSpec((keep, block), lambda side, i, order_ref: (side * steps + i, 0))
-            ]
-            * count,
+            grid=(total,),
+            in_specs=in_specs,
+            out_specs=[pl.BlockSpec((keep, block), lambda i, order_ref: (i, 0))] * count,
         ),
         compiler_params=params(),
         cost_estimate=HEAVY,
-    )(order, lhs, *([rhs] * count))
+    )(order, *operands)
 
 
 def matmul_across(lhs, rhs, first, count):
@@ -948,48 +909,38 @@
                 )
 
             needs = [blocks[distance]] if full is None else [full, blocks[distance]]
-            full = compute(3.5, needs, extend)
+            full = compute(1.0 + count / 1.2e6, needs, extend)
         return full, blocks
 
     def put_mix(full, piece, at):
-        return place(
-            full, piece, at, (3 * lanes, width), 3,
-            (sent, block), lambda i, at: (i, 0),
-            (lanes, block), lambda i, at: (i, at[0]),
-        )
+        if full is None:
+            full = jnp.zeros((3 * lanes, width), halves), jnp.zeros((hidden_width, width), halves)
+        mix, down = full
+        for i in range(3):
+            rows = piece[i * sent : (i + 1) * sent]
+            mix = lax.dynamic_update_slice(mix, rows, (i * lanes, at[0] * block))
+        return mix, lax.dynamic_update_slice(down, piece[3 * sent :], (0, at[0] * block))
 
     def put_rows(full, piece, at):
-        return place(
-            full, piece, at, (width, 2 * hidden_width), 2,
-            (block, hidden_width), lambda i, at: (0, i),
-            (block, hidden_width), lambda i, at: (at[0], i),
-        )
-
-    def put_columns(full, piece, at):
-        tall = hidden_width // 2
-        return place(
-            full, piece, at, (hidden_width, width), 2,
-            (tall, block), lambda i, at: (i, 0),
-            (tall, block), lambda i, at: (i, at[0]),
-        )
-
-    def mix_of(value, branch, out):
-        return jnp.concatenate(
-            [pad_dim(array, 0, sent) for array in (value.T, branch.T, out)], axis=0
-        )
-
-    mix = compute(3.0, [], lambda v: mix_of(value_weight, branch_weight, out_weight), 8.0)
+        if full is None:
+            full = jnp.zeros((width, 2 * hidden_width), halves)
+        return lax.dynamic_update_slice(full, piece, (at[0] * block, 0))
+
+    def mix_of(value, branch, out, down):
+        pieces = [pad_dim(array, 0, sent) for array in (value.T, branch.T, out)]
+        return jnp.concatenate([*pieces, down], axis=0)
+
+    mix = compute(
+        3.0, [], lambda v: mix_of(value_weight, branch_weight, out_weight, down_weight), 8.0
+    )
     both_own = compute(2.0, [], lambda v: jnp.concatenate([gate_weight, up_weight], axis=1), 1.0)
-    mix_full, mix_blocks = gather_weight(mix, 3 * sent * block, False, 9.0, {}, put_mix)
+    mix_full, mix_blocks = gather_weight(
+        mix, (3 * sent + hidden_width) * block, False, 9.0, {}, put_mix
+    )
     far = dp.count // 2
-    both_full, both_blocks = gather_weight(
+    both_full, _ = gather_weight(
         both_own, 2 * hidden_width * block, True, 8.0,
         {(AHEAD, 0): mix_blocks[far], (BACK, 0): mix_blocks[far + 1]}, put_rows,
-    )
-    down_own = compute(0.5, [], lambda v: down_weight)
-    down_full, down_blocks = gather_weight(
-        down_own, hidden_width * block, False, 7.0,
-        {(AHEAD, 0): both_blocks[far - 1], (BACK, 0): both_blocks[far]}, put_columns,
     )
 
     def spread(gate):
@@ -1041,7 +992,7 @@
                 pieces += [(v[term], 0) for term in passing]
                 return add_up(pieces, halves if s else floats, part)
 
-            made = compute(3.0, [product, *terms, *passing], add, 10.0)
+            made = compute(2.0, [product, *terms, *passing], add, 10.0)
             if s:
                 passing = [
                     plan.add(CROSS, 26.5, [made], lambda v, made=made: cross(v[made], 1), 3.0)
@@ -1076,7 +1027,7 @@
     branches = compute(
         10.8,
         [norm_in, mix_full],
-        lambda v: matmul_across(v[norm_in][0], v[mix_full], 0, 2 * lanes),
+        lambda v: matmul_across(v[norm_in][0], v[mix_full][0], 0, 2 * lanes),
     )
     recur = compute(
         20.2,
@@ -1087,7 +1038,7 @@
     mixed_out = compute(
         9.2,
         [mixed, mix_full],
-        lambda v: matmul_halves(v[mixed], v[mix_full], row_places, cores, 2 * lanes),
+        lambda v: matmul_halves(v[mixed], v[mix_full][0], row_places, cores, 2 * lanes),
     )
     branch_out = reduce_rows(mixed_out)
 
@@ -1106,31 +1057,21 @@
     )
     hidden = compute(0.0, [gated], lambda v: v[gated][2], 30.0)
 
-    def gradient(lhs, lhs_of, rhs, rhs_of, cost, bias, tile=None, keep=None):
+    def gradient(needs, groups, tile, keep, cost, bias):
         return [
             compute(
                 cost,
-                [lhs, rhs],
-                lambda v, h=h: gradient_blocks(lhs_of(v), rhs_of(v), order, h, tile, keep),
+                needs,
+                lambda v, h=h: gradient_blocks(groups(v), order, h, tile, keep),
                 bias - 3 * h,
             )
             for h in range(2)
         ]
 
-    grad_down = ring_reduce(
-        plan,
-        dp,
-        gradient(
-            hidden, lambda v: v[hidden][None], cot_full, lambda v: v[cot_full], 7.0, 6.0
-        ),
-        hidden_width * block,
-        lambda total: total,
-        after=[down_blocks[far]],
-    )
     back_both = compute(
         14.7,
-        [gated, cot_full, down_full],
-        lambda v: gated_backward(v[cot_full], v[down_full], *v[gated][:2]),
+        [gated, cot_full, mix_full],
+        lambda v: gated_backward(v[cot_full], v[mix_full][1], *v[gated][:2]),
     )
     back_product = compute(
         20.5,
@@ -1138,18 +1079,27 @@
         lambda v: pair_halves(v[back_both], v[both_full], row_places, cores),
     )
     back_mid = reduce_rows(back_product)
-    grad_both = ring_reduce(
+    tile = tile_of(hidden_width)
+    grad_ffn = ring_reduce(
         plan,
         dp,
-        gradient(back_both, lambda v: v[back_both], mid_full, lambda v: v[mid_full], 11.0, 0.0),
-        2 * hidden_width * block,
-        lambda total: (total[:hidden_width].T, total[hidden_width:].T),
-        True,
+        gradient(
+            [hidden, cot_full, back_both, mid_full],
+            lambda v: [(v[hidden][None], v[cot_full]), (v[back_both], v[mid_full])],
+            tile, tile, 18.0, 2.0,
+        ),
+        3 * hidden_width * block,
+        lambda total: (
+            total[:hidden_width],
+            total[hidden_width : 2 * hidden_width].T,
+            total[2 * hidden_width :].T,
+        ),
+        False,
     )
     ffn_product = compute(
         12.0,
-        [hidden, down_full],
-        lambda v: matmul_halves(v[hidden], v[down_full], row_places, cores),
+        [hidden, mix_full],
+        lambda v: matmul_halves(v[hidden], v[mix_full][1], row_places, cores),
         -2.0,
     )
 
@@ -1177,7 +1127,7 @@
     back_mixed = compute(
         6.7,
         [branch_full, mix_full],
-        lambda v: matmul_across(v[branch_full], v[mix_full], 2 * lanes, lanes),
+        lambda v: matmul_across(v[branch_full], v[mix_full][0], 2 * lanes, lanes),
     )
     recur_back = compute(
         26.5,
@@ -1186,32 +1136,27 @@
             v[back_mixed], v[branches], *v[recur][1:], doc_ends, v[small][1], v[small][0], parts
         ),
     )
-    grad_out = ring_reduce(
+    grad_mix = ring_reduce(
         plan,
         dp,
         gradient(
-            mixed, lambda v: v[mixed][None], branch_full, lambda v: v[branch_full],
-            3.5, 2.0, lanes, sent,
-        ),
-        sent * block,
-        lambda total: total[:channels],
+            [recur_back, norm_in, mixed, branch_full],
+            lambda v: [(v[recur_back][0][None], v[norm_in][0]), (v[mixed][None], v[branch_full])],
+            lanes, sent, 9.0, 4.0,
+        ),
+        3 * sent * block,
+        lambda total: (
+            total[:channels].T,
+            total[sent : sent + channels].T,
+            total[2 * sent : 2 * sent + channels],
+        ),
         True,
-    )
-    grad_pair = ring_reduce(
-        plan,
-        dp,
-        gradient(
-            recur_back, lambda v: v[recur_back][0][None], norm_in, lambda v: v[norm_in][0],
-            5.5, 4.0, lanes, sent,
-        ),
-        2 * sent * block,
-        lambda total: (total[:channels].T, total[sent : sent + channels].T),
     )
     back_pair = compute(
         13.0,
         [recur_back, mix_full, norm_in],
         lambda v: matmul_halves(
-            v[recur_back][0], v[mix_full], row_places, cores, 0,
+            v[recur_back][0], v[mix_full][0], row_places, cores, 0,
             (tokens.reshape(seq_len, width), v[norm_in][2]),
         ),
         2.0,
@@ -1273,11 +1218,10 @@
 
     done = plan.execute(
         [
-            output, back_first, grad_pair, grad_out, sum_results, gate_result,
-            grad_both, grad_down,
+            output, back_first, grad_mix, sum_results, gate_result, grad_ffn,
         ]
     )
-    output, first, (value, branch), out, summed, (recur, admit), (gate, up), down = done
+    output, first, (value, branch, out), summed, (recur, admit), (down, gate, up) = done
     return (
         output.reshape(part, 1, width),
         first.reshape(part, 1, width),

time: 800 us -> 728 us (0.910)
  Pallas kernels: 370 us -> 212 us
  local copies, waits for them, and re-layouts: 48.4 us -> 107 us
  other arithmetic: 28.4 us -> 65.1 us
  starting transfers between devices: 62.7 us -> 42.3 us
  waiting for transfers between devices: 261 us -> 269 us
    pallas_call x60 -> x4, Pallas kernels: 212 us -> 53.8 us  [gradient_blocks(): pl.pallas_call(body, out_shape=[jax.ShapeDtypeStruct((total * keep, block...]
    dynamic_update_slice x0 -> x40, local copies, waits for them, and re-layouts: none -> 55.9 us  [the longest x24 25.8 us: put_mix(): mix = lax.dynamic_update_slice(mix, rows, (i * lanes, at[0] * block))]
    convert_element_type x0 -> x14, other arithmetic: none -> 37.7 us  [add_up(): sum((array[first:first + rows].astype(floats) for array, first in terms))]
    all_gather x3, waiting for transfers between devices: 6.41 us -> 38.5 us  [gather_rows(): lax.all_gather(v[own], CHAN, axis=0, tiled=True)]
    ppermute x49 -> x28, waiting for transfers between devices: 211 us -> 182 us  [hop(): return lax.ppermute(value, self.axis, pairs)]
    ppermute x4, waiting for transfers between devices: 29.9 us -> 4.96 us  [cross(): return lax.ppermute(value, CHAN, pairs)]
    psum x1, waiting for transfers between devices: 7.96 us -> 31.6 us  [on_device(): lax.psum(v[gate_terms], DP)]
    ppermute x49 -> x28, starting transfers between devices: 54.4 us -> 33.8 us  [hop(): return lax.ppermute(value, self.axis, pairs)]
  transfers between devices with their start and end apart: 66 -> 45, of which waited for: 28 -> 18; matrix products, arithmetic and copies ran while one was open for 6% -> 20% of each run, Pallas kernels for 44% -> 25%
where the time goes in v3:
time: 728 us; the launch traced here: 719 us
  waiting for transfers between devices  269 us (37%)
  Pallas kernels  212 us (29%)
  local copies, waits for them, and re-layouts  107 us (15%)
  other arithmetic  65.1 us (9%)
  starting transfers between devices  42.3 us (6%)
  between operations  20.3 us (3%)
    ppermute x28, waiting for transfers between devices, hop(): return lax.ppermute(value, self.axis, pairs)  182 us
    pallas_call x4, Pallas kernels, gradient_blocks(): pl.pallas_call(body, out_shape=[jax.ShapeDtypeStruct((total * keep, block...  53.8 us
    all_gather x3, waiting for transfers between devices, gather_rows(): lax.all_gather(v[own], CHAN, axis=0, tiled=True)  38.5 us
    convert_element_type x14, other arithmetic, add_up(): sum((array[first:first + rows].astype(floats) for array, first in terms))  37.7 us
    pallas_call x3, Pallas kernels, matmul_halves(): pl.pallas_call(body, out_shape=(jax.ShapeDtypeStruct((half, wide), floats...  35.2 us
    ppermute x28, starting transfers between devices, hop(): return lax.ppermute(value, self.axis, pairs)  33.8 us
    psum x1, waiting for transfers between devices, on_device(): lax.psum(v[gate_terms], DP)  31.6 us
    unnamed x165, local copies, waits for them, and re-layouts  30.3 us
  transfers between devices with their start and end apart: 45, of which 18 were waited for; matrix products, arithmetic and copies ran while one was open for 20% of the time, Pallas kernels for 25%

profile of v3, /device:TPU:0, one launch (start us, length us, event | category | flops | bytes accessed | tf_op | source)
XLA Modules:
  0.0 718.6 jit_solution(8179284019213008153)
XLA Ops:
  30.3 4.0 shard_map.305
  43.5 6.2 broadcast_in_dim.102
  71.9 24.0 %collective-permute-done.2 = bf16[3600,256]{1,0:T(8,128)(2,1)S(1)} collective-permute-done((bf16[3600,256]{1,0:T(8,128)(2,1)}, bf16[3600,256]{1,0:T(8,128)(2,1)S(1)}, u32[]{:S(2)}, u32[]{:S(2)}) %collective-permute-start.2) | collective-permute-done | bytes 1843232 | tf_op jit(solution)/shard_map/ppermute | solution.py:61
  104.8 31.4 %collective-permute-done.4 = bf16[3600,256]{1,0:T(8,128)(2,1)S(1)} collective-permute-done((bf16[3600,256]{1,0:T(8,128)(2,1)S(1)}, bf16[3600,256]{1,0:T(8,128)(2,1)S(1)}, u32[]{:S(2)}, u32[]{:S(2)}) %collective-permute-start.4) | collective-permute-done | bytes 1843232 | tf_op jit(solution)/shard_map/ppermute | solution.py:61
  145.0 26.4 %collective-permute-done.6 = bf16[256,3072]{1,0:T(8,128)(2,1)} collective-permute-done((bf16[256,3072]{1,0:T(8,128)(2,1)}, bf16[256,3072]{1,0:T(8,128)(2,1)}, u32[]{:S(2)}, u32[]{:S(2)}) %collective-permute-start.6) | collective-permute-done | bytes 1572896 | tf_op jit(solution)/shard_map/ppermute | solution.py:61
  179.5 10.8 %shard_map.306.x_ref.y_ref = f32[1024,1536]{1,0:T(8,128)} custom-call(bf16[1024,2048]{1,0:T(8,128)(2,1)S(1)} %copy-done.31, bf16[2304,2048]{1,0:T(8,128)(2,1)} %slice_dynamic-update-slice_fusion.8.rhs_ref), custom_call_target="tpu_custom_call" | custom-call | flops 199999995904 | bytes 1 | tf_op jit(solution)/shard_map/pallas_call | solution.py:379
  190.4 20.1 %shard_map.307 = (bf16[1024,768]{1,0:T(8,128)(2,1)S(1)}, bf16[1024,768]{1,0:T(8,128)(2,1)S(1)}, f32[1024,1536]{1,0:T(8,128)}, f32[1024,768]{1,0:T(8,128)}) custom-call(s32[4]{0:T(128)S(1)} %bitcast.97, f32[1024,1536]{1,0:T(8,128)} %shard_map.306.x_ref.y_ref, f32[1024,1536]{1,0:T(8,128)} %shard_map.306.x_ref.y_ref, f32[8,768]{1,0:T(8,128)S(1)} %pad.53.vec_ref, ...), custom_call_target="tpu_custom_call" | custom-call | flops 199999995904 | bytes 1 | tf_op jit(solution)/shard_map/pallas_call | solution.py:687
  210.5 9.7 %shard_map.308 = (f32[512,2048]{1,0:T(8,128)}, bf16[512,2048]{1,0:T(8,128)(2,1)S(1)}) custom-call(s32[4]{0:T(128)S(1)} %fusion.30.places_ref, bf16[1024,768]{1,0:T(8,128)(2,1)S(1)} %get-tuple-element.3018.lhs_ref, bf16[2304,2048]{1,0:T(8,128)(2,1)} %slice_dynamic-update-slice_fusion.8.rhs_ref), custom_call_target="tpu_custom_call" | custom-call | flops 199999995904 | bytes 1 | tf_op jit(solution)/shard_map/pallas_call | solution.py:437
  229.5 27.8 %collective-permute-done.11 = bf16[256,3072]{1,0:T(8,128)(2,1)S(1)} collective-permute-done((bf16[256,3072]{1,0:T(8,128)(2,1)}, bf16[256,3072]{1,0:T(8,128)(2,1)S(1)}, u32[]{:S(2)}, u32[]{:S(2)}) %collective-permute-start.11) | collective-permute-done | bytes 1572896 | tf_op jit(solution)/shard_map/ppermute | solution.py:61
  267.2 33.8 %collective-permute-done.14 = bf16[256,3072]{1,0:T(8,128)(2,1)} collective-permute-done((bf16[256,3072]{1,0:T(8,128)(2,1)}, bf16[256,3072]{1,0:T(8,128)(2,1)}, u32[]{:S(2)}, u32[]{:S(2)}) %collective-permute-start.14) | collective-permute-done | bytes 1572896 | tf_op jit(solution)/shard_map/ppermute | solution.py:61
  307.6 20.6 %shard_map.309 = (f32[1024,1536]{1,0:T(8,128)}, f32[1024,1536]{1,0:T(8,128)}, bf16[1024,1536]{1,0:T(8,128)(2,1)S(1)}) custom-call(bf16[1024,2048]{1,0:T(8,128)(2,1)} %all-gather.4.cloned.1.call-done.in_ref.refs_6_.refs_7_.refs_8_.refs_9_, bf16[2048,3072]{1,0:T(8,128)(2,1)} %constant_dynamic-update-slice_fusion.gate_ref.up_ref, ...), custom_call_target="tpu_custom_call" | custom-call | flops 199999995904 | bytes 1 | tf_op jit(solution)/shard_map/pallas_call | solution.py:473
  329.9 6.0 all-gather.6.cloned.1.call-done.cot_ref.refs_1_.refs_2_.refs_3_.refs_4_
  338.1 14.6 %shard_map.310.refs_5_.pair_ref = bf16[2,1024,1536]{2,1,0:T(8,128)(2,1)} custom-call(bf16[1024,2048]{1,0:T(8,128)(2,1)S(1)} %copy-done.16, bf16[1536,2048]{1,0:T(8,128)(2,1)} %slice_dynamic-update-slice_fusion.down_ref.rhs_ref, f32[1024,1536]{1,0:T(8,128)} %get-tuple-element.2210.gate_ref, f32[1024,1536]{1,0:T(8,128)} %get-tuple-element.2211.up_ref), custom_call_target="tpu_custom_call" | custom-call | flops 199999995904 | bytes 1 | tf_op jit(solution)/shard_map/pallas_call | solution.py:506
  352.7 17.4 %shard_map.311 = (bf16[4608,256]{1,0:T(8,128)(2,1)}, bf16[4608,256]{1,0:T(8,128)(2,1)}, bf16[4608,256]{1,0:T(8,128)(2,1)}, bf16[4608,256]{1,0:T(8,128)(2,1)}) custom-call(s32[8]{0:T(128)S(1)} %copy-done.13, bf16[1,1024,1536]{2,1,0:T(8,128)(2,1)} %bitcast.93, bf16[1024,2048]{1,0:T(8,128)(2,1)} %all-gather.6.cloned.1.call-done.cot_ref.refs_1_.refs_2_.refs_3_.refs_4_, ...), custom_call_target="tpu_custom_call" | custom-call | flops 199999995904 | bytes 1 | tf_op jit(solution)/shard_map/pallas_call | solution.py:356
  372.7 20.2 %shard_map.312 = (f32[512,2048]{1,0:T(8,128)}, bf16[512,2048]{1,0:T(8,128)(2,1)}) custom-call(s32[4]{0:T(128)S(1)} %copy-done.25, bf16[2,1024,1536]{2,1,0:T(8,128)(2,1)} %shard_map.310.refs_5_.pair_ref, bf16[2048,3072]{1,0:T(8,128)(2,1)} %constant_dynamic-update-slice_fusion.gate_ref.up_ref, bf16[2048,3072]{1,0:T(8,128)(2,1)} %constant_dynamic-update-slice_fusion.gate_ref.up_ref), custom_call_target="tpu_custom_call" | custom-call | flops 199999995904 | bytes 1 | tf_op jit(solution)/shard_map/pallas_call | solution.py:537
  392.9 17.3 %shard_map.313 = (bf16[4608,256]{1,0:T(8,128)(2,1)S(1)}, bf16[4608,256]{1,0:T(8,128)(2,1)S(1)}, bf16[4608,256]{1,0:T(8,128)(2,1)}, bf16[4608,256]{1,0:T(8,128)(2,1)}) custom-call(s32[8]{0:T(128)S(1)} %copy-done.13, bf16[1,1024,1536]{2,1,0:T(8,128)(2,1)} %bitcast.94, bf16[1024,2048]{1,0:T(8,128)(2,1)} %all-gather.6.cloned.1.call-done.cot_ref.refs_1_.refs_2_.refs_3_.refs_4_, ...), custom_call_target="tpu_custom_call" | custom-call | flops 199999995904 | bytes 1 | tf_op jit(solution)/shard_map/pallas_call | solution.py:356
  414.7 12.2 %shard_map.314 = (f32[512,2048]{1,0:T(8,128)}, bf16[512,2048]{1,0:T(8,128)(2,1)S(1)}) custom-call(s32[4]{0:T(128)S(1)} %copy-done.26, bf16[1024,1536]{1,0:T(8,128)(2,1)S(1)} %copy-done.20, bf16[1536,2048]{1,0:T(8,128)(2,1)} %slice_dynamic-update-slice_fusion.down_ref.rhs_ref), custom_call_target="tpu_custom_call" | custom-call | flops 199999995904 | bytes 1 | tf_op jit(solution)/shard_map/pallas_call | solution.py:437
  426.9 4.5 add_convert_fusion.4
  431.4 3.8 add_convert_fusion.3
  435.2 5.0 collective-permute-done.19
  448.3 32.5 %all-gather.8.cloned.1.call-done.lhs_ref.refs_6_.refs_7_.refs_8_.refs_9_ = bf16[1024,2048]{1,0:T(8,128)(2,1)} async-done(((bf16[256,2048]{1,0:T(8,128)(2,1)}), bf16[1024,2048]{1,0:T(8,128)(2,1)}) %all-gather.8.cloned.1.call-update) | async-done | bytes 4194320 | tf_op jit(solution)/shard_map/all_gather | solution.py:980
  481.0 6.7 shard_map.315.bm_ref
  487.8 12.8 %collective-permute-done.20 = bf16[4608,256]{1,0:T(8,128)(2,1)} collective-permute-done((bf16[4608,256]{1,0:T(8,128)(2,1)}, bf16[4608,256]{1,0:T(8,128)(2,1)}, u32[]{:S(2)}, u32[]{:S(2)}) %collective-permute-start.20) | collective-permute-done | bytes 2359328 | tf_op jit(solution)/shard_map/ppermute | solution.py:61
  504.3 4.0 add_convert_fusion.1
  513.5 26.4 %shard_map.316 = (bf16[1024,1536]{1,0:T(8,128)(2,1)}, bf16[1024,1536]{1,0:T(8,128)(2,1)}, f32[8,768]{1,0:T(8,128)S(1)}) custom-call(s32[4]{0:T(128)S(1)} %bitcast.98, f32[1024,768]{1,0:T(8,128)} %copy-done.32, f32[1024,1536]{1,0:T(8,128)} %shard_map.306.x_ref.y_ref, f32[1024,1536]{1,0:T(8,128)} %shard_map.306.x_ref.y_ref, bf16[1024,768]{1,0:T(8,128)(2,1)S(1)} %copy-done.28, ...), custom_call_target="tpu_custom_call" | custom-call | flops 199999995904 | bytes 1 | tf_op jit(solution)/shard_map/pallas_call | solution.py:823
  539.9 10.1 %shard_map.317 = (bf16[2064,256]{1,0:T(8,128)(2,1)}, bf16[2064,256]{1,0:T(8,128)(2,1)S(1)}, bf16[2064,256]{1,0:T(8,128)(2,1)}, bf16[2064,256]{1,0:T(8,128)(2,1)S(1)}) custom-call(s32[8]{0:T(128)S(1)} %copy-done.14, bf16[1,1024,1536]{2,1,0:T(8,128)(2,1)} %bitcast.91, bf16[1024,2048]{1,0:T(8,128)(2,1)} %copy-done.30, bf16[1024,2048]{1,0:T(8,128)(2,1)} %copy-done.30, ...), custom_call_target="tpu_custom_call" | custom-call | flops 199999995904 | bytes 1 | tf_op jit(solution)/shard_map/pallas_call | solution.py:356
  550.1 3.7 convert_add_fusion.3
  560.8 13.2 %shard_map.318 = (f32[512,2048]{1,0:T(8,128)}, bf16[512,2048]{1,0:T(8,128)(2,1)}, f32[8,2048]{1,0:T(8,128)S(1)}) custom-call(s32[4]{0:T(128)S(1)} %copy-done.26, bf16[1024,1536]{1,0:T(8,128)(2,1)S(1)} %copy-done.18, bf16[2304,2048]{1,0:T(8,128)(2,1)} %slice_dynamic-update-slice_fusion.8.rhs_ref, bf16[1024,2048]{1,0:T(8,128)(2,1)} %bitcast.108, ...), custom_call_target="tpu_custom_call" | custom-call | flops 199999995904 | bytes 1 | tf_op jit(solution)/shard_map/pallas_call | solution.py:437
  582.4 9.0 %shard_map.319 = (bf16[2064,256]{1,0:T(8,128)(2,1)S(1)}, bf16[2064,256]{1,0:T(8,128)(2,1)S(1)}, bf16[2064,256]{1,0:T(8,128)(2,1)S(1)}, bf16[2064,256]{1,0:T(8,128)(2,1)S(1)}) custom-call(s32[8]{0:T(128)S(1)} %copy-done.15, bf16[1,1024,1536]{2,1,0:T(8,128)(2,1)} %bitcast.92, bf16[1024,2048]{1,0:T(8,128)(2,1)} %copy-done.30, bf16[1024,2048]{1,0:T(8,128)(2,1)} %copy-done.30, ...), custom_call_target="tpu_custom_call" | custom-call | flops 199999995904 | bytes 1 | tf_op jit(solution)/shard_map/pallas_call | solution.py:356
  611.6 31.6 %all-reduce.14.cloned.1.call-done = bf16[8,171,171]{2,1,0:T(8,128)(2,1)} async-done(((bf16[8,171,171]{2,1,0:T(8,128)(2,1)}), bf16[8,171,171]{2,1,0:T(8,128)(2,1)}) %all-reduce.14.cloned.1.call-update) | async-done | bytes 467872 | tf_op jit(solution)/shard_map/psum | solution.py:1190
  662.1 15.3 %collective-permute-done.36 = bf16[2064,256]{1,0:T(8,128)(2,1)S(1)} collective-permute-done((bf16[2064,256]{1,0:T(8,128)(2,1)S(1)}, bf16[2064,256]{1,0:T(8,128)(2,1)S(1)}, u32[]{:S(2)}, u32[]{:S(2)}) %collective-permute-start.36) | collective-permute-done | bytes 1056800 | tf_op jit(solution)/shard_map/ppermute | solution.py:61
  695.2 11.7 %collective-permute-done.38 = f32[8,1280]{1,0:T(8,128)S(1)} collective-permute-done((f32[8,1280]{1,0:T(8,128)S(1)}, f32[8,1280]{1,0:T(8,128)S(1)}, u32[]{:S(2)}, u32[]{:S(2)}) %collective-permute-start.38) | collective-permute-done | bytes 40992 | tf_op jit(solution)/shard_map/ppermute | solution.py:1011
  (357 shorter events, 205.4 us)
Async XLA Ops:
  7.2 300.4 %all-gather.4.cloned.1.call-start = ((), (), s32[]{:S(2)}) async-start(), calls=%async_computation | async-start | bytes 5242880 | tf_op jit(solution)/shard_map/all_gather | solution.py:980
  9.9 45.3 %collective-permute-start.1 = (bf16[3600,256]{1,0:T(8,128)(2,1)}, bf16[3600,256]{1,0:T(8,128)(2,1)}, u32[]{:S(2)}, u32[]{:S(2)}) collective-permute-start(bf16[3600,256]{1,0:T(8,128)(2,1)} %fusion.10), channel_id=1, source_target_pairs={{0,8},{8,16},{16,24},{24,28},{28,20},{20,12},{12,4},{4,0},{1,9},{9... | collective-permute-start | bytes 5529608 | tf_op jit(solution)/shard_map/ppermute | solution.py:61
  13.0 42.0 %collective-permute-start = (bf16[3600,256]{1,0:T(8,128)(2,1)}, bf16[3600,256]{1,0:T(8,128)(2,1)}, u32[]{:S(2)}, u32[]{:S(2)}) collective-permute-start(bf16[3600,256]{1,0:T(8,128)(2,1)} %fusion.10), channel_id=1, source_target_pairs={{0,4},{8,0},{16,8},{24,16},{28,24},{20,28},{12,20},{4,12},{1,5},{9... | collective-permute-start | bytes 5529608 | tf_op jit(solution)/shard_map/ppermute | solution.py:61
  54.9 40.9 %collective-permute-start.2 = (bf16[3600,256]{1,0:T(8,128)(2,1)}, bf16[3600,256]{1,0:T(8,128)(2,1)S(1)}, u32[]{:S(2)}, u32[]{:S(2)}) collective-permute-start(bf16[3600,256]{1,0:T(8,128)(2,1)} %collective-permute-done), channel_id=1, source_target_pairs={{0,4},{8,0},{16,8},{24,16},{28,24},{20,28},{12,20},{4,12},{1,5},{9... | collective-permute-start | bytes 5529608 | tf_op jit(solution)/shard_map/ppermute | solution.py:61
  55.2 41.3 %collective-permute-start.3 = (bf16[3600,256]{1,0:T(8,128)(2,1)}, bf16[3600,256]{1,0:T(8,128)(2,1)S(1)}, u32[]{:S(2)}, u32[]{:S(2)}) collective-permute-start(bf16[3600,256]{1,0:T(8,128)(2,1)} %collective-permute-done.1), channel_id=1, source_target_pairs={{0,8},{8,16},{16,24},{24,28},{28,20},{20,12},{12,4},{4,0},{1,9},{9... | collective-permute-start | bytes 5529608 | tf_op jit(solution)/shard_map/ppermute | solution.py:61
  95.9 40.4 %collective-permute-start.4 = (bf16[3600,256]{1,0:T(8,128)(2,1)S(1)}, bf16[3600,256]{1,0:T(8,128)(2,1)S(1)}, u32[]{:S(2)}, u32[]{:S(2)}) collective-permute-start(bf16[3600,256]{1,0:T(8,128)(2,1)S(1)} %collective-permute-done.2), channel_id=1, source_target_pairs={{0,4},{8,0},{16,8},{24,16},{28,24},{20,28},{12,20},{4,12},{1,5},{9... | collective-permute-start | bytes 5529608 | tf_op jit(solution)/shard_map/ppermute | solution.py:61
  96.5 40.4 %collective-permute-start.5 = (bf16[3600,256]{1,0:T(8,128)(2,1)S(1)}, bf16[3600,256]{1,0:T(8,128)(2,1)S(1)}, u32[]{:S(2)}, u32[]{:S(2)}) collective-permute-start(bf16[3600,256]{1,0:T(8,128)(2,1)S(1)} %collective-permute-done.3), channel_id=1, source_target_pairs={{0,8},{8,16},{16,24},{24,28},{28,20},{20,12},{12,4},{4,0},{1,9},{9... | collective-permute-start | bytes 5529608 | tf_op jit(solution)/shard_map/ppermute | solution.py:61
  136.2 39.0 %collective-permute-start.7 = (bf16[3600,256]{1,0:T(8,128)(2,1)S(1)}, bf16[3600,256]{1,0:T(8,128)(2,1)S(1)}, u32[]{:S(2)}, u32[]{:S(2)}) collective-permute-start(bf16[3600,256]{1,0:T(8,128)(2,1)S(1)} %collective-permute-done.4), channel_id=1, source_target_pairs={{0,4},{8,0},{16,8},{24,16},{28,24},{20,28},{12,20},{4,12},{1,5},{9... | collective-permute-start | bytes 5529608 | tf_op jit(solution)/shard_map/ppermute | solution.py:61
  136.9 34.6 %collective-permute-start.6 = (bf16[256,3072]{1,0:T(8,128)(2,1)}, bf16[256,3072]{1,0:T(8,128)(2,1)}, u32[]{:S(2)}, u32[]{:S(2)}) collective-permute-start(bf16[256,3072]{1,0:T(8,128)(2,1)} %pad_maximum_fusion.1), channel_id=1, source_target_pairs={{0,8},{8,16},{16,24},{24,28},{28,20},{20,12},{12,4},{4,0},{1,9},{9... | collective-permute-start | bytes 4718600 | tf_op jit(solution)/shard_map/ppermute | solution.py:61
  171.4 39.0 %collective-permute-start.8 = (bf16[256,3072]{1,0:T(8,128)(2,1)}, bf16[256,3072]{1,0:T(8,128)(2,1)}, u32[]{:S(2)}, u32[]{:S(2)}) collective-permute-start(bf16[256,3072]{1,0:T(8,128)(2,1)} %collective-permute-done.6), channel_id=1, source_target_pairs={{0,8},{8,16},{16,24},{24,28},{28,20},{20,12},{12,4},{4,0},{1,9},{9... | collective-permute-start | bytes 4718600 | tf_op jit(solution)/shard_map/ppermute | solution.py:61
  178.6 41.7 %collective-permute-start.9 = (bf16[256,3072]{1,0:T(8,128)(2,1)}, bf16[256,3072]{1,0:T(8,128)(2,1)}, u32[]{:S(2)}, u32[]{:S(2)}) collective-permute-start(bf16[256,3072]{1,0:T(8,128)(2,1)} %pad_maximum_fusion.1), channel_id=1, source_target_pairs={{0,4},{8,0},{16,8},{24,16},{28,24},{20,28},{12,20},{4,12},{1,5},{9... | collective-permute-start | bytes 4718600 | tf_op jit(solution)/shard_map/ppermute | solution.py:61
  220.3 37.0 %collective-permute-start.11 = (bf16[256,3072]{1,0:T(8,128)(2,1)}, bf16[256,3072]{1,0:T(8,128)(2,1)S(1)}, u32[]{:S(2)}, u32[]{:S(2)}) collective-permute-start(bf16[256,3072]{1,0:T(8,128)(2,1)} %collective-permute-done.8), channel_id=1, source_target_pairs={{0,8},{8,16},{16,24},{24,28},{28,20},{20,12},{12,4},{4,0},{1,9},{9... | collective-permute-start | bytes 4718600 | tf_op jit(solution)/shard_map/ppermute | solution.py:61
  221.4 36.9 %collective-permute-start.12 = (bf16[256,3072]{1,0:T(8,128)(2,1)}, bf16[256,3072]{1,0:T(8,128)(2,1)S(1)}, u32[]{:S(2)}, u32[]{:S(2)}) collective-permute-start(bf16[256,3072]{1,0:T(8,128)(2,1)} %collective-permute-done.9), channel_id=1, source_target_pairs={{0,4},{8,0},{16,8},{24,16},{28,24},{20,28},{12,20},{4,12},{1,5},{9... | collective-permute-start | bytes 4718600 | tf_op jit(solution)/shard_map/ppermute | solution.py:61
  228.5 33.9 %collective-permute-start.13 = (bf16[256,2048]{1,0:T(8,128)(2,1)S(1)}, bf16[256,2048]{1,0:T(8,128)(2,1)S(1)}, u32[]{:S(2)}, u32[]{:S(2)}) collective-permute-start(bf16[256,2048]{1,0:T(8,128)(2,1)S(1)} %add_convert_fusion.14), channel_id=1, source_target_pairs={{0,2},{1,3},{2,0},{3,1},{4,6},{5,7},{6,4},{7,5},{8,10},{9,11},{10,... | collective-permute-start | bytes 3145736 | tf_op jit(solution)/shard_map/ppermute | solution.py:972
  265.0 70.9 %all-gather.6.cloned.1.call-start = ((), (), s32[]{:S(2)}) async-start(), calls=%async_computation.1 | async-start | bytes 5242880 | tf_op jit(solution)/shard_map/all_gather | solution.py:980
  265.0 36.0 %collective-permute-start.14 = (bf16[256,3072]{1,0:T(8,128)(2,1)}, bf16[256,3072]{1,0:T(8,128)(2,1)}, u32[]{:S(2)}, u32[]{:S(2)}) collective-permute-start(bf16[256,3072]{1,0:T(8,128)(2,1)} %copy-done.53), channel_id=1, source_target_pairs={{0,4},{8,0},{16,8},{24,16},{28,24},{20,28},{12,20},{4,12},{1,5},{9... | collective-permute-start | bytes 4718600 | tf_op jit(solution)/shard_map/ppermute | solution.py:61
  266.0 38.9 %collective-permute-start.15 = (bf16[256,3072]{1,0:T(8,128)(2,1)}, bf16[256,3072]{1,0:T(8,128)(2,1)}, u32[]{:S(2)}, u32[]{:S(2)}) collective-permute-start(bf16[256,3072]{1,0:T(8,128)(2,1)} %copy-done.51), channel_id=1, source_target_pairs={{0,8},{8,16},{16,24},{24,28},{28,20},{20,12},{12,4},{4,0},{1,9},{9... | collective-permute-start | bytes 4718600 | tf_op jit(solution)/shard_map/ppermute | solution.py:61
  267.1 213.7 %all-gather.8.cloned.1.call-start = ((), (), s32[]{:S(2)}) async-start(), calls=%async_computation.2 | async-start | bytes 5242880 | tf_op jit(solution)/shard_map/all_gather | solution.py:980
  370.1 61.3 %collective-permute-start.18 = (bf16[4608,256]{1,0:T(8,128)(2,1)}, bf16[4608,256]{1,0:T(8,128)(2,1)}, u32[]{:S(2)}, u32[]{:S(2)}) collective-permute-start(bf16[4608,256]{1,0:T(8,128)(2,1)} %get-tuple-element.2442), channel_id=1, source_target_pairs={{0,4},{8,0},{16,8},{24,16},{28,24},{20,28},{12,20},{4,12},{1,5},{9... | collective-permute-start | bytes 7077896 | tf_op jit(solution)/shard_map/ppermute | solution.py:61
  371.6 55.2 %collective-permute-start.17 = (bf16[4608,256]{1,0:T(8,128)(2,1)}, bf16[4608,256]{1,0:T(8,128)(2,1)}, u32[]{:S(2)}, u32[]{:S(2)}) collective-permute-start(bf16[4608,256]{1,0:T(8,128)(2,1)} %get-tuple-element.2388), channel_id=1, source_target_pairs={{0,8},{8,16},{16,24},{24,28},{28,20},{20,12},{12,4},{4,0},{1,9},{9... | collective-permute-start | bytes 7077896 | tf_op jit(solution)/shard_map/ppermute | solution.py:61
  446.1 197.0 %all-reduce.14.cloned.1.call-start = ((), (), s32[]{:S(2)}) async-start(), calls=%async_computation.3 | async-start | bytes 1441792 | tf_op jit(solution)/shard_map/psum | solution.py:1190
  446.2 58.1 %collective-permute-start.21 = (bf16[4608,256]{1,0:T(8,128)(2,1)}, bf16[4608,256]{1,0:T(8,128)(2,1)}, u32[]{:S(2)}, u32[]{:S(2)}) collective-permute-start(bf16[4608,256]{1,0:T(8,128)(2,1)} %add_convert_fusion.3), channel_id=1, source_target_pairs={{0,4},{8,0},{16,8},{24,16},{28,24},{20,28},{12,20},{4,12},{1,5},{9... | collective-permute-start | bytes 7077896 | tf_op jit(solution)/shard_map/ppermute | solution.py:61
  447.7 52.9 %collective-permute-start.20 = (bf16[4608,256]{1,0:T(8,128)(2,1)}, bf16[4608,256]{1,0:T(8,128)(2,1)}, u32[]{:S(2)}, u32[]{:S(2)}) collective-permute-start(bf16[4608,256]{1,0:T(8,128)(2,1)} %add_convert_fusion.4), channel_id=1, source_target_pairs={{0,8},{8,16},{16,24},{24,28},{28,20},{20,12},{12,4},{4,0},{1,9},{9... | collective-permute-start | bytes 7077896 | tf_op jit(solution)/shard_map/ppermute | solution.py:61
  508.3 72.1 %collective-permute-start.25 = (bf16[4608,256]{1,0:T(8,128)(2,1)}, bf16[4608,256]{1,0:T(8,128)(2,1)}, u32[]{:S(2)}, u32[]{:S(2)}) collective-permute-start(bf16[4608,256]{1,0:T(8,128)(2,1)} %add_convert_fusion.1), channel_id=1, source_target_pairs={{0,4},{8,0},{16,8},{24,16},{28,24},{20,28},{12,20},{4,12},{1,5},{9... | collective-permute-start | bytes 7077896 | tf_op jit(solution)/shard_map/ppermute | solution.py:61
  509.8 64.3 %collective-permute-start.24 = (bf16[4608,256]{1,0:T(8,128)(2,1)}, bf16[4608,256]{1,0:T(8,128)(2,1)}, u32[]{:S(2)}, u32[]{:S(2)}) collective-permute-start(bf16[4608,256]{1,0:T(8,128)(2,1)} %add_convert_fusion.2), channel_id=1, source_target_pairs={{0,8},{8,16},{16,24},{24,28},{28,20},{20,12},{12,4},{4,0},{1,9},{9... | collective-permute-start | bytes 7077896 | tf_op jit(solution)/shard_map/ppermute | solution.py:61
  513.0 37.1 %collective-permute-start.23 = (bf16[256,2048]{1,0:T(8,128)(2,1)}, bf16[256,2048]{1,0:T(8,128)(2,1)}, u32[]{:S(2)}, u32[]{:S(2)}) collective-permute-start(bf16[256,2048]{1,0:T(8,128)(2,1)} %add_convert_fusion.12), channel_id=1, source_target_pairs={{0,2},{1,3},{2,0},{3,1},{4,6},{5,7},{6,4},{7,5},{8,10},{9,11},{10,... | collective-permute-start | bytes 3145736 | tf_op jit(solution)/shard_map/ppermute | solution.py:972
  558.4 35.3 %collective-permute-start.26 = (bf16[2064,256]{1,0:T(8,128)(2,1)}, bf16[2064,256]{1,0:T(8,128)(2,1)}, u32[]{:S(2)}, u32[]{:S(2)}) collective-permute-start(bf16[2064,256]{1,0:T(8,128)(2,1)} %get-tuple-element.3024), channel_id=1, source_target_pairs={{0,8},{8,16},{16,24},{24,28},{28,20},{20,12},{12,4},{4,0},{1,9},{9... | collective-permute-start | bytes 3170312 | tf_op jit(solution)/shard_map/ppermute | solution.py:61
  580.4 73.0 %collective-permute-start.34 = (bf16[4608,256]{1,0:T(8,128)(2,1)}, bf16[4608,256]{1,0:T(8,128)(2,1)}, u32[]{:S(2)}, u32[]{:S(2)}) collective-permute-start(bf16[4608,256]{1,0:T(8,128)(2,1)} %add_convert_fusion), channel_id=1, source_target_pairs={{0,8},{8,16},{16,24},{24,28},{28,20},{20,12},{12,4},{4,0},{1,9},{9... | collective-permute-start | bytes 7077896 | tf_op jit(solution)/shard_map/ppermute | solution.py:61
  603.2 41.2 %collective-permute-start.31 = (bf16[256,2048]{1,0:T(8,128)(2,1)}, bf16[256,2048]{1,0:T(8,128)(2,1)}, u32[]{:S(2)}, u32[]{:S(2)}) collective-permute-start(bf16[256,2048]{1,0:T(8,128)(2,1)} %add_convert_fusion.11), channel_id=1, source_target_pairs={{0,2},{1,3},{2,0},{3,1},{4,6},{5,7},{6,4},{7,5},{8,10},{9,11},{10,... | collective-permute-start | bytes 3145736 | tf_op jit(solution)/shard_map/ppermute | solution.py:972
  607.3 44.5 %collective-permute-start.33 = (bf16[2064,256]{1,0:T(8,128)(2,1)}, bf16[2064,256]{1,0:T(8,128)(2,1)}, u32[]{:S(2)}, u32[]{:S(2)}) collective-permute-start(bf16[2064,256]{1,0:T(8,128)(2,1)} %add_convert_fusion.8), channel_id=1, source_target_pairs={{0,4},{8,0},{16,8},{24,16},{28,24},{20,28},{12,20},{4,12},{1,5},{9... | collective-permute-start | bytes 3170312 | tf_op jit(solution)/shard_map/ppermute | solution.py:61
  609.9 39.4 %collective-permute-start.32 = (f32[8,1280]{1,0:T(8,128)S(1)}, f32[8,1280]{1,0:T(8,128)S(1)}, u32[]{:S(2)}, u32[]{:S(2)}) collective-permute-start(f32[8,1280]{1,0:T(8,128)S(1)} %pad_maximum_fusion.2), channel_id=1, source_target_pairs={{0,4},{4,0},{8,12},{12,8},{16,20},{20,16},{24,28},{28,24},{1,5},{5... | collective-permute-start | bytes 122888 | tf_op jit(solution)/shard_map/ppermute | solution.py:1011
  678.7 31.3 %collective-permute-start.39 = (bf16[2064,256]{1,0:T(8,128)(2,1)}, bf16[2064,256]{1,0:T(8,128)(2,1)S(1)}, u32[]{:S(2)}, u32[]{:S(2)}) collective-permute-start(bf16[2064,256]{1,0:T(8,128)(2,1)} %add_convert_fusion.6), channel_id=1, source_target_pairs={{0,8},{8,16},{16,24},{24,28},{28,20},{20,12},{12,4},{4,0},{1,9},{9... | collective-permute-start | bytes 3170312 | tf_op jit(solution)/shard_map/ppermute | solution.py:61
  (88 other events, 1440.4 us)
Sparse Core Ops, SparseCore 0:
  265.1 34.7 all-gather.3
  301.4 34.4 all-gather.5
  446.3 34.4 all-gather.7
  558.6 84.5 all-reduce.13

commit v4 on v3

--- a/solution.py
+++ b/solution.py
@@ -74,14 +74,15 @@
 
 LINK_RATE = 46e3
 HOP_COST = 3.5
-EARLY = 4.0
+EARLY = 0.0
 QUEUED = 2.5
 CORE, AHEAD, BACK, CHIPS, CROSS, TWIN, SMALL = range(7)
 DEPTHS = {AHEAD: 1, BACK: 1, CHIPS: 9, CROSS: 1, TWIN: 1, SMALL: 2}
 STARTS = {AHEAD: 1.5, BACK: 0.8, CHIPS: 0.5, CROSS: 1.5, TWIN: 1.5, SMALL: 2.0}
 HOPPING = (AHEAD, BACK, CROSS, TWIN, SMALL)
 HOPS = 5
-MARGINS = {CORE: 3.0, AHEAD: 0.5, BACK: 0.5, CHIPS: 1.0, CROSS: 0.5, TWIN: 0.5, SMALL: 2.0}
+PATIENCE, LONG = 6.0, 8.0
+MARGINS = {CORE: 3.0, AHEAD: 1.5, BACK: 1.5, CHIPS: 1.0, CROSS: 0.5, TWIN: 0.5, SMALL: 2.0}
 
 
 class Task:
@@ -155,7 +156,7 @@
             return task.run(values)
 
         while waiting:
-            wakes, chosen = [], None
+            wakes, hops, chosen = [], [], None
             for task in waiting:
                 at, link = when(task), task.resource
                 if at is None:
@@ -176,13 +177,16 @@
                         at = max(at, sorted(others)[len(others) - HOPS] + MARGINS[SMALL])
                 if at > now:
                     wakes.append(at)
+                    if link in (AHEAD, BACK) or task.bias >= 10.0:
+                        hops.append(at)
                 elif link != CORE:
                     chosen = task
                     break
                 elif chosen is None:
                     chosen = task
-            if chosen is None:
-                now = min(wakes)
+            soon = [at for at in hops if now < at <= now + PATIENCE]
+            if chosen is None or (chosen.resource == CORE and chosen.cost > LONG and soon):
+                now = min(soon) if chosen else min(wakes)
                 continue
             result = issue(chosen)
             link = chosen.resource
@@ -229,21 +233,21 @@
 
 
 def ring_reduce(plan, ring, parts, count, finish, flip=False, bias=2.0, after=()):
-    half = ring.count // 2
-
     def total(distance, sources):
         slot = ring.slots[distance]
-        part = parts[slot // half]
+        part, index = next(
+            (task, slot - first) for task, first, count in parts if 0 <= slot - first < count
+        )
         if not sources:
-            return plan.compute(0.0, [part], lambda v: v[part][slot % half], 20.0)
+            return plan.compute(0.0, [part], lambda v: v[part][index], 20.0)
 
         def add(v):
-            terms = [v[part][slot % half], *(v[source] for source in sources)]
+            terms = [v[part][index], *(v[source] for source in sources)]
             if distance:
                 return add_up([(term, 0) for term in terms], halves)
             return finish(sum(term.astype(floats) for term in terms))
 
-        cost = 0.5 + count / 5e5
+        cost = 0.5 + count / 3e5
         if not distance:
             cost = cost + move_cost(3 * count)
         return plan.compute(cost, [part, *sources], add, 10.0 if distance else -1.0)
@@ -315,8 +319,7 @@
     return max(step for step in range(128, 513, 128) if size % step == 0)
 
 
-def gradient_blocks(groups, order, half, tile, keep):
-    count = order.shape[0] // 2
+def gradient_blocks(groups, order, base, count, tile, keep):
     block = groups[0][1].shape[1] // order.shape[0]
     starts, total = [], 0
     for lhs, _ in groups:
@@ -333,7 +336,7 @@
 
         def column(j, tokens=tokens):
             return pl.BlockSpec(
-                (tokens, block), lambda i, order_ref: (0, order_ref[half * count + j])
+                (tokens, block), lambda i, order_ref: (0, order_ref[base + j])
             )
 
         in_specs += [pl.BlockSpec((1, tokens, tile), place_of), *(column(j) for j in range(count))]
@@ -909,7 +912,8 @@
                 )
 
             needs = [blocks[distance]] if full is None else [full, blocks[distance]]
-            full = compute(1.0 + count / 1.2e6, needs, extend)
+            first = 0.0 if full else 6.0
+            full = compute(0.6 + count / 2.6e5 + first, needs, extend)
         return full, blocks
 
     def put_mix(full, piece, at):
@@ -992,7 +996,7 @@
                 pieces += [(v[term], 0) for term in passing]
                 return add_up(pieces, halves if s else floats, part)
 
-            made = compute(2.0, [product, *terms, *passing], add, 10.0)
+            made = compute(2.8, [product, *terms, *passing], add, 10.0)
             if s:
                 passing = [
                     plan.add(CROSS, 26.5, [made], lambda v, made=made: cross(v[made], 1), 3.0)
@@ -1010,7 +1014,7 @@
                 def send(v, source=source, axis=axis, pairs=pairs):
                     return lax.ppermute(v[source], axis, pairs)
 
-                other = plan.add(SMALL, 18.0 if axis == DP else 8.0, [source], send)
+                other = plan.add(SMALL, 26.0 if axis == DP else 8.0, [source], send)
 
                 def add(v, source=source, other=other):
                     return v[source] + v[other]
@@ -1057,16 +1061,17 @@
     )
     hidden = compute(0.0, [gated], lambda v: v[gated][2], 30.0)
 
-    def gradient(needs, groups, tile, keep, cost, bias):
-        return [
-            compute(
-                cost,
-                needs,
-                lambda v, h=h: gradient_blocks(groups(v), order, h, tile, keep),
-                bias - 3 * h,
-            )
-            for h in range(2)
-        ]
+    def gradient(needs, groups, tile, keep, quarters, costs, bias):
+        first, parts = 0, []
+        for n, (quarter, cost) in enumerate(zip(quarters, costs)):
+            count = quarter * dp.count // 4
+
+            def blocks(v, first=first, count=count):
+                return gradient_blocks(groups(v), order, first, count, tile, keep)
+
+            parts.append((compute(cost, needs, blocks, -0.5 * n if n else bias), first, count))
+            first += count
+        return parts
 
     back_both = compute(
         14.7,
@@ -1086,7 +1091,7 @@
         gradient(
             [hidden, cot_full, back_both, mid_full],
             lambda v: [(v[hidden][None], v[cot_full]), (v[back_both], v[mid_full])],
-            tile, tile, 18.0, 2.0,
+            tile, tile, (1, 1, 2), (12.0, 12.0, 17.5), 2.0,
         ),
         3 * hidden_width * block,
         lambda total: (
@@ -1142,7 +1147,7 @@
         gradient(
             [recur_back, norm_in, mixed, branch_full],
             lambda v: [(v[recur_back][0][None], v[norm_in][0]), (v[mixed][None], v[branch_full])],
-            lanes, sent, 9.0, 4.0,
+            lanes, sent, (1, 3), (6.0, 14.0), 4.0,
         ),
         3 * sent * block,
         lambda total: (
@@ -1187,10 +1192,11 @@
     gate_terms = compute(
         5.0, [recur, recur_back], lambda v: gate_grads_of(v).astype(halves), 3.5
     )
-    gate_sums = plan.add(CHIPS, 60.0, [gate_terms], lambda v: lax.psum(v[gate_terms], DP), 3.0)
+    gate_sums = plan.add(CHIPS, 110.0, [gate_terms], lambda v: lax.psum(v[gate_terms], DP), 3.0)
     gate_result = compute(
-        4.0, [gate_sums], lambda v: tuple(jnp.split(v[gate_sums].astype(floats), 2))
-    )
+        4.0, [gate_sums], lambda v: tuple(jnp.split(v[gate_sums].astype(floats), 2)), -5.0
+    )
+
     def both_gains(v):
         gains = [jnp.sum(terms, axis=0).reshape(8, -1) for terms in (v[back_middle][2], v[back_pair][2])]
         return jnp.concatenate(gains, axis=1)

time: 728 us -> 717 us (0.985)
  waiting for transfers between devices: 269 us -> 246 us
  Pallas kernels: 212 us -> 221 us
    psum x1, waiting for transfers between devices: 31.6 us -> 0.01 us  [on_device(): lax.psum(v[gate_terms], DP)]
    ppermute x28, waiting for transfers between devices: 182 us -> 211 us  [hop(): return lax.ppermute(value, self.axis, pairs)]
    all_gather x3, waiting for transfers between devices: 38.5 us -> 26.3 us  [gather_rows(): lax.all_gather(v[own], CHAN, axis=0, tiled=True)]
    pallas_call x4 -> x5, Pallas kernels: 53.8 us -> 62.2 us  [gradient_blocks(): pl.pallas_call(body, out_shape=[jax.ShapeDtypeStruct((total * keep, block...]
    unnamed x165 -> x159, local copies, waits for them, and re-layouts: 30.3 us -> 31.1 us
  transfers between devices with their start and end apart: 45 -> 45, of which waited for: 18 -> 19; matrix products, arithmetic and copies ran while one was open for 20% -> 21% of each run, Pallas kernels for 25% -> 26%
where the time goes in v4:
time: 717 us; the launch traced here: 705 us
  waiting for transfers between devices  246 us (34%)
  Pallas kernels  221 us (31%)
  local copies, waits for them, and re-layouts  109 us (15%)
  other arithmetic  61.3 us (9%)
  starting transfers between devices  45.1 us (6%)
  between operations  20.4 us (3%)
    ppermute x28, waiting for transfers between devices, hop(): return lax.ppermute(value, self.axis, pairs)  211 us
    pallas_call x5, Pallas kernels, gradient_blocks(): pl.pallas_call(body, out_shape=[jax.ShapeDtypeStruct((total * keep, block...  62.2 us
    ppermute x28, starting transfers between devices, hop(): return lax.ppermute(value, self.axis, pairs)  35.2 us
    pallas_call x3, Pallas kernels, matmul_halves(): pl.pallas_call(body, out_shape=(jax.ShapeDtypeStruct((half, wide), floats...  34.7 us
    convert_element_type x14, other arithmetic, add_up(): sum((array[first:first + rows].astype(floats) for array, first in terms))  34.2 us
    unnamed x159, local copies, waits for them, and re-layouts  31.1 us
    pallas_call x1, Pallas kernels, recur_backward(): pl.pallas_call(body, out_shape=(jax.ShapeDtypeStruct((seq_len, 2 * lanes)...  26.4 us
    all_gather x3, waiting for transfers between devices, gather_rows(): lax.all_gather(v[own], CHAN, axis=0, tiled=True)  26.3 us
  transfers between devices with their start and end apart: 45, of which 19 were waited for; matrix products, arithmetic and copies ran while one was open for 21% of the time, Pallas kernels for 26%

profile of v4, /device:TPU:0, one launch (start us, length us, event | category | flops | bytes accessed | tf_op | source)
XLA Modules:
  0.0 705.3 jit_solution(13942264910391468202)
XLA Ops:
  30.3 4.0 shard_map.305
  43.4 6.2 broadcast_in_dim.105
  71.9 24.0 %collective-permute-done.2 = bf16[3600,256]{1,0:T(8,128)(2,1)S(1)} collective-permute-done((bf16[3600,256]{1,0:T(8,128)(2,1)}, bf16[3600,256]{1,0:T(8,128)(2,1)S(1)}, u32[]{:S(2)}, u32[]{:S(2)}) %collective-permute-start.2) | collective-permute-done | bytes 1843232 | tf_op jit(solution)/shard_map/ppermute | solution.py:61
  104.8 31.4 %collective-permute-done.4 = bf16[3600,256]{1,0:T(8,128)(2,1)S(1)} collective-permute-done((bf16[3600,256]{1,0:T(8,128)(2,1)S(1)}, bf16[3600,256]{1,0:T(8,128)(2,1)S(1)}, u32[]{:S(2)}, u32[]{:S(2)}) %collective-permute-start.4) | collective-permute-done | bytes 1843232 | tf_op jit(solution)/shard_map/ppermute | solution.py:61
  145.0 26.4 %collective-permute-done.6 = bf16[256,3072]{1,0:T(8,128)(2,1)} collective-permute-done((bf16[256,3072]{1,0:T(8,128)(2,1)}, bf16[256,3072]{1,0:T(8,128)(2,1)}, u32[]{:S(2)}, u32[]{:S(2)}) %collective-permute-start.6) | collective-permute-done | bytes 1572896 | tf_op jit(solution)/shard_map/ppermute | solution.py:61
  179.5 10.9 %shard_map.306.x_ref.y_ref = f32[1024,1536]{1,0:T(8,128)} custom-call(bf16[1024,2048]{1,0:T(8,128)(2,1)S(1)} %copy-done.28, bf16[2304,2048]{1,0:T(8,128)(2,1)} %slice_dynamic-update-slice_fusion.8.rhs_ref), custom_call_target="tpu_custom_call" | custom-call | flops 199999995904 | bytes 1 | tf_op jit(solution)/shard_map/pallas_call | solution.py:382
  190.5 20.1 %shard_map.307 = (bf16[1024,768]{1,0:T(8,128)(2,1)S(1)}, bf16[1024,768]{1,0:T(8,128)(2,1)S(1)}, f32[1024,1536]{1,0:T(8,128)}, f32[1024,768]{1,0:T(8,128)}) custom-call(s32[4]{0:T(128)S(1)} %bitcast.99, f32[1024,1536]{1,0:T(8,128)} %shard_map.306.x_ref.y_ref, f32[1024,1536]{1,0:T(8,128)} %shard_map.306.x_ref.y_ref, f32[8,768]{1,0:T(8,128)S(1)} %pad.53.vec_ref, ...), custom_call_target="tpu_custom_call" | custom-call | flops 199999995904 | bytes 1 | tf_op jit(solution)/shard_map/pallas_call | solution.py:690
  211.8 9.4 %shard_map.308 = (f32[512,2048]{1,0:T(8,128)}, bf16[512,2048]{1,0:T(8,128)(2,1)S(1)}) custom-call(s32[4]{0:T(128)S(1)} %fusion.30.places_ref, bf16[1024,768]{1,0:T(8,128)(2,1)S(1)} %get-tuple-element.2852.lhs_ref, bf16[2304,2048]{1,0:T(8,128)(2,1)} %slice_dynamic-update-slice_fusion.8.rhs_ref), custom_call_target="tpu_custom_call" | custom-call | flops 199999995904 | bytes 1 | tf_op jit(solution)/shard_map/pallas_call | solution.py:440
  230.5 27.7 %collective-permute-done.11 = bf16[256,3072]{1,0:T(8,128)(2,1)S(1)} collective-permute-done((bf16[256,3072]{1,0:T(8,128)(2,1)}, bf16[256,3072]{1,0:T(8,128)(2,1)S(1)}, u32[]{:S(2)}, u32[]{:S(2)}) %collective-permute-start.11) | collective-permute-done | bytes 1572896 | tf_op jit(solution)/shard_map/ppermute | solution.py:61
  268.2 33.9 %collective-permute-done.14 = bf16[256,3072]{1,0:T(8,128)(2,1)} collective-permute-done((bf16[256,3072]{1,0:T(8,128)(2,1)}, bf16[256,3072]{1,0:T(8,128)(2,1)}, u32[]{:S(2)}, u32[]{:S(2)}) %collective-permute-start.14) | collective-permute-done | bytes 1572896 | tf_op jit(solution)/shard_map/ppermute | solution.py:61
  308.7 20.6 %shard_map.309 = (f32[1024,1536]{1,0:T(8,128)}, f32[1024,1536]{1,0:T(8,128)}, bf16[1024,1536]{1,0:T(8,128)(2,1)S(1)}) custom-call(bf16[1024,2048]{1,0:T(8,128)(2,1)} %all-gather.4.cloned.1.call-done.in_ref.refs_4_.refs_5_.refs_6_.refs_7_.refs_8_.refs_9_, bf16[2048,3072]{1,0:T(8,128)(2,1)} %constant_dynamic-update-slice_fusion.gate_ref.up_ref, ...), custom_call_target="tpu_custom_call" | custom-call | flops 199999995904 | bytes 1 | tf_op jit(solution)/shard_map/pallas_call | solution.py:476
  330.9 6.0 all-gather.6.cloned.1.call-done.cot_ref.refs_1_.refs_2_.refs_3_.refs_4_
  339.1 14.7 %shard_map.310.refs_3_.pair_ref.refs_5_ = bf16[2,1024,1536]{2,1,0:T(8,128)(2,1)} custom-call(bf16[1024,2048]{1,0:T(8,128)(2,1)S(1)} %copy-done.13, bf16[1536,2048]{1,0:T(8,128)(2,1)} %slice_dynamic-update-slice_fusion.down_ref.rhs_ref, f32[1024,1536]{1,0:T(8,128)} %get-tuple-element.2144.gate_ref, f32[1024,1536]{1,0:T(8,128)} %get-tuple-element.2145.up_ref), custom_call_target="tpu_custom_call" | custom-call | flops 199999995904 | bytes 1 | tf_op jit(solution)/shard_map/pallas_call | solution.py:509
  353.9 13.1 %shard_map.311 = (bf16[4608,256]{1,0:T(8,128)(2,1)}, bf16[4608,256]{1,0:T(8,128)(2,1)}) custom-call(s32[8]{0:T(128)S(1)} %copy-done.9, bf16[1,1024,1536]{2,1,0:T(8,128)(2,1)} %bitcast.92, bf16[1024,2048]{1,0:T(8,128)(2,1)} %all-gather.6.cloned.1.call-done.cot_ref.refs_1_.refs_2_.refs_3_.refs_4_, ...), custom_call_target="tpu_custom_call" | custom-call | flops 199999995904 | bytes 1 | tf_op jit(solution)/shard_map/pallas_call | solution.py:359
  369.1 20.2 %shard_map.312 = (f32[512,2048]{1,0:T(8,128)}, bf16[512,2048]{1,0:T(8,128)(2,1)}) custom-call(s32[4]{0:T(128)S(1)} %copy-done.22, bf16[2,1024,1536]{2,1,0:T(8,128)(2,1)} %shard_map.310.refs_3_.pair_ref.refs_5_, bf16[2048,3072]{1,0:T(8,128)(2,1)} %constant_dynamic-update-slice_fusion.gate_ref.up_ref, ...), custom_call_target="tpu_custom_call" | custom-call | flops 199999995904 | bytes 1 | tf_op jit(solution)/shard_map/pallas_call | solution.py:540
  389.3 12.0 %shard_map.313 = (bf16[4608,256]{1,0:T(8,128)(2,1)S(1)}, bf16[4608,256]{1,0:T(8,128)(2,1)S(1)}) custom-call(s32[8]{0:T(128)S(1)} %copy-done.10, bf16[1,1024,1536]{2,1,0:T(8,128)(2,1)} %bitcast.93, bf16[1024,2048]{1,0:T(8,128)(2,1)} %all-gather.6.cloned.1.call-done.cot_ref.refs_1_.refs_2_.refs_3_.refs_4_, ...), custom_call_target="tpu_custom_call" | custom-call | flops 199999995904 | bytes 1 | tf_op jit(solution)/shard_map/pallas_call | solution.py:359
  404.1 17.0 %shard_map.314 = (bf16[4608,256]{1,0:T(8,128)(2,1)S(1)}, bf16[4608,256]{1,0:T(8,128)(2,1)S(1)}, bf16[4608,256]{1,0:T(8,128)(2,1)}, bf16[4608,256]{1,0:T(8,128)(2,1)}) custom-call(s32[8]{0:T(128)S(1)} %copy-done.10, bf16[1,1024,1536]{2,1,0:T(8,128)(2,1)} %bitcast.94, bf16[1024,2048]{1,0:T(8,128)(2,1)} %all-gather.6.cloned.1.call-done.cot_ref.refs_1_.refs_2_.refs_3_.refs_4_, ...), custom_call_target="tpu_custom_call" | custom-call | flops 199999995904 | bytes 1 | tf_op jit(solution)/shard_map/pallas_call | solution.py:359
  439.6 12.2 %shard_map.315 = (f32[512,2048]{1,0:T(8,128)}, bf16[512,2048]{1,0:T(8,128)(2,1)S(1)}) custom-call(s32[4]{0:T(128)S(1)} %copy-done.23, bf16[1024,1536]{1,0:T(8,128)(2,1)S(1)} %copy-done.17, bf16[1536,2048]{1,0:T(8,128)(2,1)} %slice_dynamic-update-slice_fusion.down_ref.rhs_ref), custom_call_target="tpu_custom_call" | custom-call | flops 199999995904 | bytes 1 | tf_op jit(solution)/shard_map/pallas_call | solution.py:440
  453.1 20.3 %all-gather.8.cloned.1.call-done.lhs_ref.refs_4_.refs_5_.refs_8_.refs_9_.refs_10_.refs_11_.refs_12_.refs_13_ = bf16[1024,2048]{1,0:T(8,128)(2,1)} async-done(((bf16[256,2048]{1,0:T(8,128)(2,1)}), bf16[1024,2048]{1,0:T(8,128)(2,1)}) %all-gather.8.cloned.1.call-update) | async-done | bytes 4194320 | tf_op jit(solution)/shard_map/all_gather | solution.py:984
  473.7 6.7 shard_map.316.bm_ref
  480.4 4.3 collective-permute-done.20
  488.5 3.9 add_convert_fusion.1
  498.6 26.4 %shard_map.317 = (bf16[1024,1536]{1,0:T(8,128)(2,1)}, bf16[1024,1536]{1,0:T(8,128)(2,1)}, f32[8,768]{1,0:T(8,128)S(1)}) custom-call(s32[4]{0:T(128)S(1)} %bitcast.100, f32[1024,768]{1,0:T(8,128)} %copy-done.29, f32[1024,1536]{1,0:T(8,128)} %shard_map.306.x_ref.y_ref, f32[1024,1536]{1,0:T(8,128)} %shard_map.306.x_ref.y_ref, bf16[1024,768]{1,0:T(8,128)(2,1)S(1)} %copy-done.25, ...), custom_call_target="tpu_custom_call" | custom-call | flops 199999995904 | bytes 1 | tf_op jit(solution)/shard_map/pallas_call | solution.py:826
  525.1 6.8 shard_map.318
  540.0 6.5 collective-permute-done.24
  546.4 4.4 add_convert_fusion
  552.8 13.1 %shard_map.319 = (f32[512,2048]{1,0:T(8,128)}, bf16[512,2048]{1,0:T(8,128)(2,1)S(1)}, f32[8,2048]{1,0:T(8,128)S(1)}) custom-call(s32[4]{0:T(128)S(1)} %copy-done.23, bf16[1024,1536]{1,0:T(8,128)(2,1)S(1)} %copy-done.18, bf16[2304,2048]{1,0:T(8,128)(2,1)} %slice_dynamic-update-slice_fusion.8.rhs_ref, bf16[1024,2048]{1,0:T(8,128)(2,1)} %bitcast.110, ...), custom_call_target="tpu_custom_call" | custom-call | flops 199999995904 | bytes 1 | tf_op jit(solution)/shard_map/pallas_call | solution.py:440
  568.5 13.4 %shard_map.320 = (bf16[2064,256]{1,0:T(8,128)(2,1)S(1)}, bf16[2064,256]{1,0:T(8,128)(2,1)S(1)}, bf16[2064,256]{1,0:T(8,128)(2,1)S(1)}, bf16[2064,256]{1,0:T(8,12...) custom-call(s32[8]{0:T(128)S(1)} %copy-done.12, bf16[1,1024,1536]{2,1,0:T(8,128)(2,1)} %bitcast.96, ...), custom_call_target="tpu_custom_call" | custom-call | flops 199999995904 | bytes 1 | tf_op jit(solution)/shard_map/pallas_call | solution.py:359
  594.5 21.9 %collective-permute-done.30 = bf16[4608,256]{1,0:T(8,128)(2,1)} collective-permute-done((bf16[4608,256]{1,0:T(8,128)(2,1)}, bf16[4608,256]{1,0:T(8,128)(2,1)}, u32[]{:S(2)}, u32[]{:S(2)}) %collective-permute-start.30) | collective-permute-done | bytes 2359328 | tf_op jit(solution)/shard_map/ppermute | solution.py:61
  629.9 9.5 %collective-permute-done.34 = bf16[2064,256]{1,0:T(8,128)(2,1)S(1)} collective-permute-done((bf16[2064,256]{1,0:T(8,128)(2,1)S(1)}, bf16[2064,256]{1,0:T(8,128)(2,1)S(1)}, u32[]{:S(2)}, u32[]{:S(2)}) %collective-permute-start.34) | collective-permute-done | bytes 1056800 | tf_op jit(solution)/shard_map/ppermute | solution.py:61
  651.5 15.7 %collective-permute-done.37 = bf16[2064,256]{1,0:T(8,128)(2,1)} collective-permute-done((bf16[2064,256]{1,0:T(8,128)(2,1)}, bf16[2064,256]{1,0:T(8,128)(2,1)}, u32[]{:S(2)}, u32[]{:S(2)}) %collective-permute-start.37) | collective-permute-done | bytes 1056800 | tf_op jit(solution)/shard_map/ppermute | solution.py:61
  684.1 8.1 %collective-permute-done.38 = f32[8,1280]{1,0:T(8,128)S(1)} collective-permute-done((f32[8,1280]{1,0:T(8,128)S(1)}, f32[8,1280]{1,0:T(8,128)S(1)}, u32[]{:S(2)}, u32[]{:S(2)}) %collective-permute-start.38) | collective-permute-done | bytes 40992 | tf_op jit(solution)/shard_map/ppermute | solution.py:1015
  (352 shorter events, 214.2 us)
Async XLA Ops:
  7.2 301.5 %all-gather.4.cloned.1.call-start = ((), (), s32[]{:S(2)}) async-start(), calls=%async_computation | async-start | bytes 5242880 | tf_op jit(solution)/shard_map/all_gather | solution.py:984
  9.9 45.3 %collective-permute-start.1 = (bf16[3600,256]{1,0:T(8,128)(2,1)}, bf16[3600,256]{1,0:T(8,128)(2,1)}, u32[]{:S(2)}, u32[]{:S(2)}) collective-permute-start(bf16[3600,256]{1,0:T(8,128)(2,1)} %fusion.10), channel_id=1, source_target_pairs={{0,8},{8,16},{16,24},{24,28},{28,20},{20,12},{12,4},{4,0},{1,9},{9... | collective-permute-start | bytes 5529608 | tf_op jit(solution)/shard_map/ppermute | solution.py:61
  13.0 42.0 %collective-permute-start = (bf16[3600,256]{1,0:T(8,128)(2,1)}, bf16[3600,256]{1,0:T(8,128)(2,1)}, u32[]{:S(2)}, u32[]{:S(2)}) collective-permute-start(bf16[3600,256]{1,0:T(8,128)(2,1)} %fusion.10), channel_id=1, source_target_pairs={{0,4},{8,0},{16,8},{24,16},{28,24},{20,28},{12,20},{4,12},{1,5},{9... | collective-permute-start | bytes 5529608 | tf_op jit(solution)/shard_map/ppermute | solution.py:61
  54.9 40.9 %collective-permute-start.2 = (bf16[3600,256]{1,0:T(8,128)(2,1)}, bf16[3600,256]{1,0:T(8,128)(2,1)S(1)}, u32[]{:S(2)}, u32[]{:S(2)}) collective-permute-start(bf16[3600,256]{1,0:T(8,128)(2,1)} %collective-permute-done), channel_id=1, source_target_pairs={{0,4},{8,0},{16,8},{24,16},{28,24},{20,28},{12,20},{4,12},{1,5},{9... | collective-permute-start | bytes 5529608 | tf_op jit(solution)/shard_map/ppermute | solution.py:61
  55.2 41.3 %collective-permute-start.3 = (bf16[3600,256]{1,0:T(8,128)(2,1)}, bf16[3600,256]{1,0:T(8,128)(2,1)S(1)}, u32[]{:S(2)}, u32[]{:S(2)}) collective-permute-start(bf16[3600,256]{1,0:T(8,128)(2,1)} %collective-permute-done.1), channel_id=1, source_target_pairs={{0,8},{8,16},{16,24},{24,28},{28,20},{20,12},{12,4},{4,0},{1,9},{9... | collective-permute-start | bytes 5529608 | tf_op jit(solution)/shard_map/ppermute | solution.py:61
  95.9 40.4 %collective-permute-start.4 = (bf16[3600,256]{1,0:T(8,128)(2,1)S(1)}, bf16[3600,256]{1,0:T(8,128)(2,1)S(1)}, u32[]{:S(2)}, u32[]{:S(2)}) collective-permute-start(bf16[3600,256]{1,0:T(8,128)(2,1)S(1)} %collective-permute-done.2), channel_id=1, source_target_pairs={{0,4},{8,0},{16,8},{24,16},{28,24},{20,28},{12,20},{4,12},{1,5},{9... | collective-permute-start | bytes 5529608 | tf_op jit(solution)/shard_map/ppermute | solution.py:61
  96.5 40.4 %collective-permute-start.5 = (bf16[3600,256]{1,0:T(8,128)(2,1)S(1)}, bf16[3600,256]{1,0:T(8,128)(2,1)S(1)}, u32[]{:S(2)}, u32[]{:S(2)}) collective-permute-start(bf16[3600,256]{1,0:T(8,128)(2,1)S(1)} %collective-permute-done.3), channel_id=1, source_target_pairs={{0,8},{8,16},{16,24},{24,28},{28,20},{20,12},{12,4},{4,0},{1,9},{9... | collective-permute-start | bytes 5529608 | tf_op jit(solution)/shard_map/ppermute | solution.py:61
  136.2 39.0 %collective-permute-start.7 = (bf16[3600,256]{1,0:T(8,128)(2,1)S(1)}, bf16[3600,256]{1,0:T(8,128)(2,1)S(1)}, u32[]{:S(2)}, u32[]{:S(2)}) collective-permute-start(bf16[3600,256]{1,0:T(8,128)(2,1)S(1)} %collective-permute-done.4), channel_id=1, source_target_pairs={{0,4},{8,0},{16,8},{24,16},{28,24},{20,28},{12,20},{4,12},{1,5},{9... | collective-permute-start | bytes 5529608 | tf_op jit(solution)/shard_map/ppermute | solution.py:61
  136.9 34.6 %collective-permute-start.6 = (bf16[256,3072]{1,0:T(8,128)(2,1)}, bf16[256,3072]{1,0:T(8,128)(2,1)}, u32[]{:S(2)}, u32[]{:S(2)}) collective-permute-start(bf16[256,3072]{1,0:T(8,128)(2,1)} %pad_maximum_fusion.1), channel_id=1, source_target_pairs={{0,8},{8,16},{16,24},{24,28},{28,20},{20,12},{12,4},{4,0},{1,9},{9... | collective-permute-start | bytes 4718600 | tf_op jit(solution)/shard_map/ppermute | solution.py:61
  171.4 40.3 %collective-permute-start.8 = (bf16[256,3072]{1,0:T(8,128)(2,1)}, bf16[256,3072]{1,0:T(8,128)(2,1)}, u32[]{:S(2)}, u32[]{:S(2)}) collective-permute-start(bf16[256,3072]{1,0:T(8,128)(2,1)} %collective-permute-done.6), channel_id=1, source_target_pairs={{0,8},{8,16},{16,24},{24,28},{28,20},{20,12},{12,4},{4,0},{1,9},{9... | collective-permute-start | bytes 4718600 | tf_op jit(solution)/shard_map/ppermute | solution.py:61
  178.6 33.2 %collective-permute-start.9 = (bf16[256,3072]{1,0:T(8,128)(2,1)}, bf16[256,3072]{1,0:T(8,128)(2,1)}, u32[]{:S(2)}, u32[]{:S(2)}) collective-permute-start(bf16[256,3072]{1,0:T(8,128)(2,1)} %pad_maximum_fusion.1), channel_id=1, source_target_pairs={{0,4},{8,0},{16,8},{24,16},{28,24},{20,28},{12,20},{4,12},{1,5},{9... | collective-permute-start | bytes 4718600 | tf_op jit(solution)/shard_map/ppermute | solution.py:61
  221.1 37.0 %collective-permute-start.11 = (bf16[256,3072]{1,0:T(8,128)(2,1)}, bf16[256,3072]{1,0:T(8,128)(2,1)S(1)}, u32[]{:S(2)}, u32[]{:S(2)}) collective-permute-start(bf16[256,3072]{1,0:T(8,128)(2,1)} %collective-permute-done.8), channel_id=1, source_target_pairs={{0,8},{8,16},{16,24},{24,28},{28,20},{20,12},{12,4},{4,0},{1,9},{9... | collective-permute-start | bytes 4718600 | tf_op jit(solution)/shard_map/ppermute | solution.py:61
  222.2 37.2 %collective-permute-start.12 = (bf16[256,3072]{1,0:T(8,128)(2,1)}, bf16[256,3072]{1,0:T(8,128)(2,1)S(1)}, u32[]{:S(2)}, u32[]{:S(2)}) collective-permute-start(bf16[256,3072]{1,0:T(8,128)(2,1)} %collective-permute-done.9), channel_id=1, source_target_pairs={{0,4},{8,0},{16,8},{24,16},{28,24},{20,28},{12,20},{4,12},{1,5},{9... | collective-permute-start | bytes 4718600 | tf_op jit(solution)/shard_map/ppermute | solution.py:61
  229.4 34.0 %collective-permute-start.13 = (bf16[256,2048]{1,0:T(8,128)(2,1)S(1)}, bf16[256,2048]{1,0:T(8,128)(2,1)S(1)}, u32[]{:S(2)}, u32[]{:S(2)}) collective-permute-start(bf16[256,2048]{1,0:T(8,128)(2,1)S(1)} %add_convert_fusion.14), channel_id=1, source_target_pairs={{0,2},{1,3},{2,0},{3,1},{4,6},{5,7},{6,4},{7,5},{8,10},{9,11},{10,... | collective-permute-start | bytes 3145736 | tf_op jit(solution)/shard_map/ppermute | solution.py:976
  265.9 71.0 %all-gather.6.cloned.1.call-start = ((), (), s32[]{:S(2)}) async-start(), calls=%async_computation.1 | async-start | bytes 5242880 | tf_op jit(solution)/shard_map/all_gather | solution.py:984
  266.0 36.1 %collective-permute-start.14 = (bf16[256,3072]{1,0:T(8,128)(2,1)}, bf16[256,3072]{1,0:T(8,128)(2,1)}, u32[]{:S(2)}, u32[]{:S(2)}) collective-permute-start(bf16[256,3072]{1,0:T(8,128)(2,1)} %copy-done.50), channel_id=1, source_target_pairs={{0,4},{8,0},{16,8},{24,16},{28,24},{20,28},{12,20},{4,12},{1,5},{9... | collective-permute-start | bytes 4718600 | tf_op jit(solution)/shard_map/ppermute | solution.py:61
  267.0 39.0 %collective-permute-start.15 = (bf16[256,3072]{1,0:T(8,128)(2,1)}, bf16[256,3072]{1,0:T(8,128)(2,1)}, u32[]{:S(2)}, u32[]{:S(2)}) collective-permute-start(bf16[256,3072]{1,0:T(8,128)(2,1)} %copy-done.48), channel_id=1, source_target_pairs={{0,8},{8,16},{16,24},{24,28},{28,20},{20,12},{12,4},{4,0},{1,9},{9... | collective-permute-start | bytes 4718600 | tf_op jit(solution)/shard_map/ppermute | solution.py:61
  268.1 205.3 %all-gather.8.cloned.1.call-start = ((), (), s32[]{:S(2)}) async-start(), calls=%async_computation.2 | async-start | bytes 5242880 | tf_op jit(solution)/shard_map/all_gather | solution.py:984
  366.9 58.9 %collective-permute-start.18 = (bf16[4608,256]{1,0:T(8,128)(2,1)}, bf16[4608,256]{1,0:T(8,128)(2,1)}, u32[]{:S(2)}, u32[]{:S(2)}) collective-permute-start(bf16[4608,256]{1,0:T(8,128)(2,1)} %get-tuple-element.2364), channel_id=1, source_target_pairs={{0,4},{8,0},{16,8},{24,16},{28,24},{20,28},{12,20},{4,12},{1,5},{9... | collective-permute-start | bytes 7077896 | tf_op jit(solution)/shard_map/ppermute | solution.py:61
  368.4 53.6 %collective-permute-start.17 = (bf16[4608,256]{1,0:T(8,128)(2,1)}, bf16[4608,256]{1,0:T(8,128)(2,1)}, u32[]{:S(2)}, u32[]{:S(2)}) collective-permute-start(bf16[4608,256]{1,0:T(8,128)(2,1)} %get-tuple-element.2313), channel_id=1, source_target_pairs={{0,8},{8,16},{16,24},{24,28},{28,20},{20,12},{12,4},{4,0},{1,9},{9... | collective-permute-start | bytes 7077896 | tf_op jit(solution)/shard_map/ppermute | solution.py:61
  429.6 58.9 %collective-permute-start.21 = (bf16[4608,256]{1,0:T(8,128)(2,1)}, bf16[4608,256]{1,0:T(8,128)(2,1)}, u32[]{:S(2)}, u32[]{:S(2)}) collective-permute-start(bf16[4608,256]{1,0:T(8,128)(2,1)} %add_convert_fusion.3), channel_id=1, source_target_pairs={{0,4},{8,0},{16,8},{24,16},{28,24},{20,28},{12,20},{4,12},{1,5},{9... | collective-permute-start | bytes 7077896 | tf_op jit(solution)/shard_map/ppermute | solution.py:61
  431.3 53.5 %collective-permute-start.20 = (bf16[4608,256]{1,0:T(8,128)(2,1)}, bf16[4608,256]{1,0:T(8,128)(2,1)}, u32[]{:S(2)}, u32[]{:S(2)}) collective-permute-start(bf16[4608,256]{1,0:T(8,128)(2,1)} %add_convert_fusion.4), channel_id=1, source_target_pairs={{0,8},{8,16},{16,24},{24,28},{28,20},{20,12},{12,4},{4,0},{1,9},{9... | collective-permute-start | bytes 7077896 | tf_op jit(solution)/shard_map/ppermute | solution.py:61
  437.6 209.0 %all-reduce.14.cloned.1.call-start = ((), (), s32[]{:S(2)}) async-start(), calls=%async_computation.3 | async-start | bytes 1441792 | tf_op jit(solution)/shard_map/psum | solution.py:1195
  492.5 100.8 %collective-permute-start.29 = (bf16[4608,256]{1,0:T(8,128)(2,1)}, bf16[4608,256]{1,0:T(8,128)(2,1)}, u32[]{:S(2)}, u32[]{:S(2)}) collective-permute-start(bf16[4608,256]{1,0:T(8,128)(2,1)} %add_convert_fusion.1), channel_id=1, source_target_pairs={{0,4},{8,0},{16,8},{24,16},{28,24},{20,28},{12,20},{4,12},{1,5},{9... | collective-permute-start | bytes 7077896 | tf_op jit(solution)/shard_map/ppermute | solution.py:61
  493.9 52.5 %collective-permute-start.24 = (bf16[4608,256]{1,0:T(8,128)(2,1)}, bf16[4608,256]{1,0:T(8,128)(2,1)}, u32[]{:S(2)}, u32[]{:S(2)}) collective-permute-start(bf16[4608,256]{1,0:T(8,128)(2,1)} %add_convert_fusion.2), channel_id=1, source_target_pairs={{0,8},{8,16},{16,24},{24,28},{28,20},{20,12},{12,4},{4,0},{1,9},{9... | collective-permute-start | bytes 7077896 | tf_op jit(solution)/shard_map/ppermute | solution.py:61
  497.2 34.7 %collective-permute-start.23 = (bf16[256,2048]{1,0:T(8,128)(2,1)}, bf16[256,2048]{1,0:T(8,128)(2,1)}, u32[]{:S(2)}, u32[]{:S(2)}) collective-permute-start(bf16[256,2048]{1,0:T(8,128)(2,1)} %add_convert_fusion.12), channel_id=1, source_target_pairs={{0,2},{1,3},{2,0},{3,1},{4,6},{5,7},{6,4},{7,5},{8,10},{9,11},{10,... | collective-permute-start | bytes 3145736 | tf_op jit(solution)/shard_map/ppermute | solution.py:976
  552.3 64.1 %collective-permute-start.30 = (bf16[4608,256]{1,0:T(8,128)(2,1)}, bf16[4608,256]{1,0:T(8,128)(2,1)}, u32[]{:S(2)}, u32[]{:S(2)}) collective-permute-start(bf16[4608,256]{1,0:T(8,128)(2,1)} %add_convert_fusion), channel_id=1, source_target_pairs={{0,8},{8,16},{16,24},{24,28},{28,20},{20,12},{12,4},{4,0},{1,9},{9... | collective-permute-start | bytes 7077896 | tf_op jit(solution)/shard_map/ppermute | solution.py:61
  583.5 38.5 %collective-permute-start.31 = (bf16[2064,256]{1,0:T(8,128)(2,1)S(1)}, bf16[2064,256]{1,0:T(8,128)(2,1)S(1)}, u32[]{:S(2)}, u32[]{:S(2)}) collective-permute-start(bf16[2064,256]{1,0:T(8,128)(2,1)S(1)} %add_convert_fusion.9), channel_id=1, source_target_pairs={{0,4},{8,0},{16,8},{24,16},{28,24},{20,28},{12,20},{4,12},{1,5},{9... | collective-permute-start | bytes 3170312 | tf_op jit(solution)/shard_map/ppermute | solution.py:61
  589.4 36.0 %collective-permute-start.32 = (bf16[256,2048]{1,0:T(8,128)(2,1)S(1)}, bf16[256,2048]{1,0:T(8,128)(2,1)S(1)}, u32[]{:S(2)}, u32[]{:S(2)}) collective-permute-start(bf16[256,2048]{1,0:T(8,128)(2,1)S(1)} %add_convert_fusion.11), channel_id=1, source_target_pairs={{0,2},{1,3},{2,0},{3,1},{4,6},{5,7},{6,4},{7,5},{8,10},{9,11},{10,... | collective-permute-start | bytes 3145736 | tf_op jit(solution)/shard_map/ppermute | solution.py:976
  592.0 37.4 %collective-permute-start.33 = (f32[8,1280]{1,0:T(8,128)S(1)}, f32[8,1280]{1,0:T(8,128)S(1)}, u32[]{:S(2)}, u32[]{:S(2)}) collective-permute-start(f32[8,1280]{1,0:T(8,128)S(1)} %pad_maximum_fusion.2), channel_id=1, source_target_pairs={{0,4},{4,0},{8,12},{12,8},{16,20},{20,16},{24,28},{28,24},{1,5},{5... | collective-permute-start | bytes 122888 | tf_op jit(solution)/shard_map/ppermute | solution.py:1015
  593.3 46.1 %collective-permute-start.34 = (bf16[2064,256]{1,0:T(8,128)(2,1)S(1)}, bf16[2064,256]{1,0:T(8,128)(2,1)S(1)}, u32[]{:S(2)}, u32[]{:S(2)}) collective-permute-start(bf16[2064,256]{1,0:T(8,128)(2,1)S(1)} %get-tuple-element.3109), channel_id=1, source_target_pairs={{0,8},{8,16},{16,24},{24,28},{28,20},{20,12},{12,4},{4,0},{1,9},{9... | collective-permute-start | bytes 3170312 | tf_op jit(solution)/shard_map/ppermute | solution.py:61
  646.7 48.6 %collective-permute-start.40 = (bf16[2064,256]{1,0:T(8,128)(2,1)}, bf16[2064,256]{1,0:T(8,128)(2,1)}, u32[]{:S(2)}, u32[]{:S(2)}) collective-permute-start(bf16[2064,256]{1,0:T(8,128)(2,1)} %add_convert_fusion.6), channel_id=1, source_target_pairs={{0,4},{8,0},{16,8},{24,16},{28,24},{20,28},{12,20},{4,12},{1,5},{9... | collective-permute-start | bytes 3170312 | tf_op jit(solution)/shard_map/ppermute | solution.py:61
  (85 other events, 1406.1 us)
Sparse Core Ops, SparseCore 0:
  266.1 34.7 all-gather.3
  302.4 34.4 all-gather.5
  437.8 35.6 all-gather.7
  540.1 79.3 all-reduce.13

commit v5 on v4

--- a/solution.py
+++ b/solution.py
@@ -1007,8 +1007,8 @@
         for axis in axes:
             count = lax.axis_size(axis)
             assert count & (count - 1) == 0
-            bit = 1
-            while bit < count:
+            bit = count // 2
+            while bit:
                 pairs = [(i, i ^ bit) for i in range(count)]
 
                 def send(v, source=source, axis=axis, pairs=pairs):
@@ -1020,7 +1020,7 @@
                     return v[source] + v[other]
 
                 source = compute(0.5, [source, other], add)
-                bit *= 2
+                bit //= 2
         return source
 
     norm_in = compute(

time: 717 us -> 719 us (level)
  transfers between devices with their start and end apart: 45 -> 45, of which waited for: 19 -> 18; matrix products, arithmetic and copies ran while one was open for 21% -> 21% of each run, Pallas kernels for 26% -> 26%
where the time goes in v5:
time: 719 us; the launch traced here: 708 us
  waiting for transfers between devices  250 us (35%)
  Pallas kernels  221 us (31%)
  local copies, waits for them, and re-layouts  109 us (15%)
  other arithmetic  61.3 us (9%)
  starting transfers between devices  43.8 us (6%)
  between operations  20.4 us (3%)
    ppermute x28, waiting for transfers between devices, hop(): return lax.ppermute(value, self.axis, pairs)  213 us
    pallas_call x5, Pallas kernels, gradient_blocks(): pl.pallas_call(body, out_shape=[jax.ShapeDtypeStruct((total * keep, block...  62.2 us
    ppermute x28, starting transfers between devices, hop(): return lax.ppermute(value, self.axis, pairs)  35.7 us
    pallas_call x3, Pallas kernels, matmul_halves(): pl.pallas_call(body, out_shape=(jax.ShapeDtypeStruct((half, wide), floats...  34.7 us
    convert_element_type x14, other arithmetic, add_up(): sum((array[first:first + rows].astype(floats) for array, first in terms))  34.2 us
    unnamed x159, local copies, waits for them, and re-layouts  31.1 us
    pallas_call x1, Pallas kernels, recur_backward(): pl.pallas_call(body, out_shape=(jax.ShapeDtypeStruct((seq_len, 2 * lanes)...  26.4 us
    all_gather x3, waiting for transfers between devices, gather_rows(): lax.all_gather(v[own], CHAN, axis=0, tiled=True)  26.3 us
  transfers between devices with their start and end apart: 45, of which 18 were waited for; matrix products, arithmetic and copies ran while one was open for 21% of the time, Pallas kernels for 26%

profile of v5, /device:TPU:0, one launch (start us, length us, event | category | flops | bytes accessed | tf_op | source)
XLA Modules:
  0.0 708.4 jit_solution(10853563917438416816)
XLA Ops:
  30.3 4.0 shard_map.305
  43.4 6.2 broadcast_in_dim.105
  71.9 24.0 %collective-permute-done.2 = bf16[3600,256]{1,0:T(8,128)(2,1)S(1)} collective-permute-done((bf16[3600,256]{1,0:T(8,128)(2,1)}, bf16[3600,256]{1,0:T(8,128)(2,1)S(1)}, u32[]{:S(2)}, u32[]{:S(2)}) %collective-permute-start.2) | collective-permute-done | bytes 1843232 | tf_op jit(solution)/shard_map/ppermute | solution.py:61
  104.8 31.4 %collective-permute-done.4 = bf16[3600,256]{1,0:T(8,128)(2,1)S(1)} collective-permute-done((bf16[3600,256]{1,0:T(8,128)(2,1)S(1)}, bf16[3600,256]{1,0:T(8,128)(2,1)S(1)}, u32[]{:S(2)}, u32[]{:S(2)}) %collective-permute-start.4) | collective-permute-done | bytes 1843232 | tf_op jit(solution)/shard_map/ppermute | solution.py:61
  145.0 26.4 %collective-permute-done.6 = bf16[256,3072]{1,0:T(8,128)(2,1)} collective-permute-done((bf16[256,3072]{1,0:T(8,128)(2,1)}, bf16[256,3072]{1,0:T(8,128)(2,1)}, u32[]{:S(2)}, u32[]{:S(2)}) %collective-permute-start.6) | collective-permute-done | bytes 1572896 | tf_op jit(solution)/shard_map/ppermute | solution.py:61
  179.5 10.9 %shard_map.306.x_ref.y_ref = f32[1024,1536]{1,0:T(8,128)} custom-call(bf16[1024,2048]{1,0:T(8,128)(2,1)S(1)} %copy-done.28, bf16[2304,2048]{1,0:T(8,128)(2,1)} %slice_dynamic-update-slice_fusion.8.rhs_ref), custom_call_target="tpu_custom_call" | custom-call | flops 199999995904 | bytes 1 | tf_op jit(solution)/shard_map/pallas_call | solution.py:382
  190.5 20.1 %shard_map.307 = (bf16[1024,768]{1,0:T(8,128)(2,1)S(1)}, bf16[1024,768]{1,0:T(8,128)(2,1)S(1)}, f32[1024,1536]{1,0:T(8,128)}, f32[1024,768]{1,0:T(8,128)}) custom-call(s32[4]{0:T(128)S(1)} %bitcast.99, f32[1024,1536]{1,0:T(8,128)} %shard_map.306.x_ref.y_ref, f32[1024,1536]{1,0:T(8,128)} %shard_map.306.x_ref.y_ref, f32[8,768]{1,0:T(8,128)S(1)} %pad.53.vec_ref, ...), custom_call_target="tpu_custom_call" | custom-call | flops 199999995904 | bytes 1 | tf_op jit(solution)/shard_map/pallas_call | solution.py:690
  211.8 9.4 %shard_map.308 = (f32[512,2048]{1,0:T(8,128)}, bf16[512,2048]{1,0:T(8,128)(2,1)S(1)}) custom-call(s32[4]{0:T(128)S(1)} %fusion.30.places_ref, bf16[1024,768]{1,0:T(8,128)(2,1)S(1)} %get-tuple-element.2852.lhs_ref, bf16[2304,2048]{1,0:T(8,128)(2,1)} %slice_dynamic-update-slice_fusion.8.rhs_ref), custom_call_target="tpu_custom_call" | custom-call | flops 199999995904 | bytes 1 | tf_op jit(solution)/shard_map/pallas_call | solution.py:440
  230.5 27.7 %collective-permute-done.11 = bf16[256,3072]{1,0:T(8,128)(2,1)S(1)} collective-permute-done((bf16[256,3072]{1,0:T(8,128)(2,1)}, bf16[256,3072]{1,0:T(8,128)(2,1)S(1)}, u32[]{:S(2)}, u32[]{:S(2)}) %collective-permute-start.11) | collective-permute-done | bytes 1572896 | tf_op jit(solution)/shard_map/ppermute | solution.py:61
  268.2 33.9 %collective-permute-done.14 = bf16[256,3072]{1,0:T(8,128)(2,1)} collective-permute-done((bf16[256,3072]{1,0:T(8,128)(2,1)}, bf16[256,3072]{1,0:T(8,128)(2,1)}, u32[]{:S(2)}, u32[]{:S(2)}) %collective-permute-start.14) | collective-permute-done | bytes 1572896 | tf_op jit(solution)/shard_map/ppermute | solution.py:61
  308.7 20.6 %shard_map.309 = (f32[1024,1536]{1,0:T(8,128)}, f32[1024,1536]{1,0:T(8,128)}, bf16[1024,1536]{1,0:T(8,128)(2,1)S(1)}) custom-call(bf16[1024,2048]{1,0:T(8,128)(2,1)} %all-gather.4.cloned.1.call-done.in_ref.refs_4_.refs_5_.refs_6_.refs_7_.refs_8_.refs_9_, bf16[2048,3072]{1,0:T(8,128)(2,1)} %constant_dynamic-update-slice_fusion.gate_ref.up_ref, ...), custom_call_target="tpu_custom_call" | custom-call | flops 199999995904 | bytes 1 | tf_op jit(solution)/shard_map/pallas_call | solution.py:476
  330.9 6.0 all-gather.6.cloned.1.call-done.cot_ref.refs_1_.refs_2_.refs_3_.refs_4_
  339.1 14.7 %shard_map.310.refs_3_.pair_ref.refs_5_ = bf16[2,1024,1536]{2,1,0:T(8,128)(2,1)} custom-call(bf16[1024,2048]{1,0:T(8,128)(2,1)S(1)} %copy-done.13, bf16[1536,2048]{1,0:T(8,128)(2,1)} %slice_dynamic-update-slice_fusion.down_ref.rhs_ref, f32[1024,1536]{1,0:T(8,128)} %get-tuple-element.2144.gate_ref, f32[1024,1536]{1,0:T(8,128)} %get-tuple-element.2145.up_ref), custom_call_target="tpu_custom_call" | custom-call | flops 199999995904 | bytes 1 | tf_op jit(solution)/shard_map/pallas_call | solution.py:509
  353.9 13.1 %shard_map.311 = (bf16[4608,256]{1,0:T(8,128)(2,1)}, bf16[4608,256]{1,0:T(8,128)(2,1)}) custom-call(s32[8]{0:T(128)S(1)} %copy-done.9, bf16[1,1024,1536]{2,1,0:T(8,128)(2,1)} %bitcast.92, bf16[1024,2048]{1,0:T(8,128)(2,1)} %all-gather.6.cloned.1.call-done.cot_ref.refs_1_.refs_2_.refs_3_.refs_4_, ...), custom_call_target="tpu_custom_call" | custom-call | flops 199999995904 | bytes 1 | tf_op jit(solution)/shard_map/pallas_call | solution.py:359
  369.1 20.2 %shard_map.312 = (f32[512,2048]{1,0:T(8,128)}, bf16[512,2048]{1,0:T(8,128)(2,1)}) custom-call(s32[4]{0:T(128)S(1)} %copy-done.22, bf16[2,1024,1536]{2,1,0:T(8,128)(2,1)} %shard_map.310.refs_3_.pair_ref.refs_5_, bf16[2048,3072]{1,0:T(8,128)(2,1)} %constant_dynamic-update-slice_fusion.gate_ref.up_ref, ...), custom_call_target="tpu_custom_call" | custom-call | flops 199999995904 | bytes 1 | tf_op jit(solution)/shard_map/pallas_call | solution.py:540
  389.3 12.0 %shard_map.313 = (bf16[4608,256]{1,0:T(8,128)(2,1)S(1)}, bf16[4608,256]{1,0:T(8,128)(2,1)S(1)}) custom-call(s32[8]{0:T(128)S(1)} %copy-done.10, bf16[1,1024,1536]{2,1,0:T(8,128)(2,1)} %bitcast.93, bf16[1024,2048]{1,0:T(8,128)(2,1)} %all-gather.6.cloned.1.call-done.cot_ref.refs_1_.refs_2_.refs_3_.refs_4_, ...), custom_call_target="tpu_custom_call" | custom-call | flops 199999995904 | bytes 1 | tf_op jit(solution)/shard_map/pallas_call | solution.py:359
  404.1 17.0 %shard_map.314 = (bf16[4608,256]{1,0:T(8,128)(2,1)S(1)}, bf16[4608,256]{1,0:T(8,128)(2,1)S(1)}, bf16[4608,256]{1,0:T(8,128)(2,1)}, bf16[4608,256]{1,0:T(8,128)(2,1)}) custom-call(s32[8]{0:T(128)S(1)} %copy-done.10, bf16[1,1024,1536]{2,1,0:T(8,128)(2,1)} %bitcast.94, bf16[1024,2048]{1,0:T(8,128)(2,1)} %all-gather.6.cloned.1.call-done.cot_ref.refs_1_.refs_2_.refs_3_.refs_4_, ...), custom_call_target="tpu_custom_call" | custom-call | flops 199999995904 | bytes 1 | tf_op jit(solution)/shard_map/pallas_call | solution.py:359
  439.6 12.2 %shard_map.315 = (f32[512,2048]{1,0:T(8,128)}, bf16[512,2048]{1,0:T(8,128)(2,1)S(1)}) custom-call(s32[4]{0:T(128)S(1)} %copy-done.23, bf16[1024,1536]{1,0:T(8,128)(2,1)S(1)} %copy-done.17, bf16[1536,2048]{1,0:T(8,128)(2,1)} %slice_dynamic-update-slice_fusion.down_ref.rhs_ref), custom_call_target="tpu_custom_call" | custom-call | flops 199999995904 | bytes 1 | tf_op jit(solution)/shard_map/pallas_call | solution.py:440
  453.1 20.3 %all-gather.8.cloned.1.call-done.lhs_ref.refs_4_.refs_5_.refs_8_.refs_9_.refs_10_.refs_11_.refs_12_.refs_13_ = bf16[1024,2048]{1,0:T(8,128)(2,1)} async-done(((bf16[256,2048]{1,0:T(8,128)(2,1)}), bf16[1024,2048]{1,0:T(8,128)(2,1)}) %all-gather.8.cloned.1.call-update) | async-done | bytes 4194320 | tf_op jit(solution)/shard_map/all_gather | solution.py:984
  473.7 6.7 shard_map.316.bm_ref
  480.4 4.3 collective-permute-done.20
  488.5 3.9 add_convert_fusion.1
  498.6 26.4 %shard_map.317 = (bf16[1024,1536]{1,0:T(8,128)(2,1)}, bf16[1024,1536]{1,0:T(8,128)(2,1)}, f32[8,768]{1,0:T(8,128)S(1)}) custom-call(s32[4]{0:T(128)S(1)} %bitcast.100, f32[1024,768]{1,0:T(8,128)} %copy-done.29, f32[1024,1536]{1,0:T(8,128)} %shard_map.306.x_ref.y_ref, f32[1024,1536]{1,0:T(8,128)} %shard_map.306.x_ref.y_ref, bf16[1024,768]{1,0:T(8,128)(2,1)S(1)} %copy-done.25, ...), custom_call_target="tpu_custom_call" | custom-call | flops 199999995904 | bytes 1 | tf_op jit(solution)/shard_map/pallas_call | solution.py:826
  525.1 6.8 shard_map.318
  540.0 6.5 collective-permute-done.24
  546.4 4.4 add_convert_fusion
  552.8 13.1 %shard_map.319 = (f32[512,2048]{1,0:T(8,128)}, bf16[512,2048]{1,0:T(8,128)(2,1)S(1)}, f32[8,2048]{1,0:T(8,128)S(1)}) custom-call(s32[4]{0:T(128)S(1)} %copy-done.23, bf16[1024,1536]{1,0:T(8,128)(2,1)S(1)} %copy-done.18, bf16[2304,2048]{1,0:T(8,128)(2,1)} %slice_dynamic-update-slice_fusion.8.rhs_ref, bf16[1024,2048]{1,0:T(8,128)(2,1)} %bitcast.110, ...), custom_call_target="tpu_custom_call" | custom-call | flops 199999995904 | bytes 1 | tf_op jit(solution)/shard_map/pallas_call | solution.py:440
  569.5 13.4 %shard_map.320 = (bf16[2064,256]{1,0:T(8,128)(2,1)S(1)}, bf16[2064,256]{1,0:T(8,128)(2,1)S(1)}, bf16[2064,256]{1,0:T(8,128)(2,1)S(1)}, bf16[2064,256]{1,0:T(8,12...) custom-call(s32[8]{0:T(128)S(1)} %copy-done.12, bf16[1,1024,1536]{2,1,0:T(8,128)(2,1)} %bitcast.96, ...), custom_call_target="tpu_custom_call" | custom-call | flops 199999995904 | bytes 1 | tf_op jit(solution)/shard_map/pallas_call | solution.py:359
  592.4 24.0 %collective-permute-done.30 = bf16[4608,256]{1,0:T(8,128)(2,1)} collective-permute-done((bf16[4608,256]{1,0:T(8,128)(2,1)}, bf16[4608,256]{1,0:T(8,128)(2,1)}, u32[]{:S(2)}, u32[]{:S(2)}) %collective-permute-start.30) | collective-permute-done | bytes 2359328 | tf_op jit(solution)/shard_map/ppermute | solution.py:61
  630.3 10.0 %collective-permute-done.34 = bf16[2064,256]{1,0:T(8,128)(2,1)S(1)} collective-permute-done((bf16[2064,256]{1,0:T(8,128)(2,1)S(1)}, bf16[2064,256]{1,0:T(8,128)(2,1)S(1)}, u32[]{:S(2)}, u32[]{:S(2)}) %collective-permute-start.34) | collective-permute-done | bytes 1056800 | tf_op jit(solution)/shard_map/ppermute | solution.py:61
  651.5 16.6 %collective-permute-done.37 = bf16[2064,256]{1,0:T(8,128)(2,1)} collective-permute-done((bf16[2064,256]{1,0:T(8,128)(2,1)}, bf16[2064,256]{1,0:T(8,128)(2,1)}, u32[]{:S(2)}, u32[]{:S(2)}) %collective-permute-start.37) | collective-permute-done | bytes 1056800 | tf_op jit(solution)/shard_map/ppermute | solution.py:61
  684.8 10.4 %collective-permute-done.38 = f32[8,1280]{1,0:T(8,128)S(1)} collective-permute-done((f32[8,1280]{1,0:T(8,128)S(1)}, f32[8,1280]{1,0:T(8,128)S(1)}, u32[]{:S(2)}, u32[]{:S(2)}) %collective-permute-start.38) | collective-permute-done | bytes 40992 | tf_op jit(solution)/shard_map/ppermute | solution.py:1015
  (352 shorter events, 211.3 us)
Async XLA Ops:
  7.2 301.5 %all-gather.4.cloned.1.call-start = ((), (), s32[]{:S(2)}) async-start(), calls=%async_computation | async-start | bytes 5242880 | tf_op jit(solution)/shard_map/all_gather | solution.py:984
  9.9 45.3 %collective-permute-start.1 = (bf16[3600,256]{1,0:T(8,128)(2,1)}, bf16[3600,256]{1,0:T(8,128)(2,1)}, u32[]{:S(2)}, u32[]{:S(2)}) collective-permute-start(bf16[3600,256]{1,0:T(8,128)(2,1)} %fusion.10), channel_id=1, source_target_pairs={{0,8},{8,16},{16,24},{24,28},{28,20},{20,12},{12,4},{4,0},{1,9},{9... | collective-permute-start | bytes 5529608 | tf_op jit(solution)/shard_map/ppermute | solution.py:61
  13.0 42.0 %collective-permute-start = (bf16[3600,256]{1,0:T(8,128)(2,1)}, bf16[3600,256]{1,0:T(8,128)(2,1)}, u32[]{:S(2)}, u32[]{:S(2)}) collective-permute-start(bf16[3600,256]{1,0:T(8,128)(2,1)} %fusion.10), channel_id=1, source_target_pairs={{0,4},{8,0},{16,8},{24,16},{28,24},{20,28},{12,20},{4,12},{1,5},{9... | collective-permute-start | bytes 5529608 | tf_op jit(solution)/shard_map/ppermute | solution.py:61
  54.9 40.9 %collective-permute-start.2 = (bf16[3600,256]{1,0:T(8,128)(2,1)}, bf16[3600,256]{1,0:T(8,128)(2,1)S(1)}, u32[]{:S(2)}, u32[]{:S(2)}) collective-permute-start(bf16[3600,256]{1,0:T(8,128)(2,1)} %collective-permute-done), channel_id=1, source_target_pairs={{0,4},{8,0},{16,8},{24,16},{28,24},{20,28},{12,20},{4,12},{1,5},{9... | collective-permute-start | bytes 5529608 | tf_op jit(solution)/shard_map/ppermute | solution.py:61
  55.2 41.3 %collective-permute-start.3 = (bf16[3600,256]{1,0:T(8,128)(2,1)}, bf16[3600,256]{1,0:T(8,128)(2,1)S(1)}, u32[]{:S(2)}, u32[]{:S(2)}) collective-permute-start(bf16[3600,256]{1,0:T(8,128)(2,1)} %collective-permute-done.1), channel_id=1, source_target_pairs={{0,8},{8,16},{16,24},{24,28},{28,20},{20,12},{12,4},{4,0},{1,9},{9... | collective-permute-start | bytes 5529608 | tf_op jit(solution)/shard_map/ppermute | solution.py:61
  95.9 40.4 %collective-permute-start.4 = (bf16[3600,256]{1,0:T(8,128)(2,1)S(1)}, bf16[3600,256]{1,0:T(8,128)(2,1)S(1)}, u32[]{:S(2)}, u32[]{:S(2)}) collective-permute-start(bf16[3600,256]{1,0:T(8,128)(2,1)S(1)} %collective-permute-done.2), channel_id=1, source_target_pairs={{0,4},{8,0},{16,8},{24,16},{28,24},{20,28},{12,20},{4,12},{1,5},{9... | collective-permute-start | bytes 5529608 | tf_op jit(solution)/shard_map/ppermute | solution.py:61
  96.5 40.4 %collective-permute-start.5 = (bf16[3600,256]{1,0:T(8,128)(2,1)S(1)}, bf16[3600,256]{1,0:T(8,128)(2,1)S(1)}, u32[]{:S(2)}, u32[]{:S(2)}) collective-permute-start(bf16[3600,256]{1,0:T(8,128)(2,1)S(1)} %collective-permute-done.3), channel_id=1, source_target_pairs={{0,8},{8,16},{16,24},{24,28},{28,20},{20,12},{12,4},{4,0},{1,9},{9... | collective-permute-start | bytes 5529608 | tf_op jit(solution)/shard_map/ppermute | solution.py:61
  136.2 39.0 %collective-permute-start.7 = (bf16[3600,256]{1,0:T(8,128)(2,1)S(1)}, bf16[3600,256]{1,0:T(8,128)(2,1)S(1)}, u32[]{:S(2)}, u32[]{:S(2)}) collective-permute-start(bf16[3600,256]{1,0:T(8,128)(2,1)S(1)} %collective-permute-done.4), channel_id=1, source_target_pairs={{0,4},{8,0},{16,8},{24,16},{28,24},{20,28},{12,20},{4,12},{1,5},{9... | collective-permute-start | bytes 5529608 | tf_op jit(solution)/shard_map/ppermute | solution.py:61
  136.9 34.6 %collective-permute-start.6 = (bf16[256,3072]{1,0:T(8,128)(2,1)}, bf16[256,3072]{1,0:T(8,128)(2,1)}, u32[]{:S(2)}, u32[]{:S(2)}) collective-permute-start(bf16[256,3072]{1,0:T(8,128)(2,1)} %pad_maximum_fusion.1), channel_id=1, source_target_pairs={{0,8},{8,16},{16,24},{24,28},{28,20},{20,12},{12,4},{4,0},{1,9},{9... | collective-permute-start | bytes 4718600 | tf_op jit(solution)/shard_map/ppermute | solution.py:61
  171.4 40.3 %collective-permute-start.8 = (bf16[256,3072]{1,0:T(8,128)(2,1)}, bf16[256,3072]{1,0:T(8,128)(2,1)}, u32[]{:S(2)}, u32[]{:S(2)}) collective-permute-start(bf16[256,3072]{1,0:T(8,128)(2,1)} %collective-permute-done.6), channel_id=1, source_target_pairs={{0,8},{8,16},{16,24},{24,28},{28,20},{20,12},{12,4},{4,0},{1,9},{9... | collective-permute-start | bytes 4718600 | tf_op jit(solution)/shard_map/ppermute | solution.py:61
  178.6 33.2 %collective-permute-start.9 = (bf16[256,3072]{1,0:T(8,128)(2,1)}, bf16[256,3072]{1,0:T(8,128)(2,1)}, u32[]{:S(2)}, u32[]{:S(2)}) collective-permute-start(bf16[256,3072]{1,0:T(8,128)(2,1)} %pad_maximum_fusion.1), channel_id=1, source_target_pairs={{0,4},{8,0},{16,8},{24,16},{28,24},{20,28},{12,20},{4,12},{1,5},{9... | collective-permute-start | bytes 4718600 | tf_op jit(solution)/shard_map/ppermute | solution.py:61
  221.1 37.0 %collective-permute-start.11 = (bf16[256,3072]{1,0:T(8,128)(2,1)}, bf16[256,3072]{1,0:T(8,128)(2,1)S(1)}, u32[]{:S(2)}, u32[]{:S(2)}) collective-permute-start(bf16[256,3072]{1,0:T(8,128)(2,1)} %collective-permute-done.8), channel_id=1, source_target_pairs={{0,8},{8,16},{16,24},{24,28},{28,20},{20,12},{12,4},{4,0},{1,9},{9... | collective-permute-start | bytes 4718600 | tf_op jit(solution)/shard_map/ppermute | solution.py:61
  222.2 37.2 %collective-permute-start.12 = (bf16[256,3072]{1,0:T(8,128)(2,1)}, bf16[256,3072]{1,0:T(8,128)(2,1)S(1)}, u32[]{:S(2)}, u32[]{:S(2)}) collective-permute-start(bf16[256,3072]{1,0:T(8,128)(2,1)} %collective-permute-done.9), channel_id=1, source_target_pairs={{0,4},{8,0},{16,8},{24,16},{28,24},{20,28},{12,20},{4,12},{1,5},{9... | collective-permute-start | bytes 4718600 | tf_op jit(solution)/shard_map/ppermute | solution.py:61
  229.4 34.0 %collective-permute-start.13 = (bf16[256,2048]{1,0:T(8,128)(2,1)S(1)}, bf16[256,2048]{1,0:T(8,128)(2,1)S(1)}, u32[]{:S(2)}, u32[]{:S(2)}) collective-permute-start(bf16[256,2048]{1,0:T(8,128)(2,1)S(1)} %add_convert_fusion.14), channel_id=1, source_target_pairs={{0,2},{1,3},{2,0},{3,1},{4,6},{5,7},{6,4},{7,5},{8,10},{9,11},{10,... | collective-permute-start | bytes 3145736 | tf_op jit(solution)/shard_map/ppermute | solution.py:976
  265.9 71.0 %all-gather.6.cloned.1.call-start = ((), (), s32[]{:S(2)}) async-start(), calls=%async_computation.1 | async-start | bytes 5242880 | tf_op jit(solution)/shard_map/all_gather | solution.py:984
  266.0 36.1 %collective-permute-start.14 = (bf16[256,3072]{1,0:T(8,128)(2,1)}, bf16[256,3072]{1,0:T(8,128)(2,1)}, u32[]{:S(2)}, u32[]{:S(2)}) collective-permute-start(bf16[256,3072]{1,0:T(8,128)(2,1)} %copy-done.50), channel_id=1, source_target_pairs={{0,4},{8,0},{16,8},{24,16},{28,24},{20,28},{12,20},{4,12},{1,5},{9... | collective-permute-start | bytes 4718600 | tf_op jit(solution)/shard_map/ppermute | solution.py:61
  267.0 39.0 %collective-permute-start.15 = (bf16[256,3072]{1,0:T(8,128)(2,1)}, bf16[256,3072]{1,0:T(8,128)(2,1)}, u32[]{:S(2)}, u32[]{:S(2)}) collective-permute-start(bf16[256,3072]{1,0:T(8,128)(2,1)} %copy-done.48), channel_id=1, source_target_pairs={{0,8},{8,16},{16,24},{24,28},{28,20},{20,12},{12,4},{4,0},{1,9},{9... | collective-permute-start | bytes 4718600 | tf_op jit(solution)/shard_map/ppermute | solution.py:61
  268.1 205.3 %all-gather.8.cloned.1.call-start = ((), (), s32[]{:S(2)}) async-start(), calls=%async_computation.2 | async-start | bytes 5242880 | tf_op jit(solution)/shard_map/all_gather | solution.py:984
  366.9 58.9 %collective-permute-start.18 = (bf16[4608,256]{1,0:T(8,128)(2,1)}, bf16[4608,256]{1,0:T(8,128)(2,1)}, u32[]{:S(2)}, u32[]{:S(2)}) collective-permute-start(bf16[4608,256]{1,0:T(8,128)(2,1)} %get-tuple-element.2364), channel_id=1, source_target_pairs={{0,4},{8,0},{16,8},{24,16},{28,24},{20,28},{12,20},{4,12},{1,5},{9... | collective-permute-start | bytes 7077896 | tf_op jit(solution)/shard_map/ppermute | solution.py:61
  368.4 53.6 %collective-permute-start.17 = (bf16[4608,256]{1,0:T(8,128)(2,1)}, bf16[4608,256]{1,0:T(8,128)(2,1)}, u32[]{:S(2)}, u32[]{:S(2)}) collective-permute-start(bf16[4608,256]{1,0:T(8,128)(2,1)} %get-tuple-element.2313), channel_id=1, source_target_pairs={{0,8},{8,16},{16,24},{24,28},{28,20},{20,12},{12,4},{4,0},{1,9},{9... | collective-permute-start | bytes 7077896 | tf_op jit(solution)/shard_map/ppermute | solution.py:61
  429.6 58.9 %collective-permute-start.21 = (bf16[4608,256]{1,0:T(8,128)(2,1)}, bf16[4608,256]{1,0:T(8,128)(2,1)}, u32[]{:S(2)}, u32[]{:S(2)}) collective-permute-start(bf16[4608,256]{1,0:T(8,128)(2,1)} %add_convert_fusion.3), channel_id=1, source_target_pairs={{0,4},{8,0},{16,8},{24,16},{28,24},{20,28},{12,20},{4,12},{1,5},{9... | collective-permute-start | bytes 7077896 | tf_op jit(solution)/shard_map/ppermute | solution.py:61
  431.3 53.5 %collective-permute-start.20 = (bf16[4608,256]{1,0:T(8,128)(2,1)}, bf16[4608,256]{1,0:T(8,128)(2,1)}, u32[]{:S(2)}, u32[]{:S(2)}) collective-permute-start(bf16[4608,256]{1,0:T(8,128)(2,1)} %add_convert_fusion.4), channel_id=1, source_target_pairs={{0,8},{8,16},{16,24},{24,28},{28,20},{20,12},{12,4},{4,0},{1,9},{9... | collective-permute-start | bytes 7077896 | tf_op jit(solution)/shard_map/ppermute | solution.py:61
  437.6 209.0 %all-reduce.14.cloned.1.call-start = ((), (), s32[]{:S(2)}) async-start(), calls=%async_computation.3 | async-start | bytes 1441792 | tf_op jit(solution)/shard_map/psum | solution.py:1195
  492.5 99.0 %collective-permute-start.29 = (bf16[4608,256]{1,0:T(8,128)(2,1)}, bf16[4608,256]{1,0:T(8,128)(2,1)}, u32[]{:S(2)}, u32[]{:S(2)}) collective-permute-start(bf16[4608,256]{1,0:T(8,128)(2,1)} %add_convert_fusion.1), channel_id=1, source_target_pairs={{0,4},{8,0},{16,8},{24,16},{28,24},{20,28},{12,20},{4,12},{1,5},{9... | collective-permute-start | bytes 7077896 | tf_op jit(solution)/shard_map/ppermute | solution.py:61
  493.9 52.5 %collective-permute-start.24 = (bf16[4608,256]{1,0:T(8,128)(2,1)}, bf16[4608,256]{1,0:T(8,128)(2,1)}, u32[]{:S(2)}, u32[]{:S(2)}) collective-permute-start(bf16[4608,256]{1,0:T(8,128)(2,1)} %add_convert_fusion.2), channel_id=1, source_target_pairs={{0,8},{8,16},{16,24},{24,28},{28,20},{20,12},{12,4},{4,0},{1,9},{9... | collective-permute-start | bytes 7077896 | tf_op jit(solution)/shard_map/ppermute | solution.py:61
  497.2 34.7 %collective-permute-start.23 = (bf16[256,2048]{1,0:T(8,128)(2,1)}, bf16[256,2048]{1,0:T(8,128)(2,1)}, u32[]{:S(2)}, u32[]{:S(2)}) collective-permute-start(bf16[256,2048]{1,0:T(8,128)(2,1)} %add_convert_fusion.12), channel_id=1, source_target_pairs={{0,2},{1,3},{2,0},{3,1},{4,6},{5,7},{6,4},{7,5},{8,10},{9,11},{10,... | collective-permute-start | bytes 3145736 | tf_op jit(solution)/shard_map/ppermute | solution.py:976
  552.3 64.1 %collective-permute-start.30 = (bf16[4608,256]{1,0:T(8,128)(2,1)}, bf16[4608,256]{1,0:T(8,128)(2,1)}, u32[]{:S(2)}, u32[]{:S(2)}) collective-permute-start(bf16[4608,256]{1,0:T(8,128)(2,1)} %add_convert_fusion), channel_id=1, source_target_pairs={{0,8},{8,16},{16,24},{24,28},{28,20},{20,12},{12,4},{4,0},{1,9},{9... | collective-permute-start | bytes 7077896 | tf_op jit(solution)/shard_map/ppermute | solution.py:61
  584.5 37.6 %collective-permute-start.31 = (bf16[2064,256]{1,0:T(8,128)(2,1)S(1)}, bf16[2064,256]{1,0:T(8,128)(2,1)S(1)}, u32[]{:S(2)}, u32[]{:S(2)}) collective-permute-start(bf16[2064,256]{1,0:T(8,128)(2,1)S(1)} %add_convert_fusion.9), channel_id=1, source_target_pairs={{0,4},{8,0},{16,8},{24,16},{28,24},{20,28},{12,20},{4,12},{1,5},{9... | collective-permute-start | bytes 3170312 | tf_op jit(solution)/shard_map/ppermute | solution.py:61
  588.9 37.4 %collective-permute-start.32 = (bf16[256,2048]{1,0:T(8,128)(2,1)S(1)}, bf16[256,2048]{1,0:T(8,128)(2,1)S(1)}, u32[]{:S(2)}, u32[]{:S(2)}) collective-permute-start(bf16[256,2048]{1,0:T(8,128)(2,1)S(1)} %add_convert_fusion.11), channel_id=1, source_target_pairs={{0,2},{1,3},{2,0},{3,1},{4,6},{5,7},{6,4},{7,5},{8,10},{9,11},{10,... | collective-permute-start | bytes 3145736 | tf_op jit(solution)/shard_map/ppermute | solution.py:976
  590.9 39.3 %collective-permute-start.33 = (f32[8,1280]{1,0:T(8,128)S(1)}, f32[8,1280]{1,0:T(8,128)S(1)}, u32[]{:S(2)}, u32[]{:S(2)}) collective-permute-start(f32[8,1280]{1,0:T(8,128)S(1)} %pad_maximum_fusion.2), channel_id=1, source_target_pairs={{0,16},{4,20},{8,24},{12,28},{16,0},{20,4},{24,8},{28,12},{1,17},{... | collective-permute-start | bytes 122888 | tf_op jit(solution)/shard_map/ppermute | solution.py:1015
  591.4 48.9 %collective-permute-start.34 = (bf16[2064,256]{1,0:T(8,128)(2,1)S(1)}, bf16[2064,256]{1,0:T(8,128)(2,1)S(1)}, u32[]{:S(2)}, u32[]{:S(2)}) collective-permute-start(bf16[2064,256]{1,0:T(8,128)(2,1)S(1)} %get-tuple-element.3109), channel_id=1, source_target_pairs={{0,8},{8,16},{16,24},{24,28},{28,20},{20,12},{12,4},{4,0},{1,9},{9... | collective-permute-start | bytes 3170312 | tf_op jit(solution)/shard_map/ppermute | solution.py:61
  646.6 51.7 %collective-permute-start.40 = (bf16[2064,256]{1,0:T(8,128)(2,1)}, bf16[2064,256]{1,0:T(8,128)(2,1)}, u32[]{:S(2)}, u32[]{:S(2)}) collective-permute-start(bf16[2064,256]{1,0:T(8,128)(2,1)} %add_convert_fusion.6), channel_id=1, source_target_pairs={{0,4},{8,0},{16,8},{24,16},{28,24},{20,28},{12,20},{4,12},{1,5},{9... | collective-permute-start | bytes 3170312 | tf_op jit(solution)/shard_map/ppermute | solution.py:61
  (85 other events, 1415.0 us)
Sparse Core Ops, SparseCore 0:
  266.1 34.7 all-gather.3
  302.4 34.4 all-gather.5
  437.8 35.6 all-gather.7
  540.1 81.3 all-reduce.13
